TPU v7x, 512 devices: a whole 4x8x8 slice. The times are simulated.
512 devices in a mesh: rows: 128 (over y, z, core), cols: 4 (over x).
Axes of the slice: x: 4, y: 8, z: 8, core: 2. Of those that a mesh axis runs over, the one named last changes fastest.
Arguments:
- gradient: float32 [8192, 29568], P('rows', 'cols'), as said below
- start_block: float32 [29568, 64], P('cols'), may hold values from -0.03125 to 0.03125
- activations: float32 [8192, 29568], P('rows', 'cols'), may hold values from -6 to 6
- out_grads: float32 [8192, 8192], P('rows', 'cols'), may hold values from -6 to 6
Outputs:
- left_factor: float32 [8192, 64], P('rows')
- right_factor: float32 [29568, 64], P('cols')
- scores: float32 [8192], P('rows')
Inputs may be any that keep to these rules, and one draw needn't show every extreme that they name: real-valued gradient entries, of order 29568 ** -0.5.
All inputs are finite; a program needn't handle non-finite values.
Results may differ from a plain program's by a relative error of at most 0.00013.
Values sent between devices are 32-bit elements; how exact they have to be, the bound alone decides.
No kernel may reach another device: no remote copies, remote signals or barrier semaphores. Data moves between devices by JAX's collectives and lax.ppermute only.
A program may use at most 64 MiB of HBM per device.

v0:
```python
import jax
import jax.numpy as jnp
from jax import lax
from jax.sharding import Mesh
from jax.sharding import PartitionSpec as P

ITERS = 2
ROWS = ("rows_0", "rows_1", "rows_2")


HIGH = lax.Precision.HIGHEST


def sent_to_all(shard, axis):
    copies = jnp.broadcast_to(shard, (lax.axis_size(axis), *shard.shape))
    return lax.all_to_all(copies, axis, split_axis=0, concat_axis=0, tiled=True)


def over_copies(shard, axis):
    everything = sent_to_all(shard, axis)
    return jnp.sum(everything, axis=0)


def joined_along(pieces, dim):
    pieces = jnp.moveaxis(pieces, 0, dim)
    lengths = pieces.shape
    return pieces.reshape(*lengths[:dim], lengths[dim] * lengths[dim + 1], *lengths[dim + 2 :])


def whole_of(shard, axes, dim):
    far, near = axes
    first = sent_to_all(shard, far)
    pieces = jnp.swapaxes(sent_to_all(first, near), 0, 1)
    return joined_along(pieces.reshape(-1, *shard.shape), dim)


def split_up(shard, dim, length):
    before, after = (shard.shape[:dim], shard.shape[dim + 1 :])
    return jnp.moveaxis(shard.reshape(*before, length, -1, *after), dim, 0)


def summed_on_arrival(shard, axis, dim):
    pieces = split_up(shard, dim, lax.axis_size(axis))
    arrived = lax.all_to_all(pieces, axis, split_axis=0, concat_axis=0, tiled=True)
    return arrived.sum(axis=0)


def sum_in_two_steps(shard, axes, dim):
    far, near = axes
    pieces = split_up(shard, dim, lax.axis_size(far))
    nearer = summed_on_arrival(pieces, near, dim + 1)
    arrived = lax.all_to_all(nearer, far, split_axis=0, concat_axis=0, tiled=True)
    return arrived.sum(axis=0)


def padded_to(lines, length):
    spare = -len(lines) % length
    return jnp.pad(lines, [(0, spare)] + [(0, 0)] * (lines.ndim - 1))


def sum_by_parts(shard, axes):
    lines = shard.reshape(-1)
    own = sum_in_two_steps(
        padded_to(lines, lax.axis_size(axes[0]) * lax.axis_size(axes[1])), axes, 0
    )
    whole = whole_of(own, axes, 0)
    return whole[: len(lines)].reshape(shard.shape)


def packed_total(arrays, axis):
    ends = [0]
    for a in arrays:
        ends.append(ends[-1] + a.size)
    so_far = over_copies(jnp.concatenate([a.ravel() for a in arrays]), axis)
    return tuple((so_far[b:e].reshape(a.shape) for a, b, e in zip(arrays, ends, ends[1:])))


def factor_with(block, gram):
    lower = jnp.linalg.cholesky(gram)
    return (
        lax.linalg.triangular_solve(lower, block, left_side=False, lower=True, transpose_a=True),
        lower,
    )


def inner_gram(block):
    return jnp.dot(block.T, block, precision=HIGH, preferred_element_type=jnp.float32)


def per_device(gradient, start_block, activations, out_grads):
    row_count = gradient.shape[0]
    grad_cols = out_grads.shape[1]
    row_index = lax.axis_index(ROWS)
    col_index = lax.axis_index("cols")
    omega = start_block
    whole_left = None
    for step in range(ITERS):
        ysum = over_copies(
            jnp.dot(gradient, omega, precision=HIGH, preferred_element_type=jnp.float32), "cols"
        )
        whole_y = whole_of(ysum, (("rows_0", "rows_1"), "rows_2"), 0)
        whole_left, lower_y = factor_with(whole_y, inner_gram(whole_y))
        left = lax.dynamic_slice_in_dim(whole_left, row_index * row_count, row_count, 0)
        partial_z = jnp.dot(gradient.T, left, precision=HIGH, preferred_element_type=jnp.float32)
        zsum = sum_by_parts(partial_z, (("rows_0", "rows_1"), "rows_2"))
        zgram = over_copies(inner_gram(zsum), "cols")
        right, lower_z = factor_with(zsum, zgram)
        omega = right
    left_cols = lax.dynamic_slice_in_dim(whole_left, col_index * grad_cols, grad_cols, 0)
    left_part = jnp.dot(out_grads, left_cols, precision=HIGH, preferred_element_type=jnp.float32)
    right_part = jnp.dot(activations, right, precision=HIGH, preferred_element_type=jnp.float32)
    token_left, token_right = packed_total((left_part, right_part), "cols")
    mixed = jnp.dot(token_left, lower_z, precision=HIGH, preferred_element_type=jnp.float32)
    scores = jnp.sum(mixed * token_right, axis=1)
    return (left, right, scores)


def solution(mesh):
    torus = Mesh(
        mesh.devices.reshape(8, 8, 2, mesh.shape["cols"]), ("rows_0", "rows_1", "rows_2", "cols")
    )
    placed = (P(ROWS, "cols"), P("cols", None), P(ROWS, "cols"), P(ROWS, "cols"))
    return jax.shard_map(
        per_device,
        mesh=torus,
        in_specs=placed,
        out_specs=(P(ROWS, None), P("cols", None), P(ROWS)),
        check_vma=False,
    )
```

profile of v0, /device:TPU:16, one launch (start us, length us, event | category | flops | bytes accessed | tf_op | source)
XLA Modules:
  0.0 562.7 jit_solution(3564703122325787170)
XLA Ops:
  2.2 3.2 fusion.44
  5.5 9.7 %all_to_all.102 = f32[4,1,4096]{2,1,0:T(1,128)S(1)} all-to-all(f32[4,1,4096]{2,1,0:T(1,128)S(1)} %reshape.83), channel_id=1, replica_groups=mesh['rows_0'=8,'rows_1'=8,'rows_2'=2,'cols'=4] {'cols'}, dimensions={0} | all-to-all | bytes 131072 | tf_op jit(solution)/shard_map/all_to_all | solution.py:16
  18.3 3.4 reshape.85
  21.7 16.7 %all-to-all-start.1 = ((f32[64,1,4096]{2,1,0:T(1,128)}), f32[64,1,4096]{2,1,0:T(1,128)}, u32[]{:S(2)}, u32[]{:S(2)}) async-start(f32[64,1,4096]{2,1,0:T(1,128)} %reshape.85), calls=%async_computation.1 | async-start | bytes 2097152 | tf_op jit(solution)/shard_map/all_to_all | solution.py:16
  38.4 28.8 %all-to-all-done.1 = f32[64,1,4096]{2,1,0:T(1,128)} async-done(((f32[64,1,4096]{2,1,0:T(1,128)}), f32[64,1,4096]{2,1,0:T(1,128)}, u32[]{:S(2)}, u32[]{:S(2)}) %all-to-all-start.1) | async-done | bytes 1048608 | tf_op jit(solution)/shard_map/all_to_all | solution.py:16
  67.3 4.4 reduce.8
  71.6 2.2 reshape.86
  73.8 4.1 broadcast_in_dim.42
  77.9 5.2 reshape.87
  83.1 8.6 %all_to_all.103 = f32[2,1,262144]{2,1,0:T(1,128)} all-to-all(f32[2,1,262144]{2,1,0:T(1,128)} %reshape.87), channel_id=1, replica_groups=mesh['rows_0'=8,'rows_1'=8,'rows_2'=2,'cols'=4] {'rows_2'}, dimensions={0} | all-to-all | bytes 4194304 | tf_op jit(solution)/shard_map/all_to_all | solution.py:16
  91.7 9.6 %reduce.9 = f32[2,262144]{1,0:T(2,128)} reduce(f32[2,1,262144]{2,1,0:T(1,128)} %all_to_all.103, f32[]{:T(128)} %broadcast.55), dimensions={1}, to_apply=%all_to_all.66.reduce_sub_computation | reduce | bytes 4194308 | tf_op jit(solution)/shard_map/all_to_all | solution.py:16
  101.3 5.8 %reshape.88 = f32[2,64,64,64]{3,2,1,0:T(8,128)} reshape(f32[2,262144]{1,0:T(2,128)} %reduce.9) | data formatting | bytes 4194304
  107.1 10.6 %fusion.6 = f32[64,64]{1,0:T(8,128)S(1)} fusion(f32[2,64,64,64]{3,2,1,0:T(8,128)} %reshape.88), kind=kOutput, calls=%fused_computation.12 | convolution fusion | flops 402653184 | bytes 2113536 | tf_op jit(solution)/shard_map/dot_general | solution.py:87
  117.7 2.2 copy.66
  120.0 5.8 %cholesky.74 = f32[64,64]{1,0:T(8,128)S(1)} custom-call(f32[64,64]{1,0:T(8,128)S(1)} %fusion.28), custom_call_target="Cholesky" | custom-call | tf_op jit(solution)/shard_map/jit(cholesky)/cholesky | solution.py:79
  127.2 4.9 custom-call.10
  132.1 6.5 %convolution_bitcast_fusion.5 = f32[8192,64]{0,1:T(8,128)S(1)} fusion(f32[8192,64]{1,0:T(8,128)} %bitcast.113, f32[1,64,64]{1,2,0:T(8,128)S(1)} %custom-call.10), kind=kOutput, calls=%fused_computation.5 | convolution fusion | flops 402653184 | bytes 4210688 | tf_op jit(solution)/shard_map/triangular_solve/dot.13 | solution.py:81
  138.6 3.0 convolution_bitcast_fusion.4
  141.6 3.6 copy.69
  145.2 5.4 reshape_reshape.13
  152.3 6.1 %all_to_all.104 = f32[2,64,3696]{2,1,0:T(8,128)} all-to-all(f32[2,64,3696]{2,1,0:T(8,128)S(1)} %copy.70), channel_id=1, replica_groups=mesh['rows_0'=8,'rows_1'=8,'rows_2'=2,'cols'=4] {'rows_2'}, dimensions={0} | all-to-all | bytes 3784704 | tf_op jit(solution)/shard_map/all_to_all | solution.py:44
  160.8 34.4 %all_to_all.105 = f32[64,1,3696]{2,1,0:T(1,128)S(1)} all-to-all(f32[64,1,3696]{2,1,0:T(1,128)S(1)} %all_to_all.68), channel_id=1, replica_groups=mesh['rows_0'=8,'rows_1'=8,'rows_2'=2,'cols'=4] {'rows_0','rows_1'}, dimensions={0} | all-to-all | bytes 1892352 | tf_op jit(solution)/shard_map/all_to_all | solution.py:52
  196.2 33.4 %all_to_all.106 = f32[64,1,3696]{2,1,0:T(1,128)S(1)} all-to-all(f32[64,1,3696]{2,1,0:T(1,128)S(1)} %broadcast_in_dim.43), channel_id=1, replica_groups=mesh['rows_0'=8,'rows_1'=8,'rows_2'=2,'cols'=4] {'rows_0','rows_1'}, dimensions={0} | all-to-all | bytes 1892352 | tf_op jit(solution)/shard_map/all_to_all | solution.py:16
  229.8 5.6 %all_to_all.107 = f32[2,64,3696]{2,1,0:T(8,128)S(1)} all-to-all(f32[2,64,3696]{2,1,0:T(8,128)S(1)} %broadcast_in_dim.44), channel_id=1, replica_groups=mesh['rows_0'=8,'rows_1'=8,'rows_2'=2,'cols'=4] {'rows_2'}, dimensions={0} | all-to-all | bytes 3784704 | tf_op jit(solution)/shard_map/all_to_all | solution.py:16
  235.5 2.7 copy.71
  238.2 5.7 %reshape_reshape_reshape.6 = f32[7392,64]{1,0:T(8,128)} reshape(f32[64,2,3696]{2,1,0:T(2,128)} %copy.71) | data formatting | bytes 3784704 | tf_op jit(solution)/shard_map/reshape;reshape;reshape | solution.py:67
  243.9 9.5 %fusion.45 = f32[64,64]{1,0:T(8,128)S(1)} fusion(f32[7392,64]{1,0:T(8,128)} %reshape_reshape_reshape.6), kind=kOutput, calls=%fused_computation.68 | convolution fusion | flops 363331584 | bytes 1908736 | tf_op jit(solution)/shard_map/dot_general | solution.py:87
  253.6 8.2 %all_to_all.108 = f32[4,1,4096]{2,1,0:T(1,128)S(1)} all-to-all(f32[4,1,4096]{2,1,0:T(1,128)S(1)} %reshape.89), channel_id=1, replica_groups=mesh['rows_0'=8,'rows_1'=8,'rows_2'=2,'cols'=4] {'cols'}, dimensions={0} | all-to-all | bytes 131072 | tf_op jit(solution)/shard_map/all_to_all | solution.py:16
  262.9 5.8 %cholesky.85 = f32[64,64]{1,0:T(8,128)S(1)} custom-call(f32[64,64]{1,0:T(8,128)S(1)} %fusion.26), custom_call_target="Cholesky" | custom-call | tf_op jit(solution)/shard_map/jit(cholesky)/cholesky | solution.py:79
  270.1 4.9 custom-call.11
  275.0 5.9 %convolution_bitcast_fusion.3 = f32[7392,64]{0,1:T(8,128)S(1)} fusion(f32[7392,64]{1,0:T(8,128)} %reshape_reshape_reshape.6, f32[1,64,64]{1,2,0:T(8,128)S(1)} %custom-call.11), kind=kOutput, calls=%fused_computation.3 | convolution fusion | flops 363331584 | bytes 3801088 | tf_op jit(solution)/shard_map/triangular_solve/dot.14 | solution.py:81
  282.8 8.0 %all_to_all.109 = f32[4,1,4096]{2,1,0:T(1,128)S(1)} all-to-all(f32[4,1,4096]{2,1,0:T(1,128)S(1)} %reshape.91), channel_id=1, replica_groups=mesh['rows_0'=8,'rows_1'=8,'rows_2'=2,'cols'=4] {'cols'}, dimensions={0} | all-to-all | bytes 131072 | tf_op jit(solution)/shard_map/all_to_all | solution.py:16
  293.3 2.7 reshape.93
  296.0 33.9 %all_to_all.110 = f32[64,1,4096]{2,1,0:T(1,128)} all-to-all(f32[64,1,4096]{2,1,0:T(1,128)S(1)} %reshape.93), channel_id=1, replica_groups=mesh['rows_0'=8,'rows_1'=8,'rows_2'=2,'cols'=4] {'rows_0','rows_1'}, dimensions={0} | all-to-all | bytes 2097152 | tf_op jit(solution)/shard_map/all_to_all | solution.py:16
  330.0 4.4 reduce.12
  334.3 2.2 reshape.94
  336.5 4.1 broadcast_in_dim.48
  340.6 5.2 reshape.95
  345.8 8.6 %all_to_all.111 = f32[2,1,262144]{2,1,0:T(1,128)} all-to-all(f32[2,1,262144]{2,1,0:T(1,128)} %reshape.95), channel_id=1, replica_groups=mesh['rows_0'=8,'rows_1'=8,'rows_2'=2,'cols'=4] {'rows_2'}, dimensions={0} | all-to-all | bytes 4194304 | tf_op jit(solution)/shard_map/all_to_all | solution.py:16
  354.4 9.8 %reduce.13 = f32[2,262144]{1,0:T(2,128)} reduce(f32[2,1,262144]{2,1,0:T(1,128)} %all_to_all.111, f32[]{:T(128)} %broadcast.55), dimensions={1}, to_apply=%all_to_all.76.reduce_sub_computation | reduce | bytes 4194308 | tf_op jit(solution)/shard_map/all_to_all | solution.py:16
  364.2 5.8 %reshape.96 = f32[2,64,64,64]{3,2,1,0:T(8,128)} reshape(f32[2,262144]{1,0:T(2,128)} %reduce.13) | data formatting | bytes 4194304
  370.0 10.6 %fusion.11 = f32[64,64]{1,0:T(8,128)S(1)} fusion(f32[2,64,64,64]{3,2,1,0:T(8,128)} %reshape.96), kind=kOutput, calls=%fused_computation.13 | convolution fusion | flops 402653184 | bytes 2113536 | tf_op jit(solution)/shard_map/dot_general | solution.py:87
  380.6 2.2 copy.74
  382.9 5.8 %cholesky.96 = f32[64,64]{1,0:T(8,128)S(1)} custom-call(f32[64,64]{1,0:T(8,128)S(1)} %fusion.24), custom_call_target="Cholesky" | custom-call | tf_op jit(solution)/shard_map/jit(cholesky)/cholesky | solution.py:79
  390.1 4.9 custom-call.12
  395.0 6.4 %convolution_bitcast_fusion.2 = f32[8192,64]{0,1:T(8,128)S(1)} fusion(f32[8192,64]{1,0:T(8,128)} %bitcast.114, f32[1,64,64]{1,2,0:T(8,128)S(1)} %custom-call.12), kind=kOutput, calls=%fused_computation.2 | convolution fusion | flops 402653184 | bytes 4210688 | tf_op jit(solution)/shard_map/triangular_solve/dot.13 | solution.py:81
  402.9 3.0 convolution_bitcast_fusion.1
  405.9 3.6 copy.77
  409.5 5.4 reshape_reshape.15
  416.6 6.1 %all_to_all.112 = f32[2,64,3696]{2,1,0:T(8,128)} all-to-all(f32[2,64,3696]{2,1,0:T(8,128)S(1)} %copy.78), channel_id=1, replica_groups=mesh['rows_0'=8,'rows_1'=8,'rows_2'=2,'cols'=4] {'rows_2'}, dimensions={0} | all-to-all | bytes 3784704 | tf_op jit(solution)/shard_map/all_to_all | solution.py:44
  425.1 34.1 %all_to_all.113 = f32[64,1,3696]{2,1,0:T(1,128)S(1)} all-to-all(f32[64,1,3696]{2,1,0:T(1,128)S(1)} %all_to_all.78), channel_id=1, replica_groups=mesh['rows_0'=8,'rows_1'=8,'rows_2'=2,'cols'=4] {'rows_0','rows_1'}, dimensions={0} | all-to-all | bytes 1892352 | tf_op jit(solution)/shard_map/all_to_all | solution.py:52
  461.2 5.6 all-to-all-start.13
  466.8 28.0 %all-to-all-done.13 = f32[64,1,3696]{2,1,0:T(1,128)S(1)} async-done(((f32[64,1,3696]{2,1,0:T(1,128)}), f32[64,1,3696]{2,1,0:T(1,128)S(1)}, u32[]{:S(2)}, u32[]{:S(2)}) %all-to-all-start.13) | async-done | bytes 946208 | tf_op jit(solution)/shard_map/all_to_all | solution.py:16
  495.0 5.5 all_to_all.114
  500.5 2.7 copy.79
  503.2 5.7 %reshape_reshape_reshape.7 = f32[7392,64]{1,0:T(8,128)} reshape(f32[64,2,3696]{2,1,0:T(2,128)} %copy.79) | data formatting | bytes 3784704 | tf_op jit(solution)/shard_map/reshape;reshape;reshape | solution.py:67
  509.0 9.6 %fusion.46 = f32[64,64]{1,0:T(8,128)S(1)} fusion(f32[7392,64]{1,0:T(8,128)} %reshape_reshape_reshape.7), kind=kOutput, calls=%fused_computation.69 | convolution fusion | flops 363331584 | bytes 1908736 | tf_op jit(solution)/shard_map/dot_general | solution.py:87
  519.3 3.5 all-to-all-start.15
  524.6 3.8 all-to-all-done.15
  529.5 5.8 %cholesky.107 = f32[64,64]{1,0:T(8,128)S(1)} custom-call(f32[64,64]{1,0:T(8,128)S(1)} %fusion.22), custom_call_target="Cholesky" | custom-call | tf_op jit(solution)/shard_map/jit(cholesky)/cholesky | solution.py:79
  536.6 4.9 custom-call.13
  541.5 6.0 %convolution_bitcast_fusion = f32[7392,64]{0,1:T(8,128)S(1)} fusion(f32[7392,64]{1,0:T(8,128)} %reshape_reshape_reshape.7, f32[1,64,64]{1,2,0:T(8,128)S(1)} %custom-call.13), kind=kOutput, calls=%fused_computation | convolution fusion | flops 363331584 | bytes 3801088 | tf_op jit(solution)/shard_map/triangular_solve/dot.14 | solution.py:81
  551.3 3.3 all-to-all-start.16
  555.3 5.2 all-to-all-done.16
  (89 shorter events, 38.4 us)
Async XLA Ops:
  0.6 1.5 copy-start
  21.7 45.5 %all-to-all-start.1 = ((f32[64,1,4096]{2,1,0:T(1,128)}), f32[64,1,4096]{2,1,0:T(1,128)}, u32[]{:S(2)}, u32[]{:S(2)}) async-start(f32[64,1,4096]{2,1,0:T(1,128)} %reshape.85), calls=%async_computation.1 | async-start | bytes 2097152 | tf_op jit(solution)/shard_map/all_to_all | solution.py:16
  107.1 10.6 %copy-start.1 = (f32[2,64,64,64]{3,2,1,0:T(8,128)S(1)}, f32[2,64,64,64]{3,2,1,0:T(8,128)}, u32[]{:S(2)}) copy-start(f32[2,64,64,64]{3,2,1,0:T(8,128)} %reshape.88) | copy-start | bytes 6291460
  370.0 10.6 %copy-start.2 = (f32[2,64,64,64]{3,2,1,0:T(8,128)S(1)}, f32[2,64,64,64]{3,2,1,0:T(8,128)}, u32[]{:S(2)}) copy-start(f32[2,64,64,64]{3,2,1,0:T(8,128)} %reshape.96) | copy-start | bytes 6291460
  401.4 1.3 copy-start.4
  461.2 33.6 %all-to-all-start.13 = ((f32[64,1,3696]{2,1,0:T(1,128)}), f32[64,1,3696]{2,1,0:T(1,128)S(1)}, u32[]{:S(2)}, u32[]{:S(2)}) async-start(f32[64,1,3696]{2,1,0:T(1,128)} %broadcast_in_dim.49), calls=%async_computation.13 | async-start | bytes 1900544 | tf_op jit(solution)/shard_map/all_to_all | solution.py:16
  509.0 13.9 %copy-start.6 = (f32[64,2048]{1,0:T(8,128)S(1)}, f32[64,2048]{1,0:T(8,128)}, u32[]{:S(2)}) copy-start(f32[64,2048]{1,0:T(8,128)} %param.12) | copy-start | bytes 1572868
  519.3 9.1 %all-to-all-start.15 = ((f32[4,1,4096]{2,1,0:T(1,128)}), f32[4,1,4096]{2,1,0:T(1,128)S(1)}, u32[]{:S(2)}, u32[]{:S(2)}) async-start(f32[4,1,4096]{2,1,0:T(1,128)} %reshape.97), calls=%async_computation.15 | async-start | bytes 131072 | tf_op jit(solution)/shard_map/all_to_all | solution.py:16
  541.5 7.3 %copy-start.5 = (f32[64,7392]{1,0:T(8,128)S(1)}, f32[64,7392]{1,0:T(8,128)}, u32[]{:S(2)}) copy-start(f32[64,7392]{1,0:T(8,128)} %param.11) | copy-start | bytes 5677060
  547.5 1.3 copy-start.3
  551.3 9.3 %all-to-all-start.16 = ((f32[4,1,8192]{2,1,0:T(1,128)}), f32[4,1,8192]{2,1,0:T(1,128)S(1)}, u32[]{:S(2)}, u32[]{:S(2)}) async-start(f32[4,1,8192]{2,1,0:T(1,128)} %broadcast_in_dim.52), calls=%async_computation.16 | async-start | bytes 262144 | tf_op jit(solution)/shard_map/all_to_all | solution.py:16
where the time goes:
time: 573 us; the launch traced here: 563 us
  blocking collectives  202 us (35%)
  local copies, waits for them, and re-layouts  98.9 us (17%)
  other arithmetic  84.5 us (15%)
  matrix products  80.5 us (14%)
  waiting for transfers between devices  65.9 us (12%)
  starting transfers between devices  29.1 us (5%)
    all_to_all x9, blocking collectives, sent_to_all(): return lax.all_to_all(copies, axis, split_axis=0, concat_axis=0, tiled=True)  121 us
    all_to_all x2, blocking collectives, sum_in_two_steps(): lax.all_to_all(nearer, far, split_axis=0, concat_axis=0, tiled=True)  68.5 us
    all_to_all x4, waiting for transfers between devices, sent_to_all(): return lax.all_to_all(copies, axis, split_axis=0, concat_axis=0, tiled=True)  65.9 us
    dot_general x4, matrix products, inner_gram(): jnp.dot(block.T, block, precision=HIGH, preferred_element_type=jnp.float32)  40.2 us
    unnamed x33, local copies, waits for them, and re-layouts  39.1 us
    all_to_all x8, other arithmetic, sent_to_all(): return lax.all_to_all(copies, axis, split_axis=0, concat_axis=0, tiled=True)  31.4 us
    all_to_all x4, starting transfers between devices, sent_to_all(): return lax.all_to_all(copies, axis, split_axis=0, concat_axis=0, tiled=True)  29.1 us
    another operation x12, other arithmetic, factor_with(): lower = jnp.linalg.cholesky(gram)  26.1 us
  transfers between devices with their start and end apart: 4, of which 4 were waited for; matrix products, arithmetic and copies ran while one was open for 0% of the time, Pallas kernels for 0%

commit v1 on v0

v1 whole, which is shorter than its diff:
```python
import functools

import jax
import jax.numpy as jnp
from jax import lax
from jax.experimental import pallas as pl
from jax.experimental.pallas import tpu as pltpu
from jax.sharding import Mesh
from jax.sharding import PartitionSpec as P

ITERS = 2
R = 64
H = R // 2
LANES = 128
F32 = jnp.float32
ROWS = ("y", "z", "c")
CHIPS = ("y", "z")
PEERS = ("c", "x")
HIGH = lax.Precision.HIGHEST

VMEM = pl.BlockSpec(memory_space=pltpu.VMEM)
SMEM = pl.BlockSpec(memory_space=pltpu.SMEM)


def nn(a, b):
    return lax.dot_general(a, b, (((1,), (0,)), ((), ())), precision=HIGH, preferred_element_type=F32)


def nt(a, b):
    return lax.dot_general(a, b, (((1,), (1,)), ((), ())), precision=HIGH, preferred_element_type=F32)


def call(body, out_shape, n_in, scalars=0, scratch=()):
    specs = [SMEM] * scalars + [VMEM] * (n_in - scalars)
    outs = jax.tree.map(lambda _: VMEM, out_shape)
    return pl.pallas_call(
        body,
        out_shape=out_shape,
        in_specs=specs,
        out_specs=outs,
        scratch_shapes=list(scratch),
        compiler_params=pltpu.CompilerParams(vmem_limit_bytes=48 * 2**20),
    )


def shape(*dims):
    return jax.ShapeDtypeStruct(dims, F32)


def rsqrt(s):
    t = lax.rsqrt(s)
    return t * (1.5 - 0.5 * s * t * t)


def fold(square):
    return jnp.concatenate([square[:H], square[H:]], axis=1)


def unfold(half):
    return jnp.concatenate([half[:, :R], half[:, R:]], axis=0)


def factor(gram, rows_ref):
    b = 4
    line = lax.broadcasted_iota(jnp.int32, (R, R), 0)
    lane = lax.broadcasted_iota(jnp.int32, (R, R), 1)
    both = jnp.concatenate([gram, (line == lane).astype(F32)], axis=1)
    groups = [both[8 * g : 8 * g + 8] for g in range(R // 8)]
    sub = lax.broadcasted_iota(jnp.int32, (8, LANES), 0)
    for k in range(0, R, b):
        g0, off = divmod(k, 8)
        rows = [jnp.broadcast_to(groups[g0][off + i : off + i + 1], (8, LANES)) for i in range(b)]
        live = range(g0 if off + b < 8 else g0 + 1, R // 8)
        cols = {
            g: [jnp.broadcast_to(groups[g][:, k + j : k + j + 1], (8, LANES)) for j in range(b)]
            for g in live
        }
        low = [[None] * b for _ in range(b)]
        inv = [None] * b
        for i in range(b):
            splat = [jnp.broadcast_to(rows[i][:, k + j : k + j + 1], (8, LANES)) for j in range(i + 1)]
            for j in range(i):
                s = splat[j]
                for q in range(j):
                    s = s - low[i][q] * low[j][q]
                low[i][j] = s * inv[j]
            d = splat[i]
            for q in range(i):
                d = d - low[i][q] * low[i][q]
            inv[i] = rsqrt(d)

        def solved(lines):
            done = []
            for i in range(b):
                s = lines[i]
                for q in range(i):
                    s = s - low[i][q] * done[q]
                done.append(s * inv[i])
            return done

        new_rows = solved(rows)
        for i in range(b):
            rows_ref[k + i : k + i + 1, :] = new_rows[i][0:1]
        for g in live:
            f = solved(cols[g])
            upd = f[0] * new_rows[0]
            for i in range(1, b):
                upd = upd + f[i] * new_rows[i]
            if g == g0:
                upd = jnp.where(sub >= off + b, upd, 0.0)
            groups[g] = groups[g] - upd


def inverse_of(rows_ref):
    line = lax.broadcasted_iota(jnp.int32, (R, R), 0)
    lane = lax.broadcasted_iota(jnp.int32, (R, R), 1)
    return jnp.where(line >= lane, rows_ref[:, R:], 0.0)


def lower_t_of(rows_ref):
    line = lax.broadcasted_iota(jnp.int32, (R, R), 0)
    lane = lax.broadcasted_iota(jnp.int32, (R, R), 1)
    return jnp.where(line <= lane, rows_ref[:, :R], 0.0)


def halves_body(c_ref, a_ref, keep_ref, send_ref):
    width = keep_ref.shape[1]
    rest = a_ref.shape[1] - width

    @pl.when(c_ref[0] == 0)
    def _():
        keep_ref[...] = a_ref[:, :width]
        send_ref[...] = jnp.zeros_like(send_ref)
        send_ref[:, :rest] = a_ref[:, width:]

    @pl.when(c_ref[0] != 0)
    def _():
        send_ref[...] = a_ref[:, :width]
        keep_ref[...] = jnp.zeros_like(keep_ref)
        keep_ref[:, :rest] = a_ref[:, width:]


def swapped(core, a, width):
    lines = a.shape[0]
    keep, send = call(halves_body, (shape(lines, width), shape(lines, width)), 2, scalars=1)(core, a)
    got = lax.ppermute(send, "c", [(0, 1), (1, 0)])
    return keep, got


def first_body(g_ref, o_ref, out_ref):
    y = fold(nn(g_ref[...], o_ref[...]).T)
    for i in range(out_ref.shape[0]):
        out_ref[i] = y


def put_slots(yt, g_refs, core, out_ref):
    mine, other = g_refs[0][...], g_refs[1][...]
    low = yt[:, :R]
    high = yt[:, R:]
    a = jnp.where(core == 0, low, high)
    b = jnp.where(core == 0, high, low)
    z = nn(a, mine) + nn(b, other)
    tiles = z.shape[1] // LANES
    for t in range(tiles):
        part = z[:, t * LANES : (t + 1) * LANES]
        out_ref[2 * t] = part[:H]
        out_ref[2 * t + 1] = part[H:]
    out_ref[2 * tiles] = fold(nt(yt, yt))
    for s in range(2 * tiles + 1, out_ref.shape[0]):
        out_ref[s] = jnp.zeros((H, LANES), F32)


def spread_first_body(c_ref, got_ref, g_ref, h_ref, out_ref):
    n = got_ref.shape[0] // 2
    parts = []
    for c in range(2):
        s = got_ref[c * n]
        for i in range(1, n):
            s = s + got_ref[c * n + i]
        parts.append(unfold(s))
    yt = jnp.concatenate(parts, axis=1)
    put_slots(yt, (g_ref, h_ref), c_ref[0], out_ref)


def spread_body(c_ref, got_ref, g_ref, h_ref, out_ref, yt_ref, rows_ref):
    s = got_ref[0]
    for i in range(1, got_ref.shape[0]):
        s = s + got_ref[i]
    factor(unfold(s[R:]), rows_ref)
    yt = nn(inverse_of(rows_ref), s[:R])
    yt_ref[...] = yt
    put_slots(yt, (g_ref, h_ref), c_ref[0], out_ref)


def total_body(got_ref, out_ref):
    n = got_ref.shape[0]
    s = got_ref[0]
    for i in range(1, n):
        s = s + got_ref[i]
    for i in range(n):
        out_ref[i] = s


def total_with_body(got_ref, more_ref, out_ref):
    n = got_ref.shape[0]
    s = got_ref[0]
    for i in range(1, n):
        s = s + got_ref[i]
    more = more_ref[...]
    for i in range(n):
        out_ref[i, :H] = s
        out_ref[i, H:] = more


def gathered(z_ref, tiles):
    parts = [
        jnp.concatenate([z_ref[2 * t, :H], z_ref[2 * t + 1, :H]], axis=0) for t in range(tiles)
    ]
    return jnp.concatenate(parts, axis=1)


def both_cores(core, mine, other):
    return jnp.where(core == 0, jnp.concatenate([mine, other], axis=1), jnp.concatenate([other, mine], axis=1))


def back_body(c_ref, z_ref, g_ref, h_ref, out_ref, rows_ref):
    tiles = g_ref.shape[1] // LANES
    factor(unfold(z_ref[2 * tiles]), rows_ref)
    z = nn(inverse_of(rows_ref), gathered(z_ref, tiles))
    y = both_cores(c_ref[0], nt(z, g_ref[...]), nt(z, h_ref[...]))
    gram = fold(nt(z, z))
    for i in range(out_ref.shape[0]):
        out_ref[i, :R] = y
        out_ref[i, R:] = gram


def last_body(c_ref, z_ref, yt_ref, a_ref, b_ref, o_ref, p_ref, out_ref, inv_ref, left_ref, rows_ref):
    core = c_ref[0]
    tiles = a_ref.shape[1] // LANES
    factor(unfold(z_ref[2 * tiles, :H]), rows_ref)
    inv = inverse_of(rows_ref)
    inv_ref[...] = inv
    left = nn(inv, yt_ref[...])
    left_ref[...] = jnp.where(core == 0, left[:, :R], left[:, R:]).T
    z = nn(inv, gathered(z_ref, tiles))
    right = [nt(z, a_ref[...]), nt(z, b_ref[...])]
    far = z_ref.shape[0] // (o_ref.shape[1] // LANES)
    near = z_ref.shape[0] // far
    feats = jnp.concatenate(
        [
            jnp.concatenate([z_ref[e * near + q, H:] for e in range(far)], axis=0)
            for q in range(near)
        ],
        axis=1,
    )
    lefts = nn(inv, feats)
    both = [nt(lefts, o_ref[...]), nt(lefts, p_ref[...])]
    gram = fold(nt(z, z))
    n = out_ref.shape[0] // 2
    mine = jnp.concatenate([both[0], right[0]], axis=1)
    other = jnp.concatenate([both[1], right[1]], axis=1)
    for c in range(2):
        tokens = jnp.where(core == c, mine, other)
        for i in range(n):
            out_ref[c * n + i, :R] = tokens
            out_ref[c * n + i, R:] = gram


def finish_body(c_ref, got_ref, inv_ref, z_ref, w_ref, right_ref, scores_ref, rows_ref):
    s = got_ref[0]
    for i in range(1, got_ref.shape[0]):
        s = s + got_ref[i]
    factor(unfold(s[R:]), rows_ref)
    inv = inverse_of(rows_ref)
    mixed = nn(lower_t_of(rows_ref), s[:R, :R])
    token_right = nn(inv, s[:R, R:])
    scores_ref[...] = jnp.sum(mixed * token_right, axis=0, keepdims=True)
    whole = nn(inv, inv_ref[...])
    core = c_ref[0]
    n = right_ref.shape[0]
    tiles = -(-n // (2 * LANES))
    mine, other = gathered(z_ref, tiles), gathered(w_ref, tiles)
    for c in range(2):
        r = nn(whole, jnp.where(core == c, mine, other))
        for t in range(tiles):
            start = (c * tiles + t) * LANES
            length = min(LANES, n - start)
            right_ref[start : start + length] = r[:, t * LANES : (t + 1) * LANES].T[:length]


def exchanged(a, axes):
    return lax.all_to_all(a, axes, split_axis=0, concat_axis=0, tiled=True)


def per_device(gradient, start_block, activations, out_grads):
    far, near = lax.axis_size("y"), lax.axis_size("z")
    cols = lax.axis_size("x")
    slots, peers = far * near, 2 * cols
    core_at = lax.axis_index("c")
    core = core_at.astype(jnp.int32).reshape(1)
    n = gradient.shape[1]
    width = -(-n // (2 * LANES)) * LANES
    piece = R // peers

    first = call(first_body, shape(peers, H, LANES), 2)(gradient, start_block)
    got = exchanged(first, PEERS)
    g, h = swapped(core, gradient, width)
    a, b = swapped(core, activations, width)
    o, p = swapped(core, out_grads, out_grads.shape[1] // 2)
    square = pltpu.VMEM((R, LANES), F32)

    parts = call(spread_first_body, shape(slots, H, LANES), 4, scalars=1)(core, got, g, h)
    for step in range(ITERS):
        arrived = exchanged(parts, CHIPS)
        if step < ITERS - 1:
            sums = call(total_body, shape(slots, H, LANES), 1)(arrived)
            z = exchanged(sums, CHIPS)
            partial = call(
                back_body, shape(peers, R + H, LANES), 4, scalars=1, scratch=[square]
            )(core, z, g, h)
            got = exchanged(partial, PEERS)
            parts, yt = call(
                spread_body,
                (shape(slots, H, LANES), shape(R, LANES)),
                4,
                scalars=1,
                scratch=[square],
            )(core, got, g, h)
    eighth = lax.axis_index("x") * 2 + core_at
    mine = lax.dynamic_slice_in_dim(yt, eighth * piece, piece, 0)
    moves = []
    for ys in range(far):
        for cs in range(2):
            for xs in range(cols):
                source = (ys * 2 + cs) * cols + xs
                target = ((2 * xs + cs) * 2 + ys % 2) * cols + ys // 2
                moves.append((source, target))
    lines = lax.ppermute(mine, ("y", "c", "x"), moves)
    sums = call(total_with_body, shape(slots, H + piece, LANES), 2)(arrived, lines)
    z = exchanged(sums, CHIPS)
    w = lax.ppermute(z[:, :H], "c", [(0, 1), (1, 0)])
    partial, inv, left = call(
        last_body,
        (shape(peers, R + H, LANES), shape(R, R), shape(R, R)),
        7,
        scalars=1,
        scratch=[square],
    )(core, z, yt, a, b, o, p)
    got = exchanged(partial, PEERS)
    right, scores = call(
        finish_body, (shape(n, R), shape(1, R)), 5, scalars=1, scratch=[square]
    )(core, got, inv, z, w)
    return (left, right, scores.reshape(-1))


def solution(mesh):
    sizes = (8, 8, 2, mesh.shape["cols"])
    torus = Mesh(mesh.devices.reshape(sizes), ("y", "z", "c", "x"))
    placed = (P(ROWS, "x"), P("x", None), P(ROWS, "x"), P(ROWS, "x"))
    return jax.shard_map(
        per_device,
        mesh=torus,
        in_specs=placed,
        out_specs=(P(ROWS, None), P("x", None), P(ROWS)),
        check_vma=False,
    )
```

time: 573 us -> 249 us (0.43)
  the two profiles are of different devices: /device:TPU:16 before, /device:TPU:1 now
where the time goes in v1:
time: 249 us; the launch traced here: 248 us
  blocking collectives  109 us (44%)
  waiting for transfers between devices  51.3 us (21%)
  starting transfers between devices  39 us (16%)
  Pallas kernels  35.1 us (14%)
  local copies, waits for them, and re-layouts  13.4 us (5%)
    all_to_all x5, blocking collectives, exchanged(): return lax.all_to_all(a, axes, split_axis=0, concat_axis=0, tiled=True)  109 us
    all_to_all x2, waiting for transfers between devices, exchanged(): return lax.all_to_all(a, axes, split_axis=0, concat_axis=0, tiled=True)  28.8 us
    ppermute x1, waiting for transfers between devices, per_device(): lines = lax.ppermute(mine, ('y', 'c', 'x'), moves)  20.9 us
    all_to_all x2, starting transfers between devices, exchanged(): return lax.all_to_all(a, axes, split_axis=0, concat_axis=0, tiled=True)  15 us
    ppermute x3, starting transfers between devices, swapped(): got = lax.ppermute(send, 'c', [(0, 1), (1, 0)])  14.1 us
    unnamed x16, local copies, waits for them, and re-layouts  13.3 us
    pallas_call x1, Pallas kernels, per_device(): call(last_body, (shape(peers, R + H, LANES), shape(R, R), shape(R, R)), 7...  8.45 us
    pallas_call x1, Pallas kernels, per_device(): call(finish_body, (shape(n, R), shape(1, R)), 5, scalars=1, scratch=[squa...  7.06 us
  transfers between devices with their start and end apart: 7, of which 4 were waited for; matrix products, arithmetic and copies ran while one was open for 2% of the time, Pallas kernels for 5%

profile of v1, /device:TPU:1, one launch (start us, length us, event | category | flops | bytes accessed | tf_op | source)
XLA Modules:
  0.0 248.1 jit_solution(3368008074944281480)
XLA Ops:
  0.6 0.0 copy-start.1
  0.6 1.5 copy-done.1
  2.2 0.1 shard_map.68
  2.3 8.8 %collective-permute-start = (f32[64,3712]{1,0:T(8,128)S(1)}, f32[64,3712]{1,0:T(8,128)S(1)}, u32[]{:S(2)}, u32[]{:S(2)}) collective-permute-start(f32[64,3712]{1,0:T(8,128)S(1)} %get-tuple-element.17), channel_id=1, source_target_pairs={{0,4},{4,0},{1,5},{5,1},{2,6},{6,2},{3,7},{7,3},{8,12},{12,8},{9,1... | collective-permute-start | bytes 2850824 | tf_op jit(solution)/shard_map/ppermute | solution.py:146
  11.1 3.6 %copy.7.o_ref = f32[7392,64]{1,0:T(8,128)} copy(f32[7392,64]{0,1:T(8,128)} %param.5) | data formatting | bytes 3784704 | tf_op args[1]
  14.7 0.0 copy-start
  14.7 2.1 copy-done
  16.8 0.0 copy-start.2
  16.8 1.5 copy-done.2
  18.3 2.1 shard_map.67
  20.4 7.6 %all_to_all.35.got_ref = f32[8,32,128]{2,1,0:T(8,128)S(1)} all-to-all(f32[8,32,128]{2,1,0:T(8,128)S(1)} %shard_map.67), channel_id=1, replica_groups=mesh['y'=8,'z'=8,'c'=2,'x'=4] {'c','x'}, dimensions={0} | all-to-all | bytes 262144 | tf_op jit(solution)/shard_map/all_to_all | solution.py:292
  28.0 0.0 collective-permute-done.h_ref
  28.0 2.0 shard_map.69
  30.0 39.5 %all_to_all.36.got_ref = f32[64,32,128]{2,1,0:T(8,128)S(1)} all-to-all(f32[64,32,128]{2,1,0:T(8,128)S(1)} %shard_map.69), channel_id=1, replica_groups=mesh['y'=8,'z'=8,'c'=2,'x'=4] {'y','z'}, dimensions={0} | all-to-all | bytes 2097152 | tf_op jit(solution)/shard_map/all_to_all | solution.py:292
  69.4 0.2 shard_map.70
  69.6 35.1 %all_to_all.37.z_ref = f32[64,32,128]{2,1,0:T(8,128)S(1)} all-to-all(f32[64,32,128]{2,1,0:T(8,128)S(1)} %shard_map.70), channel_id=1, replica_groups=mesh['y'=8,'z'=8,'c'=2,'x'=4] {'y','z'}, dimensions={0} | all-to-all | bytes 2097152 | tf_op jit(solution)/shard_map/all_to_all | solution.py:292
  104.7 6.7 %shard_map.71 = f32[8,96,128]{2,1,0:T(8,128)S(1)} custom-call(s32[1]{0:T(128)} %bitcast.c_ref, f32[64,32,128]{2,1,0:T(8,128)S(1)} %all_to_all.37.z_ref, f32[64,3712]{1,0:T(8,128)S(1)} %get-tuple-element.16.g_ref, f32[64,3712]{1,0:T(8,128)S(1)} %collective-permute-done.h_ref), custom_call_target="tpu_custom_call" | custom-call | tf_op jit(solution)/shard_map/pallas_call | solution.py:318
  111.3 14.7 %all_to_all.38.got_ref = f32[8,96,128]{2,1,0:T(8,128)S(1)} all-to-all(f32[8,96,128]{2,1,0:T(8,128)S(1)} %shard_map.71), channel_id=1, replica_groups=mesh['y'=8,'z'=8,'c'=2,'x'=4] {'c','x'}, dimensions={0} | all-to-all | bytes 786432 | tf_op jit(solution)/shard_map/all_to_all | solution.py:292
  126.0 6.2 %shard_map.72 = (f32[64,32,128]{2,1,0:T(8,128)}, f32[64,128]{1,0:T(8,128)S(1)}) custom-call(s32[1]{0:T(128)} %bitcast.c_ref, f32[8,96,128]{2,1,0:T(8,128)S(1)} %all_to_all.38.got_ref, f32[64,3712]{1,0:T(8,128)S(1)} %get-tuple-element.16.g_ref, f32[64,3712]{1,0:T(8,128)S(1)} %collective-permute-done.h_ref), custom_call_target="tpu_custom_call" | custom-call | tf_op jit(solution)/shard_map/pallas_call | solution.py:322
  132.3 6.0 %all-to-all-start.4 = ((f32[64,32,128]{2,1,0:T(8,128)}), f32[64,32,128]{2,1,0:T(8,128)S(1)}, u32[]{:S(2)}, u32[]{:S(2)}) async-start(f32[64,32,128]{2,1,0:T(8,128)} %get-tuple-element.18), calls=%async_computation.4 | async-start | bytes 2097152 | tf_op jit(solution)/shard_map/all_to_all | solution.py:292
  138.3 3.8 %collective-permute-start.1 = (f32[8,128]{1,0:T(8,128)S(1)}, f32[8,128]{1,0:T(8,128)S(1)}, u32[]{:S(2)}, u32[]{:S(2)}) collective-permute-start(f32[8,128]{1,0:T(8,128)S(1)} %constant_dynamic-slice_fusion), channel_id=1, source_target_pairs={{0,0},{1,128},{2,256},{3,384},{4,64},{5,192},{6,320},{7,448},{64,4... | collective-permute-start | bytes 12296 | tf_op jit(solution)/shard_map/ppermute | solution.py:338
  142.1 20.9 %collective-permute-done.1.more_ref = f32[8,128]{1,0:T(8,128)S(1)} collective-permute-done((f32[8,128]{1,0:T(8,128)S(1)}, f32[8,128]{1,0:T(8,128)S(1)}, u32[]{:S(2)}, u32[]{:S(2)}) %collective-permute-start.1) | collective-permute-done | bytes 4128 | tf_op jit(solution)/shard_map/ppermute | solution.py:338
  163.0 2.2 all-to-all-done.4.got_ref
  165.2 1.2 shard_map.73
  166.4 0.0 copy-start.3
  166.4 9.0 %all-to-all-start.5 = ((f32[64,40,128]{2,1,0:T(8,128)}), f32[64,40,128]{2,1,0:T(8,128)S(1)}, u32[]{:S(2)}, u32[]{:S(2)}) async-start(f32[64,40,128]{2,1,0:T(8,128)} %shard_map.73), calls=%async_computation.5 | async-start | bytes 2621440 | tf_op jit(solution)/shard_map/all_to_all | solution.py:292
  175.4 0.0 copy-done.3
  175.4 1.1 shard_map.74
  176.5 0.0 copy-start.4
  176.5 1.0 copy-done.4
  177.5 0.0 copy-start.5
  177.5 3.4 %collective-permute-start.2 = (f32[64,3712]{1,0:T(8,128)}, f32[64,3712]{1,0:T(8,128)S(1)}, u32[]{:S(2)}, u32[]{:S(2)}) collective-permute-start(f32[64,3712]{1,0:T(8,128)} %get-tuple-element.21), channel_id=1, source_target_pairs={{0,4},{4,0},{1,5},{5,1},{2,6},{6,2},{3,7},{7,3},{8,12},{12,8},{9,1... | collective-permute-start | bytes 2850824 | tf_op jit(solution)/shard_map/ppermute | solution.py:146
  180.9 26.6 %all-to-all-done.5.z_ref = f32[64,40,128]{2,1,0:T(8,128)S(1)} async-done(((f32[64,40,128]{2,1,0:T(8,128)}), f32[64,40,128]{2,1,0:T(8,128)S(1)}, u32[]{:S(2)}, u32[]{:S(2)}) %all-to-all-start.5) | async-done | bytes 1310752 | tf_op jit(solution)/shard_map/all_to_all | solution.py:292
  207.5 0.0 copy-start.6
  207.5 0.1 slice.4
  207.7 6.1 %collective-permute-start.4 = (f32[64,32,128]{2,1,0:T(8,128)S(1)}, f32[64,32,128]{2,1,0:T(8,128)S(1)}, u32[]{:S(2)}, u32[]{:S(2)}) collective-permute-start(f32[64,32,128]{2,1,0:T(8,128)S(1)} %slice.4), channel_id=1, source_target_pairs={{0,4},{4,0},{1,5},{5,1},{2,6},{6,2},{3,7},{7,3},{8,12},{12,8},{9,1... | collective-permute-start | bytes 3145736 | tf_op jit(solution)/shard_map/ppermute | solution.py:341
  213.7 0.0 copy-done.6
  213.8 1.9 collective-permute-start.3
  215.7 1.5 collective-permute-done.3.p_ref
  217.2 0.0 collective-permute-done.2.b_ref
  217.2 0.0 copy-done.5
  217.2 8.4 %shard_map.76 = (f32[8,96,128]{2,1,0:T(8,128)S(1)}, f32[64,64]{1,0:T(8,128)S(1)}, f32[64,64]{1,0:T(8,128)}) custom-call(s32[1]{0:T(128)} %bitcast.c_ref, f32[64,40,128]{2,1,0:T(8,128)S(1)} %all-to-all-done.5.z_ref, f32[64,128]{1,0:T(8,128)S(1)} %get-tuple-element.19.yt_ref, f32[64,3712]{1,0:T(8,128)S(1)} %copy-done.5, ...), custom_call_target="tpu_custom_call" | custom-call | tf_op jit(solution)/shard_map/pallas_call | solution.py:342
  225.7 11.8 %all_to_all.39.got_ref = f32[8,96,128]{2,1,0:T(8,128)S(1)} all-to-all(f32[8,96,128]{2,1,0:T(8,128)S(1)} %get-tuple-element.25), channel_id=1, replica_groups=mesh['y'=8,'z'=8,'c'=2,'x'=4] {'c','x'}, dimensions={0} | all-to-all | bytes 786432 | tf_op jit(solution)/shard_map/all_to_all | solution.py:292
  237.4 0.0 collective-permute-done.4.w_ref
  237.4 7.1 %shard_map.77 = (f32[7392,64]{1,0:T(8,128)}, f32[1,64]{1,0:T(1,128)}) custom-call(s32[1]{0:T(128)} %bitcast.c_ref, f32[8,96,128]{2,1,0:T(8,128)S(1)} %all_to_all.39.got_ref, f32[64,64]{1,0:T(8,128)S(1)} %get-tuple-element.26.inv_ref, f32[64,40,128]{2,1,0:T(8,128)S(1)} %all-to-all-done.5.z_ref, f32[64,32,128]{2,1,0:T(8,128)S(1)} %collective-permute-done.4.w_ref), custom_call_target="tpu_custom_call" | custom-call | tf_op jit(solution)/shard_map/pallas_call | solution.py:350
  244.5 3.6 %copy.8 = f32[7392,64]{0,1:T(8,128)} copy(f32[7392,64]{1,0:T(8,128)} %get-tuple-element.30) | data formatting | bytes 3784704
  (2 shorter events, 0.1 us)
Async XLA Ops:
  0.6 1.5 copy-start.1
  2.3 25.7 %collective-permute-start = (f32[64,3712]{1,0:T(8,128)S(1)}, f32[64,3712]{1,0:T(8,128)S(1)}, u32[]{:S(2)}, u32[]{:S(2)}) collective-permute-start(f32[64,3712]{1,0:T(8,128)S(1)} %get-tuple-element.17), channel_id=1, source_target_pairs={{0,4},{4,0},{1,5},{5,1},{2,6},{6,2},{3,7},{7,3},{8,12},{12,8},{9,1... | collective-permute-start | bytes 2850824 | tf_op jit(solution)/shard_map/ppermute | solution.py:146
  14.7 2.1 copy-start
  16.8 1.5 copy-start.2
  132.3 33.0 %all-to-all-start.4 = ((f32[64,32,128]{2,1,0:T(8,128)}), f32[64,32,128]{2,1,0:T(8,128)S(1)}, u32[]{:S(2)}, u32[]{:S(2)}) async-start(f32[64,32,128]{2,1,0:T(8,128)} %get-tuple-element.18), calls=%async_computation.4 | async-start | bytes 2097152 | tf_op jit(solution)/shard_map/all_to_all | solution.py:292
  138.3 24.7 %collective-permute-start.1 = (f32[8,128]{1,0:T(8,128)S(1)}, f32[8,128]{1,0:T(8,128)S(1)}, u32[]{:S(2)}, u32[]{:S(2)}) collective-permute-start(f32[8,128]{1,0:T(8,128)S(1)} %constant_dynamic-slice_fusion), channel_id=1, source_target_pairs={{0,0},{1,128},{2,256},{3,384},{4,64},{5,192},{6,320},{7,448},{64,4... | collective-permute-start | bytes 12296 | tf_op jit(solution)/shard_map/ppermute | solution.py:338
  166.4 9.0 %copy-start.3 = (f32[64,7392]{1,0:T(8,128)S(1)}, f32[64,7392]{1,0:T(8,128)}, u32[]{:S(2)}) copy-start(f32[64,7392]{1,0:T(8,128)} %a_ref.4) | copy-start | bytes 5677060
  166.4 41.1 %all-to-all-start.5 = ((f32[64,40,128]{2,1,0:T(8,128)}), f32[64,40,128]{2,1,0:T(8,128)S(1)}, u32[]{:S(2)}, u32[]{:S(2)}) async-start(f32[64,40,128]{2,1,0:T(8,128)} %shard_map.73), calls=%async_computation.5 | async-start | bytes 2621440 | tf_op jit(solution)/shard_map/all_to_all | solution.py:292
  176.5 1.0 copy-start.4
  177.5 39.7 %copy-start.5 = (f32[64,3712]{1,0:T(8,128)S(1)}, f32[64,3712]{1,0:T(8,128)}, u32[]{:S(2)}) copy-start(f32[64,3712]{1,0:T(8,128)} %copy-done.4) | copy-start | bytes 2850820
  177.5 39.7 %collective-permute-start.2 = (f32[64,3712]{1,0:T(8,128)}, f32[64,3712]{1,0:T(8,128)S(1)}, u32[]{:S(2)}, u32[]{:S(2)}) collective-permute-start(f32[64,3712]{1,0:T(8,128)} %get-tuple-element.21), channel_id=1, source_target_pairs={{0,4},{4,0},{1,5},{5,1},{2,6},{6,2},{3,7},{7,3},{8,12},{12,8},{9,1... | collective-permute-start | bytes 2850824 | tf_op jit(solution)/shard_map/ppermute | solution.py:146
  207.5 6.2 %copy-start.6 = (f32[64,2048]{1,0:T(8,128)S(1)}, f32[64,2048]{1,0:T(8,128)}, u32[]{:S(2)}) copy-start(f32[64,2048]{1,0:T(8,128)} %a_ref.5) | copy-start | bytes 1572868
  207.7 29.8 %collective-permute-start.4 = (f32[64,32,128]{2,1,0:T(8,128)S(1)}, f32[64,32,128]{2,1,0:T(8,128)S(1)}, u32[]{:S(2)}, u32[]{:S(2)}) collective-permute-start(f32[64,32,128]{2,1,0:T(8,128)S(1)} %slice.4), channel_id=1, source_target_pairs={{0,4},{4,0},{1,5},{5,1},{2,6},{6,2},{3,7},{7,3},{8,12},{12,8},{9,1... | collective-permute-start | bytes 3145736 | tf_op jit(solution)/shard_map/ppermute | solution.py:341
  213.8 3.4 %collective-permute-start.3 = (f32[64,1024]{1,0:T(8,128)S(1)}, f32[64,1024]{1,0:T(8,128)S(1)}, u32[]{:S(2)}, u32[]{:S(2)}) collective-permute-start(f32[64,1024]{1,0:T(8,128)S(1)} %get-tuple-element.23), channel_id=1, source_target_pairs={{0,4},{4,0},{1,5},{5,1},{2,6},{6,2},{3,7},{7,3},{8,12},{12,8},{9,1... | collective-permute-start | bytes 786440 | tf_op jit(solution)/shard_map/ppermute | solution.py:146

commit v2 on v1

--- a/solution.py
+++ b/solution.py
@@ -28,6 +28,35 @@
 
 def nt(a, b):
     return lax.dot_general(a, b, (((1,), (1,)), ((), ())), precision=HIGH, preferred_element_type=F32)
+
+
+def split(a):
+    high = a.astype(jnp.bfloat16)
+    return high, (a - high.astype(F32)).astype(jnp.bfloat16)
+
+
+def dot(a, b, dims):
+    return lax.dot_general(a, b, (dims, ((), ())), preferred_element_type=F32)
+
+
+def product(a, b):
+    ah, al = split(a)
+    bh, bl = split(b)
+    dims = ((1,), (0,))
+    return dot(ah, bh, dims) + (dot(al, bh, dims) + dot(ah, bl, dims))
+
+
+def against(lines, z):
+    n = lines.shape[0]
+    gh, gl = split(lines)
+    zh, zl = split(z)
+    dims = ((1,), (1,))
+    one = dot(jnp.concatenate([gh, gl, zh, zl], axis=0), zh, dims)
+    two = dot(jnp.concatenate([gh, zl], axis=0), zl, dims)
+    y = one[:n] + (one[n : 2 * n] + two[:n])
+    cross = one[2 * n + R :]
+    gram = one[2 * n : 2 * n + R] + (cross + cross.T + two[n:])
+    return y.T, gram
 
 
 def call(body, out_shape, n_in, scalars=0, scratch=()):
@@ -61,7 +90,7 @@
 
 
 def factor(gram, rows_ref):
-    b = 4
+    b = 8
     line = lax.broadcasted_iota(jnp.int32, (R, R), 0)
     lane = lax.broadcasted_iota(jnp.int32, (R, R), 1)
     both = jnp.concatenate([gram, (line == lane).astype(F32)], axis=1)
@@ -123,43 +152,54 @@
     return jnp.where(line <= lane, rows_ref[:, :R], 0.0)
 
 
-def halves_body(c_ref, a_ref, keep_ref, send_ref):
+def halves(core, a_ref, keep_ref, send_ref):
     width = keep_ref.shape[1]
     rest = a_ref.shape[1] - width
 
-    @pl.when(c_ref[0] == 0)
+    @pl.when(core == 0)
     def _():
         keep_ref[...] = a_ref[:, :width]
-        send_ref[...] = jnp.zeros_like(send_ref)
         send_ref[:, :rest] = a_ref[:, width:]
-
-    @pl.when(c_ref[0] != 0)
+        if rest < width:
+            send_ref[:, rest:] = jnp.zeros((send_ref.shape[0], width - rest), F32)
+
+    @pl.when(core != 0)
     def _():
         send_ref[...] = a_ref[:, :width]
-        keep_ref[...] = jnp.zeros_like(keep_ref)
         keep_ref[:, :rest] = a_ref[:, width:]
+        if rest < width:
+            keep_ref[:, rest:] = jnp.zeros((send_ref.shape[0], width - rest), F32)
+
+
+def halves_body(c_ref, a_ref, keep_ref, send_ref):
+    halves(c_ref[0], a_ref, keep_ref, send_ref)
 
 
 def swapped(core, a, width):
     lines = a.shape[0]
     keep, send = call(halves_body, (shape(lines, width), shape(lines, width)), 2, scalars=1)(core, a)
-    got = lax.ppermute(send, "c", [(0, 1), (1, 0)])
-    return keep, got
-
-
-def first_body(g_ref, o_ref, out_ref):
-    y = fold(nn(g_ref[...], o_ref[...]).T)
+    return keep, other_core(send)
+
+
+def other_core(a):
+    return lax.ppermute(a, "c", [(0, 1), (1, 0)])
+
+
+def first_body(c_ref, g_ref, o_ref, out_ref, keep_ref, send_ref):
+    gh, gl = split(g_ref[...])
+    oh, ol = split(o_ref[...])
+    dims = ((1,), (1,))
+    n = g_ref.shape[0]
+    one = dot(jnp.concatenate([gh, gl], axis=0), oh, dims)
+    y = fold((one[:n] + (one[n:] + dot(gh, ol, dims))).T)
     for i in range(out_ref.shape[0]):
         out_ref[i] = y
+    halves(c_ref[0], g_ref, keep_ref, send_ref)
 
 
 def put_slots(yt, g_refs, core, out_ref):
-    mine, other = g_refs[0][...], g_refs[1][...]
-    low = yt[:, :R]
-    high = yt[:, R:]
-    a = jnp.where(core == 0, low, high)
-    b = jnp.where(core == 0, high, low)
-    z = nn(a, mine) + nn(b, other)
+    lines = jnp.concatenate([g_refs[0][...], g_refs[1][...]], axis=0)
+    z = product(in_turn(core, yt), lines)
     tiles = z.shape[1] // LANES
     for t in range(tiles):
         part = z[:, t * LANES : (t + 1) * LANES]
@@ -219,16 +259,18 @@
     return jnp.concatenate(parts, axis=1)
 
 
-def both_cores(core, mine, other):
-    return jnp.where(core == 0, jnp.concatenate([mine, other], axis=1), jnp.concatenate([other, mine], axis=1))
+def in_turn(core, pair):
+    turned = jnp.concatenate([pair[:, R:], pair[:, :R]], axis=1)
+    return jnp.where(core == 0, pair, turned)
 
 
 def back_body(c_ref, z_ref, g_ref, h_ref, out_ref, rows_ref):
     tiles = g_ref.shape[1] // LANES
     factor(unfold(z_ref[2 * tiles]), rows_ref)
-    z = nn(inverse_of(rows_ref), gathered(z_ref, tiles))
-    y = both_cores(c_ref[0], nt(z, g_ref[...]), nt(z, h_ref[...]))
-    gram = fold(nt(z, z))
+    z = product(inverse_of(rows_ref), gathered(z_ref, tiles))
+    y, gram = against(jnp.concatenate([g_ref[...], h_ref[...]], axis=0), z)
+    y = in_turn(c_ref[0], y)
+    gram = fold(gram)
     for i in range(out_ref.shape[0]):
         out_ref[i, :R] = y
         out_ref[i, R:] = gram
@@ -242,10 +284,10 @@
     inv_ref[...] = inv
     left = nn(inv, yt_ref[...])
     left_ref[...] = jnp.where(core == 0, left[:, :R], left[:, R:]).T
-    z = nn(inv, gathered(z_ref, tiles))
-    right = [nt(z, a_ref[...]), nt(z, b_ref[...])]
-    far = z_ref.shape[0] // (o_ref.shape[1] // LANES)
-    near = z_ref.shape[0] // far
+    z = product(inv, gathered(z_ref, tiles))
+    rights, gram = against(jnp.concatenate([a_ref[...], b_ref[...]], axis=0), z)
+    near = o_ref.shape[1] // LANES
+    far = z_ref.shape[0] // near
     feats = jnp.concatenate(
         [
             jnp.concatenate([z_ref[e * near + q, H:] for e in range(far)], axis=0)
@@ -253,12 +295,11 @@
         ],
         axis=1,
     )
-    lefts = nn(inv, feats)
-    both = [nt(lefts, o_ref[...]), nt(lefts, p_ref[...])]
-    gram = fold(nt(z, z))
+    lefts, _ = against(jnp.concatenate([o_ref[...], p_ref[...]], axis=0), nn(inv, feats))
+    gram = fold(gram)
     n = out_ref.shape[0] // 2
-    mine = jnp.concatenate([both[0], right[0]], axis=1)
-    other = jnp.concatenate([both[1], right[1]], axis=1)
+    mine = jnp.concatenate([lefts[:, :R], rights[:, :R]], axis=1)
+    other = jnp.concatenate([lefts[:, R:], rights[:, R:]], axis=1)
     for c in range(2):
         tokens = jnp.where(core == c, mine, other)
         for i in range(n):
@@ -277,15 +318,12 @@
     scores_ref[...] = jnp.sum(mixed * token_right, axis=0, keepdims=True)
     whole = nn(inv, inv_ref[...])
     core = c_ref[0]
-    n = right_ref.shape[0]
+    n = right_ref.shape[1]
     tiles = -(-n // (2 * LANES))
+    width = tiles * LANES
     mine, other = gathered(z_ref, tiles), gathered(w_ref, tiles)
-    for c in range(2):
-        r = nn(whole, jnp.where(core == c, mine, other))
-        for t in range(tiles):
-            start = (c * tiles + t) * LANES
-            length = min(LANES, n - start)
-            right_ref[start : start + length] = r[:, t * LANES : (t + 1) * LANES].T[:length]
+    right_ref[:, :width] = product(whole, jnp.where(core == 0, mine, other))
+    right_ref[:, width:] = product(whole, jnp.where(core == 0, other, mine))[:, : n - width]
 
 
 def exchanged(a, axes):
@@ -302,9 +340,12 @@
     width = -(-n // (2 * LANES)) * LANES
     piece = R // peers
 
-    first = call(first_body, shape(peers, H, LANES), 2)(gradient, start_block)
+    lines = gradient.shape[0]
+    first, g, send = call(
+        first_body, (shape(peers, H, LANES), shape(lines, width), shape(lines, width)), 3, scalars=1
+    )(core, gradient, start_block.T)
+    h = other_core(send)
     got = exchanged(first, PEERS)
-    g, h = swapped(core, gradient, width)
     a, b = swapped(core, activations, width)
     o, p = swapped(core, out_grads, out_grads.shape[1] // 2)
     square = pltpu.VMEM((R, LANES), F32)
@@ -313,6 +354,7 @@
     for step in range(ITERS):
         arrived = exchanged(parts, CHIPS)
         if step < ITERS - 1:
+            arrived, a, b, o, p = lax.optimization_barrier((arrived, a, b, o, p))
             sums = call(total_body, shape(slots, H, LANES), 1)(arrived)
             z = exchanged(sums, CHIPS)
             partial = call(
@@ -338,7 +380,7 @@
     lines = lax.ppermute(mine, ("y", "c", "x"), moves)
     sums = call(total_with_body, shape(slots, H + piece, LANES), 2)(arrived, lines)
     z = exchanged(sums, CHIPS)
-    w = lax.ppermute(z[:, :H], "c", [(0, 1), (1, 0)])
+    w = other_core(z[:, :H])
     partial, inv, left = call(
         last_body,
         (shape(peers, R + H, LANES), shape(R, R), shape(R, R)),
@@ -348,9 +390,9 @@
     )(core, z, yt, a, b, o, p)
     got = exchanged(partial, PEERS)
     right, scores = call(
-        finish_body, (shape(n, R), shape(1, R)), 5, scalars=1, scratch=[square]
+        finish_body, (shape(R, n), shape(1, R)), 5, scalars=1, scratch=[square]
     )(core, got, inv, z, w)
-    return (left, right, scores.reshape(-1))
+    return (left, right.T, scores.reshape(-1))
 
 
 def solution(mesh):

time: 249 us -> 224 us (0.90)
  Pallas kernels: 35.1 us -> 21.9 us
  waiting for transfers between devices: 51.3 us -> 41.2 us
  local copies, waits for them, and re-layouts: 13.4 us -> 7.29 us
  starting transfers between devices: 39 us -> 41.7 us
    all_to_all x2, waiting for transfers between devices: 28.8 us -> 18.8 us  [exchanged(): return lax.all_to_all(a, axes, split_axis=0, concat_axis=0, tiled=True)]
    unnamed x16 -> x20, local copies, waits for them, and re-layouts: 13.3 us -> 7.16 us
    all_to_all x2, starting transfers between devices: 15 us -> 18.9 us  [exchanged(): return lax.all_to_all(a, axes, split_axis=0, concat_axis=0, tiled=True)]
    pallas_call x2, Pallas kernels: 9.16 us -> 5.91 us  [the longest x1 4.72 us: per_device(): call(finish_body, (shape(R, n), shape(1, R)), 5, scalars=1, scratch=[squa...]
    pallas_call x1, Pallas kernels: 8.45 us -> 5.21 us  [per_device(): call(last_body, (shape(peers, R + H, LANES), shape(R, R), shape(R, R)), 7...]
  transfers between devices with their start and end apart: 7 -> 7, of which waited for: 4 -> 4; matrix products, arithmetic and copies ran while one was open for 2% -> 0% of each run, Pallas kernels for 5% -> 2%
where the time goes in v2:
time: 224 us; the launch traced here: 223 us
  blocking collectives  110 us (49%)
  starting transfers between devices  41.7 us (19%)
  waiting for transfers between devices  41.2 us (18%)
  Pallas kernels  21.9 us (10%)
  local copies, waits for them, and re-layouts  7.29 us (3%)
    all_to_all x5, blocking collectives, exchanged(): return lax.all_to_all(a, axes, split_axis=0, concat_axis=0, tiled=True)  110 us
    ppermute x1, waiting for transfers between devices, per_device(): lines = lax.ppermute(mine, ('y', 'c', 'x'), moves)  20.9 us
    ppermute x4, starting transfers between devices, other_core(): return lax.ppermute(a, 'c', [(0, 1), (1, 0)])  19.1 us
    all_to_all x2, starting transfers between devices, exchanged(): return lax.all_to_all(a, axes, split_axis=0, concat_axis=0, tiled=True)  18.9 us
    all_to_all x2, waiting for transfers between devices, exchanged(): return lax.all_to_all(a, axes, split_axis=0, concat_axis=0, tiled=True)  18.8 us
    unnamed x20, local copies, waits for them, and re-layouts  7.16 us
    pallas_call x1, Pallas kernels, per_device(): call(last_body, (shape(peers, R + H, LANES), shape(R, R), shape(R, R)), 7...  5.21 us
    pallas_call x1, Pallas kernels, per_device(): call(finish_body, (shape(R, n), shape(1, R)), 5, scalars=1, scratch=[squa...  4.72 us
  transfers between devices with their start and end apart: 7, of which 4 were waited for; matrix products, arithmetic and copies ran while one was open for 0% of the time, Pallas kernels for 2%

profile of v2, /device:TPU:1, one launch (start us, length us, event | category | flops | bytes accessed | tf_op | source)
XLA Modules:
  0.0 222.9 jit_solution(7623629091505430642)
XLA Ops:
  0.6 0.0 copy-start
  0.6 1.5 copy-done
  2.2 0.0 copy-start.1
  2.2 1.5 copy-done.1
  3.7 1.2 shard_map.67
  4.9 8.7 %collective-permute-start = (f32[64,3712]{1,0:T(8,128)S(1)}, f32[64,3712]{1,0:T(8,128)S(1)}, u32[]{:S(2)}, u32[]{:S(2)}) collective-permute-start(f32[64,3712]{1,0:T(8,128)S(1)} %get-tuple-element.24), channel_id=1, source_target_pairs={{0,4},{4,0},{1,5},{5,1},{2,6},{6,2},{3,7},{7,3},{8,12},{12,8},{9,1... | collective-permute-start | bytes 2850824 | tf_op jit(solution)/shard_map/ppermute | solution.py:185
  13.6 7.5 %all_to_all.35.got_ref = f32[8,32,128]{2,1,0:T(8,128)S(1)} all-to-all(f32[8,32,128]{2,1,0:T(8,128)S(1)} %get-tuple-element.22), channel_id=1, replica_groups=mesh['y'=8,'z'=8,'c'=2,'x'=4] {'c','x'}, dimensions={0} | all-to-all | bytes 262144 | tf_op jit(solution)/shard_map/all_to_all | solution.py:330
  21.1 0.0 collective-permute-done.h_ref
  21.1 1.8 shard_map.68
  23.0 0.0 copy-start.7
  23.0 12.9 %all-to-all-start.1 = ((f32[64,32,128]{2,1,0:T(8,128)}), f32[64,32,128]{2,1,0:T(8,128)S(1)}, u32[]{:S(2)}, u32[]{:S(2)}) async-start(f32[64,32,128]{2,1,0:T(8,128)} %shard_map.68), calls=%async_computation.1 | async-start | bytes 2097152 | tf_op jit(solution)/shard_map/all_to_all | solution.py:330
  35.8 0.0 copy-start.2
  35.9 1.5 copy-done.2
  37.4 0.1 shard_map.69
  37.5 0.0 copy-start.3
  37.5 0.9 copy-done.3
  38.5 2.6 %collective-permute-start.1 = (f32[64,3712]{1,0:T(8,128)S(1)}, f32[64,3712]{1,0:T(8,128)S(1)}, u32[]{:S(2)}, u32[]{:S(2)}) collective-permute-start(f32[64,3712]{1,0:T(8,128)S(1)} %get-tuple-element.26), channel_id=1, source_target_pairs={{0,4},{4,0},{1,5},{5,1},{2,6},{6,2},{3,7},{7,3},{8,12},{12,8},{9,1... | collective-permute-start | bytes 2850824 | tf_op jit(solution)/shard_map/ppermute | solution.py:185
  41.0 0.0 copy-done.7
  41.1 0.0 copy-start.8
  41.1 0.7 copy-done.8
  41.8 1.9 collective-permute-start.2
  43.7 1.5 collective-permute-done.2.p_ref
  45.2 0.0 collective-permute-done.1.b_ref
  45.2 0.0 copy-start.5
  45.2 1.0 copy-done.5
  46.2 16.6 %all-to-all-done.1.got_ref = f32[64,32,128]{2,1,0:T(8,128)S(1)} async-done(((f32[64,32,128]{2,1,0:T(8,128)}), f32[64,32,128]{2,1,0:T(8,128)S(1)}, u32[]{:S(2)}, u32[]{:S(2)}) %all-to-all-start.1) | async-done | bytes 1048608 | tf_op jit(solution)/shard_map/all_to_all | solution.py:330
  62.8 0.2 shard_map.71
  63.0 35.1 %all_to_all.36.z_ref = f32[64,32,128]{2,1,0:T(8,128)S(1)} all-to-all(f32[64,32,128]{2,1,0:T(8,128)S(1)} %shard_map.71), channel_id=1, replica_groups=mesh['y'=8,'z'=8,'c'=2,'x'=4] {'y','z'}, dimensions={0} | all-to-all | bytes 2097152 | tf_op jit(solution)/shard_map/all_to_all | solution.py:330
  98.0 4.2 %shard_map.72 = f32[8,96,128]{2,1,0:T(8,128)S(1)} custom-call(s32[1]{0:T(128)} %bitcast.c_ref, f32[64,32,128]{2,1,0:T(8,128)S(1)} %all_to_all.36.z_ref, f32[64,3712]{1,0:T(8,128)S(1)} %get-tuple-element.23.g_ref, f32[64,3712]{1,0:T(8,128)S(1)} %collective-permute-done.h_ref), custom_call_target="tpu_custom_call" | custom-call | tf_op jit(solution)/shard_map/pallas_call | solution.py:360
  102.3 14.6 %all_to_all.37.got_ref = f32[8,96,128]{2,1,0:T(8,128)S(1)} all-to-all(f32[8,96,128]{2,1,0:T(8,128)S(1)} %shard_map.72), channel_id=1, replica_groups=mesh['y'=8,'z'=8,'c'=2,'x'=4] {'c','x'}, dimensions={0} | all-to-all | bytes 786432 | tf_op jit(solution)/shard_map/all_to_all | solution.py:330
  116.9 4.2 %shard_map.73 = (f32[64,32,128]{2,1,0:T(8,128)}, f32[64,128]{1,0:T(8,128)S(1)}) custom-call(s32[1]{0:T(128)} %bitcast.c_ref, f32[8,96,128]{2,1,0:T(8,128)S(1)} %all_to_all.37.got_ref, f32[64,3712]{1,0:T(8,128)S(1)} %get-tuple-element.23.g_ref, f32[64,3712]{1,0:T(8,128)S(1)} %collective-permute-done.h_ref), custom_call_target="tpu_custom_call" | custom-call | tf_op jit(solution)/shard_map/pallas_call | solution.py:364
  121.1 6.0 %all-to-all-start.4 = ((f32[64,32,128]{2,1,0:T(8,128)}), f32[64,32,128]{2,1,0:T(8,128)S(1)}, u32[]{:S(2)}, u32[]{:S(2)}) async-start(f32[64,32,128]{2,1,0:T(8,128)} %get-tuple-element.30), calls=%async_computation.4 | async-start | bytes 2097152 | tf_op jit(solution)/shard_map/all_to_all | solution.py:330
  127.2 3.8 %collective-permute-start.3 = (f32[8,128]{1,0:T(8,128)S(1)}, f32[8,128]{1,0:T(8,128)S(1)}, u32[]{:S(2)}, u32[]{:S(2)}) collective-permute-start(f32[8,128]{1,0:T(8,128)S(1)} %constant_dynamic-slice_fusion), channel_id=1, source_target_pairs={{0,0},{1,128},{2,256},{3,384},{4,64},{5,192},{6,320},{7,448},{64,4... | collective-permute-start | bytes 12296 | tf_op jit(solution)/shard_map/ppermute | solution.py:380
  130.9 20.9 %collective-permute-done.3.more_ref = f32[8,128]{1,0:T(8,128)S(1)} collective-permute-done((f32[8,128]{1,0:T(8,128)S(1)}, f32[8,128]{1,0:T(8,128)S(1)}, u32[]{:S(2)}, u32[]{:S(2)}) %collective-permute-start.3) | collective-permute-done | bytes 4128 | tf_op jit(solution)/shard_map/ppermute | solution.py:380
  151.8 2.2 %all-to-all-done.4.got_ref = f32[64,32,128]{2,1,0:T(8,128)S(1)} async-done(((f32[64,32,128]{2,1,0:T(8,128)}), f32[64,32,128]{2,1,0:T(8,128)S(1)}, u32[]{:S(2)}, u32[]{:S(2)}) %all-to-all-start.4) | async-done | bytes 1048608 | tf_op jit(solution)/shard_map/all_to_all | solution.py:330
  154.1 0.1 shard_map.74
  154.2 0.0 copy-start.4
  154.2 0.0 copy-start.6
  154.2 0.0 copy-start.9
  154.3 40.9 %all_to_all.38.z_ref = f32[64,40,128]{2,1,0:T(8,128)S(1)} all-to-all(f32[64,40,128]{2,1,0:T(8,128)S(1)} %shard_map.74), channel_id=1, replica_groups=mesh['y'=8,'z'=8,'c'=2,'x'=4] {'y','z'}, dimensions={0} | all-to-all | bytes 2621440 | tf_op jit(solution)/shard_map/all_to_all | solution.py:330
  195.2 0.1 slice.4
  195.3 5.9 %collective-permute-start.4 = (f32[64,32,128]{2,1,0:T(8,128)S(1)}, f32[64,32,128]{2,1,0:T(8,128)S(1)}, u32[]{:S(2)}, u32[]{:S(2)}) collective-permute-start(f32[64,32,128]{2,1,0:T(8,128)S(1)} %slice.4), channel_id=1, source_target_pairs={{0,4},{4,0},{1,5},{5,1},{2,6},{6,2},{3,7},{7,3},{8,12},{12,8},{9,1... | collective-permute-start | bytes 3145736 | tf_op jit(solution)/shard_map/ppermute | solution.py:185
  201.2 0.0 copy-done.4
  201.2 0.0 copy-done.6
  201.2 0.0 copy-done.9
  201.3 5.2 %shard_map.75 = (f32[8,96,128]{2,1,0:T(8,128)S(1)}, f32[64,64]{1,0:T(8,128)S(1)}, f32[64,64]{1,0:T(8,128)}) custom-call(s32[1]{0:T(128)} %bitcast.c_ref, f32[64,40,128]{2,1,0:T(8,128)S(1)} %all_to_all.38.z_ref, f32[64,128]{1,0:T(8,128)S(1)} %get-tuple-element.31.yt_ref, f32[64,3712]{1,0:T(8,128)S(1)} %copy-done.4, f32[64,3712]{1,0:T(8,128)S(1)} %copy-done.6, ...), custom_call_target="tpu_custom_call" | custom-call | tf_op jit(solution)/shard_map/pallas_call | solution.py:384
  206.5 11.7 %all_to_all.39.got_ref = f32[8,96,128]{2,1,0:T(8,128)S(1)} all-to-all(f32[8,96,128]{2,1,0:T(8,128)S(1)} %get-tuple-element.37), channel_id=1, replica_groups=mesh['y'=8,'z'=8,'c'=2,'x'=4] {'c','x'}, dimensions={0} | all-to-all | bytes 786432 | tf_op jit(solution)/shard_map/all_to_all | solution.py:330
  218.2 0.0 collective-permute-done.4.w_ref
  218.2 4.7 %shard_map.76 = (f32[64,7392]{1,0:T(8,128)}, f32[1,64]{1,0:T(1,128)}) custom-call(s32[1]{0:T(128)} %bitcast.c_ref, f32[8,96,128]{2,1,0:T(8,128)S(1)} %all_to_all.39.got_ref, f32[64,64]{1,0:T(8,128)S(1)} %get-tuple-element.38.inv_ref, f32[64,40,128]{2,1,0:T(8,128)S(1)} %all_to_all.38.z_ref, f32[64,32,128]{2,1,0:T(8,128)S(1)} %collective-permute-done.4.w_ref), custom_call_target="tpu_custom_call" | custom-call | tf_op jit(solution)/shard_map/pallas_call | solution.py:392
  (2 shorter events, 0.1 us)
Async XLA Ops:
  0.6 1.5 copy-start
  2.2 1.5 copy-start.1
  4.9 16.3 %collective-permute-start = (f32[64,3712]{1,0:T(8,128)S(1)}, f32[64,3712]{1,0:T(8,128)S(1)}, u32[]{:S(2)}, u32[]{:S(2)}) collective-permute-start(f32[64,3712]{1,0:T(8,128)S(1)} %get-tuple-element.24), channel_id=1, source_target_pairs={{0,4},{4,0},{1,5},{5,1},{2,6},{6,2},{3,7},{7,3},{8,12},{12,8},{9,1... | collective-permute-start | bytes 2850824 | tf_op jit(solution)/shard_map/ppermute | solution.py:185
  23.0 18.1 %copy-start.7 = (f32[64,2048]{1,0:T(8,128)S(1)}, f32[64,2048]{1,0:T(8,128)}, u32[]{:S(2)}) copy-start(f32[64,2048]{1,0:T(8,128)} %a_ref.3) | copy-start | bytes 1572868
  23.0 39.8 %all-to-all-start.1 = ((f32[64,32,128]{2,1,0:T(8,128)}), f32[64,32,128]{2,1,0:T(8,128)S(1)}, u32[]{:S(2)}, u32[]{:S(2)}) async-start(f32[64,32,128]{2,1,0:T(8,128)} %shard_map.68), calls=%async_computation.1 | async-start | bytes 2097152 | tf_op jit(solution)/shard_map/all_to_all | solution.py:330
  35.8 1.5 copy-start.2
  37.5 1.0 copy-start.3
  38.5 6.8 %collective-permute-start.1 = (f32[64,3712]{1,0:T(8,128)S(1)}, f32[64,3712]{1,0:T(8,128)S(1)}, u32[]{:S(2)}, u32[]{:S(2)}) collective-permute-start(f32[64,3712]{1,0:T(8,128)S(1)} %get-tuple-element.26), channel_id=1, source_target_pairs={{0,4},{4,0},{1,5},{5,1},{2,6},{6,2},{3,7},{7,3},{8,12},{12,8},{9,1... | collective-permute-start | bytes 2850824 | tf_op jit(solution)/shard_map/ppermute | solution.py:185
  41.1 0.7 copy-start.8
  41.8 3.4 %collective-permute-start.2 = (f32[64,1024]{1,0:T(8,128)S(1)}, f32[64,1024]{1,0:T(8,128)S(1)}, u32[]{:S(2)}, u32[]{:S(2)}) collective-permute-start(f32[64,1024]{1,0:T(8,128)S(1)} %get-tuple-element.28), channel_id=1, source_target_pairs={{0,4},{4,0},{1,5},{5,1},{2,6},{6,2},{3,7},{7,3},{8,12},{12,8},{9,1... | collective-permute-start | bytes 786440 | tf_op jit(solution)/shard_map/ppermute | solution.py:185
  45.2 1.0 copy-start.5
  121.1 33.0 %all-to-all-start.4 = ((f32[64,32,128]{2,1,0:T(8,128)}), f32[64,32,128]{2,1,0:T(8,128)S(1)}, u32[]{:S(2)}, u32[]{:S(2)}) async-start(f32[64,32,128]{2,1,0:T(8,128)} %get-tuple-element.30), calls=%async_computation.4 | async-start | bytes 2097152 | tf_op jit(solution)/shard_map/all_to_all | solution.py:330
  127.2 24.7 %collective-permute-start.3 = (f32[8,128]{1,0:T(8,128)S(1)}, f32[8,128]{1,0:T(8,128)S(1)}, u32[]{:S(2)}, u32[]{:S(2)}) collective-permute-start(f32[8,128]{1,0:T(8,128)S(1)} %constant_dynamic-slice_fusion), channel_id=1, source_target_pairs={{0,0},{1,128},{2,256},{3,384},{4,64},{5,192},{6,320},{7,448},{64,4... | collective-permute-start | bytes 12296 | tf_op jit(solution)/shard_map/ppermute | solution.py:380
  154.2 47.0 %copy-start.4 = (f32[64,3712]{1,0:T(8,128)S(1)}, f32[64,3712]{1,0:T(8,128)}, u32[]{:S(2)}) copy-start(f32[64,3712]{1,0:T(8,128)} %copy-done.3) | copy-start | bytes 2850820
  154.2 47.0 %copy-start.6 = (f32[64,3712]{1,0:T(8,128)S(1)}, f32[64,3712]{1,0:T(8,128)}, u32[]{:S(2)}) copy-start(f32[64,3712]{1,0:T(8,128)} %copy-done.5) | copy-start | bytes 2850820
  154.2 47.0 %copy-start.9 = (f32[64,1024]{1,0:T(8,128)S(1)}, f32[64,1024]{1,0:T(8,128)}, u32[]{:S(2)}) copy-start(f32[64,1024]{1,0:T(8,128)} %copy-done.8) | copy-start | bytes 786436
  195.3 22.9 %collective-permute-start.4 = (f32[64,32,128]{2,1,0:T(8,128)S(1)}, f32[64,32,128]{2,1,0:T(8,128)S(1)}, u32[]{:S(2)}, u32[]{:S(2)}) collective-permute-start(f32[64,32,128]{2,1,0:T(8,128)S(1)} %slice.4), channel_id=1, source_target_pairs={{0,4},{4,0},{1,5},{5,1},{2,6},{6,2},{3,7},{7,3},{8,12},{12,8},{9,1... | collective-permute-start | bytes 3145736 | tf_op jit(solution)/shard_map/ppermute | solution.py:185

commit v3 on v2

--- a/solution.py
+++ b/solution.py
@@ -1,5 +1,3 @@
-import functools
-
 import jax
 import jax.numpy as jnp
 from jax import lax
@@ -8,7 +6,6 @@
 from jax.sharding import Mesh
 from jax.sharding import PartitionSpec as P
 
-ITERS = 2
 R = 64
 H = R // 2
 LANES = 128
@@ -32,7 +29,9 @@
 
 def split(a):
     high = a.astype(jnp.bfloat16)
-    return high, (a - high.astype(F32)).astype(jnp.bfloat16)
+    rest = a - high.astype(F32)
+    middle = rest.astype(jnp.bfloat16)
+    return high, middle, (rest - middle.astype(F32)).astype(jnp.bfloat16)
 
 
 def dot(a, b, dims):
@@ -40,23 +39,31 @@
 
 
 def product(a, b):
-    ah, al = split(a)
-    bh, bl = split(b)
+    n = a.shape[0]
+    lines = jnp.concatenate(split(a), axis=0)
+    high, middle, low = split(b)
     dims = ((1,), (0,))
-    return dot(ah, bh, dims) + (dot(al, bh, dims) + dot(ah, bl, dims))
+    one = dot(lines, high, dims)
+    two = dot(lines[: 2 * n], middle, dims)
+    three = dot(lines[:n], low, dims)
+    return one[:n] + (one[n : 2 * n] + two[:n] + (one[2 * n :] + two[n:] + three))
 
 
 def against(lines, z):
+    parts = split(z)
+    blocks = [*split(lines), *parts]
     n = lines.shape[0]
-    gh, gl = split(lines)
-    zh, zl = split(z)
-    dims = ((1,), (1,))
-    one = dot(jnp.concatenate([gh, gl, zh, zl], axis=0), zh, dims)
-    two = dot(jnp.concatenate([gh, zl], axis=0), zl, dims)
-    y = one[:n] + (one[n : 2 * n] + two[:n])
-    cross = one[2 * n + R :]
-    gram = one[2 * n : 2 * n + R] + (cross + cross.T + two[n:])
-    return y.T, gram
+    out = dot(jnp.concatenate(blocks, axis=0), jnp.concatenate(parts, axis=0), ((1,), (1,)))
+
+    def total(start, length):
+        def block(i, j):
+            top = start + i * length
+            return out[top : top + length, j * R : (j + 1) * R]
+
+        small = block(1, 1) + block(0, 2) + block(2, 0)
+        return block(0, 0) + (block(0, 1) + block(1, 0) + small)
+
+    return total(0, n).T, total(3 * n, R)
 
 
 def call(body, out_shape, n_in, scalars=0, scratch=()):
@@ -186,12 +193,7 @@
 
 
 def first_body(c_ref, g_ref, o_ref, out_ref, keep_ref, send_ref):
-    gh, gl = split(g_ref[...])
-    oh, ol = split(o_ref[...])
-    dims = ((1,), (1,))
-    n = g_ref.shape[0]
-    one = dot(jnp.concatenate([gh, gl], axis=0), oh, dims)
-    y = fold((one[:n] + (one[n:] + dot(gh, ol, dims))).T)
+    y = fold(against(g_ref[...], o_ref[...])[0])
     for i in range(out_ref.shape[0]):
         out_ref[i] = y
     halves(c_ref[0], g_ref, keep_ref, send_ref)
@@ -205,12 +207,11 @@
         part = z[:, t * LANES : (t + 1) * LANES]
         out_ref[2 * t] = part[:H]
         out_ref[2 * t + 1] = part[H:]
-    out_ref[2 * tiles] = fold(nt(yt, yt))
-    for s in range(2 * tiles + 1, out_ref.shape[0]):
+    for s in range(2 * tiles, out_ref.shape[0]):
         out_ref[s] = jnp.zeros((H, LANES), F32)
 
 
-def spread_first_body(c_ref, got_ref, g_ref, h_ref, out_ref):
+def spread_first_body(c_ref, got_ref, g_ref, h_ref, out_ref, gram_ref):
     n = got_ref.shape[0] // 2
     parts = []
     for c in range(2):
@@ -220,16 +221,36 @@
         parts.append(unfold(s))
     yt = jnp.concatenate(parts, axis=1)
     put_slots(yt, (g_ref, h_ref), c_ref[0], out_ref)
-
-
-def spread_body(c_ref, got_ref, g_ref, h_ref, out_ref, yt_ref, rows_ref):
+    gram_ref[...] = fold(nt(yt, yt))
+
+
+def spread_body(c_ref, got_ref, g_ref, h_ref, out_ref, raw_ref):
     s = got_ref[0]
     for i in range(1, got_ref.shape[0]):
         s = s + got_ref[i]
-    factor(unfold(s[R:]), rows_ref)
-    yt = nn(inverse_of(rows_ref), s[:R])
-    yt_ref[...] = yt
-    put_slots(yt, (g_ref, h_ref), c_ref[0], out_ref)
+    raw_ref[...] = s
+    put_slots(s[:R], (g_ref, h_ref), c_ref[0], out_ref)
+
+
+def factor_body(gram_ref, inv_ref, rows_ref):
+    factor(unfold(gram_ref[...]), rows_ref)
+    inv_ref[...] = inverse_of(rows_ref)
+
+
+def normal_body(raw_ref, inv_ref, gram_ref, rows_ref):
+    factor(unfold(raw_ref[R:]), rows_ref)
+    inv = inverse_of(rows_ref)
+    inv_ref[...] = inv
+    yt = nn(inv, raw_ref[:R])
+    gram_ref[...] = fold(nt(yt, yt))
+
+
+def left_body(c_ref, gram_ref, raw_ref, prior_ref, inv_ref, left_ref, rows_ref):
+    factor(unfold(gram_ref[...]), rows_ref)
+    inv = inverse_of(rows_ref)
+    left = nn(inv, nn(prior_ref[...], raw_ref[:R]))
+    left_ref[...] = jnp.where(c_ref[0] == 0, left[:, :R], left[:, R:]).T
+    inv_ref[...] = nn(inv, prior_ref[...])
 
 
 def total_body(got_ref, out_ref):
@@ -264,10 +285,9 @@
     return jnp.where(core == 0, pair, turned)
 
 
-def back_body(c_ref, z_ref, g_ref, h_ref, out_ref, rows_ref):
+def back_body(c_ref, z_ref, g_ref, h_ref, inv_ref, out_ref):
     tiles = g_ref.shape[1] // LANES
-    factor(unfold(z_ref[2 * tiles]), rows_ref)
-    z = product(inverse_of(rows_ref), gathered(z_ref, tiles))
+    z = product(inv_ref[...], gathered(z_ref, tiles))
     y, gram = against(jnp.concatenate([g_ref[...], h_ref[...]], axis=0), z)
     y = in_turn(c_ref[0], y)
     gram = fold(gram)
@@ -276,14 +296,10 @@
         out_ref[i, R:] = gram
 
 
-def last_body(c_ref, z_ref, yt_ref, a_ref, b_ref, o_ref, p_ref, out_ref, inv_ref, left_ref, rows_ref):
+def last_body(c_ref, z_ref, inv_ref, a_ref, b_ref, o_ref, p_ref, out_ref):
     core = c_ref[0]
     tiles = a_ref.shape[1] // LANES
-    factor(unfold(z_ref[2 * tiles, :H]), rows_ref)
-    inv = inverse_of(rows_ref)
-    inv_ref[...] = inv
-    left = nn(inv, yt_ref[...])
-    left_ref[...] = jnp.where(core == 0, left[:, :R], left[:, R:]).T
+    inv = inv_ref[...]
     z = product(inv, gathered(z_ref, tiles))
     rights, gram = against(jnp.concatenate([a_ref[...], b_ref[...]], axis=0), z)
     near = o_ref.shape[1] // LANES
@@ -330,6 +346,13 @@
     return lax.all_to_all(a, axes, split_axis=0, concat_axis=0, tiled=True)
 
 
+def summed(part, rounds):
+    for axis, bit in rounds:
+        pairs = [(i, i ^ bit) for i in range(lax.axis_size(axis))]
+        part = part + lax.ppermute(part, axis, pairs)
+    return part
+
+
 def per_device(gradient, start_block, activations, out_grads):
     far, near = lax.axis_size("y"), lax.axis_size("z")
     cols = lax.axis_size("x")
@@ -340,6 +363,8 @@
     width = -(-n // (2 * LANES)) * LANES
     piece = R // peers
 
+    rounds = [(axis, 1 << k) for axis in CHIPS for k in range(lax.axis_size(axis).bit_length() - 1)]
+    early, late = rounds[: len(rounds) // 2], rounds[len(rounds) // 2 :]
     lines = gradient.shape[0]
     first, g, send = call(
         first_body, (shape(peers, H, LANES), shape(lines, width), shape(lines, width)), 3, scalars=1
@@ -348,28 +373,26 @@
     got = exchanged(first, PEERS)
     a, b = swapped(core, activations, width)
     o, p = swapped(core, out_grads, out_grads.shape[1] // 2)
-    square = pltpu.VMEM((R, LANES), F32)
-
-    parts = call(spread_first_body, shape(slots, H, LANES), 4, scalars=1)(core, got, g, h)
-    for step in range(ITERS):
-        arrived = exchanged(parts, CHIPS)
-        if step < ITERS - 1:
-            arrived, a, b, o, p = lax.optimization_barrier((arrived, a, b, o, p))
-            sums = call(total_body, shape(slots, H, LANES), 1)(arrived)
-            z = exchanged(sums, CHIPS)
-            partial = call(
-                back_body, shape(peers, R + H, LANES), 4, scalars=1, scratch=[square]
-            )(core, z, g, h)
-            got = exchanged(partial, PEERS)
-            parts, yt = call(
-                spread_body,
-                (shape(slots, H, LANES), shape(R, LANES)),
-                4,
-                scalars=1,
-                scratch=[square],
-            )(core, got, g, h)
+    square = [pltpu.VMEM((R, LANES), F32)]
+    block, whole = shape(slots, H, LANES), shape(peers, R + H, LANES)
+    half, small = shape(H, LANES), shape(R, R)
+
+    parts, gram = call(spread_first_body, (block, half), 4, scalars=1)(core, got, g, h)
+    arrived = exchanged(parts, CHIPS)
+    gram = summed(gram, early)
+    arrived, gram, a, b, o, p = lax.optimization_barrier((arrived, gram, a, b, o, p))
+    z = exchanged(call(total_body, block, 1)(arrived), CHIPS)
+    inv = call(factor_body, small, 1, scratch=square)(summed(gram, late))
+    partial = call(back_body, whole, 5, scalars=1)(core, z, g, h, inv)
+
+    got = exchanged(partial, PEERS)
+    raw_shape = shape(R + H, LANES)
+    parts, raw = call(spread_body, (block, raw_shape), 4, scalars=1)(core, got, g, h)
+    arrived = exchanged(parts, CHIPS)
+    prior, gram = call(normal_body, (small, half), 1, scratch=square)(raw)
+    gram = summed(gram, early)
     eighth = lax.axis_index("x") * 2 + core_at
-    mine = lax.dynamic_slice_in_dim(yt, eighth * piece, piece, 0)
+    mine = lax.dynamic_slice_in_dim(raw, eighth * piece, piece, 0)
     moves = []
     for ys in range(far):
         for cs in range(2):
@@ -378,19 +401,19 @@
                 target = ((2 * xs + cs) * 2 + ys % 2) * cols + ys // 2
                 moves.append((source, target))
     lines = lax.ppermute(mine, ("y", "c", "x"), moves)
-    sums = call(total_with_body, shape(slots, H + piece, LANES), 2)(arrived, lines)
-    z = exchanged(sums, CHIPS)
+    arrived, gram, lines = lax.optimization_barrier((arrived, gram, lines))
+    z = exchanged(
+        call(total_with_body, shape(slots, H + piece, LANES), 2)(arrived, lines), CHIPS
+    )
+    inv, left = call(left_body, (small, small), 4, scalars=1, scratch=square)(
+        core, summed(gram, late), raw, prior
+    )
+    z, inv, left = lax.optimization_barrier((z, inv, left))
     w = other_core(z[:, :H])
-    partial, inv, left = call(
-        last_body,
-        (shape(peers, R + H, LANES), shape(R, R), shape(R, R)),
-        7,
-        scalars=1,
-        scratch=[square],
-    )(core, z, yt, a, b, o, p)
+    partial = call(last_body, whole, 7, scalars=1)(core, z, inv, a, b, o, p)
     got = exchanged(partial, PEERS)
     right, scores = call(
-        finish_body, (shape(R, n), shape(1, R)), 5, scalars=1, scratch=[square]
+        finish_body, (shape(R, n), shape(1, R)), 5, scalars=1, scratch=square
     )(core, got, inv, z, w)
     return (left, right.T, scores.reshape(-1))
 

time: 224 us -> 289 us (1.29)
  starting transfers between devices: 41.7 us -> 125 us
  blocking collectives: 110 us -> 42 us
  waiting for transfers between devices: 41.2 us -> 82.5 us
  local copies, waits for them, and re-layouts: 7.29 us -> 11.4 us
  Pallas kernels: 21.9 us -> 26 us
    ppermute x0 -> x12, waiting for transfers between devices: none -> 81.2 us  [summed(): part = part + lax.ppermute(part, axis, pairs)]
    all_to_all x5 -> x3, blocking collectives: 110 us -> 42 us  [exchanged(): return lax.all_to_all(a, axes, split_axis=0, concat_axis=0, tiled=True)]
    ppermute x0 -> x12, starting transfers between devices: none -> 39.8 us  [summed(): part = part + lax.ppermute(part, axis, pairs)]
    all_to_all x2 -> x4, starting transfers between devices: 18.9 us -> 47.4 us  [exchanged(): return lax.all_to_all(a, axes, split_axis=0, concat_axis=0, tiled=True)]
    ppermute x1, waiting for transfers between devices: 20.9 us -> 1.28 us  [per_device(): lines = lax.ppermute(mine, ('y', 'c', 'x'), moves)]
    all_to_all x2 -> x4, waiting for transfers between devices: 18.8 us -> 0.01 us  [exchanged(): return lax.all_to_all(a, axes, split_axis=0, concat_axis=0, tiled=True)]
    ppermute x4, starting transfers between devices: 19.1 us -> 32 us  [other_core(): return lax.ppermute(a, 'c', [(0, 1), (1, 0)])]
    unnamed x20 -> x32, local copies, waits for them, and re-layouts: 7.16 us -> 11.2 us
  transfers between devices with their start and end apart: 7 -> 21, of which waited for: 4 -> 12; matrix products, arithmetic and copies ran while one was open for 0% -> 0% of each run, Pallas kernels for 2% -> 4%
where the time goes in v3:
time: 289 us; the launch traced here: 288 us
  starting transfers between devices  125 us (43%)
  waiting for transfers between devices  82.5 us (29%)
  blocking collectives  42 us (15%)
  Pallas kernels  26 us (9%)
  local copies, waits for them, and re-layouts  11.4 us (4%)
    ppermute x12, waiting for transfers between devices, summed(): part = part + lax.ppermute(part, axis, pairs)  81.2 us
    all_to_all x4, starting transfers between devices, exchanged(): return lax.all_to_all(a, axes, split_axis=0, concat_axis=0, tiled=True)  47.4 us
    all_to_all x3, blocking collectives, exchanged(): return lax.all_to_all(a, axes, split_axis=0, concat_axis=0, tiled=True)  42 us
    ppermute x12, starting transfers between devices, summed(): part = part + lax.ppermute(part, axis, pairs)  39.8 us
    ppermute x4, starting transfers between devices, other_core(): return lax.ppermute(a, 'c', [(0, 1), (1, 0)])  32 us
    unnamed x32, local copies, waits for them, and re-layouts  11.2 us
    ppermute x1, starting transfers between devices, per_device(): lines = lax.ppermute(mine, ('y', 'c', 'x'), moves)  6.02 us
  transfers between devices with their start and end apart: 21, of which 12 were waited for; matrix products, arithmetic and copies ran while one was open for 0% of the time, Pallas kernels for 4%

profile of v3, /device:TPU:1, one launch (start us, length us, event | category | flops | bytes accessed | tf_op | source)
XLA Modules:
  0.0 288.2 jit_solution(9154160109359679933)
XLA Ops:
  0.6 1.5 copy-done.1
  2.2 1.5 copy-done.2
  3.7 2.0 shard_map.67
  5.7 8.7 %collective-permute-start = (f32[64,3712]{1,0:T(8,128)S(1)}, f32[64,3712]{1,0:T(8,128)S(1)}, u32[]{:S(2)}, u32[]{:S(2)}) collective-permute-start(f32[64,3712]{1,0:T(8,128)S(1)} %get-tuple-element.34), channel_id=1, source_target_pairs={{0,4},{4,0},{1,5},{5,1},{2,6},{6,2},{3,7},{7,3},{8,12},{12,8},{9,1... | collective-permute-start | bytes 2850824 | tf_op jit(solution)/shard_map/ppermute | solution.py:192
  14.4 7.5 %all_to_all.35.got_ref = f32[8,32,128]{2,1,0:T(8,128)S(1)} all-to-all(f32[8,32,128]{2,1,0:T(8,128)S(1)} %get-tuple-element.32), channel_id=1, replica_groups=mesh['y'=8,'z'=8,'c'=2,'x'=4] {'c','x'}, dimensions={0} | all-to-all | bytes 262144 | tf_op jit(solution)/shard_map/all_to_all | solution.py:346
  22.0 1.2 shard_map.68
  23.2 1.0 copy-done.4
  24.1 12.9 %all-to-all-start.1 = ((f32[64,32,128]{2,1,0:T(8,128)}), f32[64,32,128]{2,1,0:T(8,128)S(1)}, u32[]{:S(2)}, u32[]{:S(2)}) async-start(f32[64,32,128]{2,1,0:T(8,128)} %copy-done.4), calls=%async_computation.1 | async-start | bytes 2097152 | tf_op jit(solution)/shard_map/all_to_all | solution.py:346
  37.0 0.0 copy-start.3
  37.1 1.5 copy-done.3
  38.6 0.1 shard_map.69
  38.7 1.0 copy-done.5
  39.7 2.6 collective-permute-start.4
  42.3 0.7 copy-done.10
  43.0 1.9 collective-permute-start.5
  44.9 3.2 %collective-permute-start.1 = (f32[32,128]{1,0:T(8,128)S(1)}, f32[32,128]{1,0:T(8,128)S(1)}, u32[]{:S(2)}, u32[]{:S(2)}) collective-permute-start(f32[32,128]{1,0:T(8,128)S(1)} %get-tuple-element.36), channel_id=1, source_target_pairs={{0,64},{64,0},{128,192},{192,128},{256,320},{320,256},{384,448},{4... | collective-permute-start | bytes 49160 | tf_op jit(solution)/shard_map/ppermute | solution.py:352
  48.1 12.5 %collective-permute-done.1 = f32[32,128]{1,0:T(8,128)S(1)} collective-permute-done((f32[32,128]{1,0:T(8,128)S(1)}, f32[32,128]{1,0:T(8,128)S(1)}, u32[]{:S(2)}, u32[]{:S(2)}) %collective-permute-start.1) | collective-permute-done | bytes 16416 | tf_op jit(solution)/shard_map/ppermute | solution.py:352
  60.6 2.8 collective-permute-start.2
  63.4 2.9 %collective-permute-done.2 = f32[32,128]{1,0:T(8,128)S(1)} collective-permute-done((f32[32,128]{1,0:T(8,128)S(1)}, f32[32,128]{1,0:T(8,128)S(1)}, u32[]{:S(2)}, u32[]{:S(2)}) %collective-permute-start.2) | collective-permute-done | bytes 16416 | tf_op jit(solution)/shard_map/ppermute | solution.py:352
  66.3 6.7 %collective-permute-start.3 = (f32[32,128]{1,0:T(8,128)S(1)}, f32[32,128]{1,0:T(8,128)S(1)}, u32[]{:S(2)}, u32[]{:S(2)}) collective-permute-start(f32[32,128]{1,0:T(8,128)S(1)} %add.43), channel_id=1, source_target_pairs={{0,256},{64,320},{128,384},{192,448},{256,0},{320,64},{384,128},{4... | collective-permute-start | bytes 49160 | tf_op jit(solution)/shard_map/ppermute | solution.py:352
  73.0 1.7 collective-permute-done.3
  74.7 0.0 collective-permute-done.5.p_ref
  74.7 0.7 copy-done.12
  75.4 0.9 copy-done.7
  76.3 0.0 all-to-all-done.1.got_ref
  76.3 0.2 shard_map.71
  76.5 0.0 copy-start
  76.5 1.0 copy-done
  77.5 11.7 %all-to-all-start.2 = ((f32[64,32,128]{2,1,0:T(8,128)}), f32[64,32,128]{2,1,0:T(8,128)S(1)}, u32[]{:S(2)}, u32[]{:S(2)}) async-start(f32[64,32,128]{2,1,0:T(8,128)} %copy-done), calls=%async_computation.2 | async-start | bytes 2097152 | tf_op jit(solution)/shard_map/all_to_all | solution.py:346
  89.2 2.9 %collective-permute-start.6 = (f32[32,128]{1,0:T(8,128)S(1)}, f32[32,128]{1,0:T(8,128)S(1)}, u32[]{:S(2)}, u32[]{:S(2)}) collective-permute-start(f32[32,128]{1,0:T(8,128)S(1)} %add.44), channel_id=1, source_target_pairs={{0,8},{8,0},{16,24},{24,16},{32,40},{40,32},{48,56},{56,48},{1,9},... | collective-permute-start | bytes 49160 | tf_op jit(solution)/shard_map/ppermute | solution.py:352
  92.2 3.9 %collective-permute-done.6 = f32[32,128]{1,0:T(8,128)S(1)} collective-permute-done((f32[32,128]{1,0:T(8,128)S(1)}, f32[32,128]{1,0:T(8,128)S(1)}, u32[]{:S(2)}, u32[]{:S(2)}) %collective-permute-start.6) | collective-permute-done | bytes 16416 | tf_op jit(solution)/shard_map/ppermute | solution.py:352
  96.1 3.1 %collective-permute-start.7 = (f32[32,128]{1,0:T(8,128)S(1)}, f32[32,128]{1,0:T(8,128)S(1)}, u32[]{:S(2)}, u32[]{:S(2)}) collective-permute-start(f32[32,128]{1,0:T(8,128)S(1)} %add.45), channel_id=1, source_target_pairs={{0,16},{8,24},{16,0},{24,8},{32,48},{40,56},{48,32},{56,40},{1,17}... | collective-permute-start | bytes 49160 | tf_op jit(solution)/shard_map/ppermute | solution.py:352
  99.2 9.2 %collective-permute-done.7 = f32[32,128]{1,0:T(8,128)S(1)} collective-permute-done((f32[32,128]{1,0:T(8,128)S(1)}, f32[32,128]{1,0:T(8,128)S(1)}, u32[]{:S(2)}, u32[]{:S(2)}) %collective-permute-start.7) | collective-permute-done | bytes 16416 | tf_op jit(solution)/shard_map/ppermute | solution.py:352
  108.4 1.9 collective-permute-start.8
  110.3 7.6 %collective-permute-done.8 = f32[32,128]{1,0:T(8,128)S(1)} collective-permute-done((f32[32,128]{1,0:T(8,128)S(1)}, f32[32,128]{1,0:T(8,128)S(1)}, u32[]{:S(2)}, u32[]{:S(2)}) %collective-permute-start.8) | collective-permute-done | bytes 16416 | tf_op jit(solution)/shard_map/ppermute | solution.py:352
  118.0 2.4 shard_map.72.inv_ref
  120.3 2.4 shard_map.73
  122.8 24.1 %all_to_all.36.got_ref = f32[8,96,128]{2,1,0:T(8,128)S(1)} all-to-all(f32[8,96,128]{2,1,0:T(8,128)S(1)} %shard_map.73), channel_id=1, replica_groups=mesh['y'=8,'z'=8,'c'=2,'x'=4] {'c','x'}, dimensions={0} | all-to-all | bytes 786432 | tf_op jit(solution)/shard_map/all_to_all | solution.py:346
  146.9 1.9 shard_map.74
  148.8 10.7 %all-to-all-start.4 = ((f32[64,32,128]{2,1,0:T(8,128)}), f32[64,32,128]{2,1,0:T(8,128)S(1)}, u32[]{:S(2)}, u32[]{:S(2)}) async-start(f32[64,32,128]{2,1,0:T(8,128)} %get-tuple-element.43), calls=%async_computation.4 | async-start | bytes 2097152 | tf_op jit(solution)/shard_map/all_to_all | solution.py:346
  159.6 2.8 shard_map.75
  162.3 0.7 copy-done.14
  163.0 2.7 collective-permute-start.9
  165.7 17.2 %collective-permute-done.9 = f32[32,128]{1,0:T(8,128)S(1)} collective-permute-done((f32[32,128]{1,0:T(8,128)S(1)}, f32[32,128]{1,0:T(8,128)S(1)}, u32[]{:S(2)}, u32[]{:S(2)}) %collective-permute-start.9) | collective-permute-done | bytes 16416 | tf_op jit(solution)/shard_map/ppermute | solution.py:352
  182.9 2.8 collective-permute-start.10
  185.7 2.9 %collective-permute-done.10 = f32[32,128]{1,0:T(8,128)S(1)} collective-permute-done((f32[32,128]{1,0:T(8,128)S(1)}, f32[32,128]{1,0:T(8,128)S(1)}, u32[]{:S(2)}, u32[]{:S(2)}) %collective-permute-start.10) | collective-permute-done | bytes 16416 | tf_op jit(solution)/shard_map/ppermute | solution.py:352
  188.6 6.0 %collective-permute-start.11 = (f32[32,128]{1,0:T(8,128)S(1)}, f32[32,128]{1,0:T(8,128)S(1)}, u32[]{:S(2)}, u32[]{:S(2)}) collective-permute-start(f32[32,128]{1,0:T(8,128)S(1)} %add.49), channel_id=1, source_target_pairs={{0,256},{64,320},{128,384},{192,448},{256,0},{320,64},{384,128},{4... | collective-permute-start | bytes 49160 | tf_op jit(solution)/shard_map/ppermute | solution.py:352
  194.6 6.0 %collective-permute-start.12 = (f32[8,128]{1,0:T(8,128)S(1)}, f32[8,128]{1,0:T(8,128)S(1)}, u32[]{:S(2)}, u32[]{:S(2)}) collective-permute-start(f32[8,128]{1,0:T(8,128)S(1)} %constant_dynamic-slice_fusion), channel_id=1, source_target_pairs={{0,0},{1,128},{2,256},{3,384},{4,64},{5,192},{6,320},{7,448},{64,4... | collective-permute-start | bytes 12296 | tf_op jit(solution)/shard_map/ppermute | solution.py:403
  200.7 1.3 collective-permute-done.12.more_ref
  202.0 1.2 shard_map.76
  203.2 12.1 %all-to-all-start.5 = ((f32[64,40,128]{2,1,0:T(8,128)}), f32[64,40,128]{2,1,0:T(8,128)S(1)}, u32[]{:S(2)}, u32[]{:S(2)}) async-start(f32[64,40,128]{2,1,0:T(8,128)} %shard_map.76), calls=%async_computation.5 | async-start | bytes 2621440 | tf_op jit(solution)/shard_map/all_to_all | solution.py:346
  215.2 2.9 %collective-permute-start.13 = (f32[32,128]{1,0:T(8,128)S(1)}, f32[32,128]{1,0:T(8,128)S(1)}, u32[]{:S(2)}, u32[]{:S(2)}) collective-permute-start(f32[32,128]{1,0:T(8,128)S(1)} %add.50), channel_id=1, source_target_pairs={{0,8},{8,0},{16,24},{24,16},{32,40},{40,32},{48,56},{56,48},{1,9},... | collective-permute-start | bytes 49160 | tf_op jit(solution)/shard_map/ppermute | solution.py:352
  218.2 5.7 %collective-permute-done.13 = f32[32,128]{1,0:T(8,128)S(1)} collective-permute-done((f32[32,128]{1,0:T(8,128)S(1)}, f32[32,128]{1,0:T(8,128)S(1)}, u32[]{:S(2)}, u32[]{:S(2)}) %collective-permute-start.13) | collective-permute-done | bytes 16416 | tf_op jit(solution)/shard_map/ppermute | solution.py:352
  223.9 2.8 collective-permute-start.14
  226.6 10.1 %collective-permute-done.14 = f32[32,128]{1,0:T(8,128)S(1)} collective-permute-done((f32[32,128]{1,0:T(8,128)S(1)}, f32[32,128]{1,0:T(8,128)S(1)}, u32[]{:S(2)}, u32[]{:S(2)}) %collective-permute-start.14) | collective-permute-done | bytes 16416 | tf_op jit(solution)/shard_map/ppermute | solution.py:352
  236.8 1.9 collective-permute-start.15
  238.7 7.6 %collective-permute-done.15 = f32[32,128]{1,0:T(8,128)S(1)} collective-permute-done((f32[32,128]{1,0:T(8,128)S(1)}, f32[32,128]{1,0:T(8,128)S(1)}, u32[]{:S(2)}, u32[]{:S(2)}) %collective-permute-start.15) | collective-permute-done | bytes 16416 | tf_op jit(solution)/shard_map/ppermute | solution.py:352
  246.3 0.8 copy-done.15
  247.0 3.3 %shard_map.77 = (f32[64,64]{1,0:T(8,128)S(1)}, f32[64,64]{1,0:T(8,128)}) custom-call(s32[1]{0:T(128)} %bitcast.c_ref, f32[32,128]{1,0:T(8,128)S(1)} %add.55.gram_ref, f32[96,128]{1,0:T(8,128)S(1)} %get-tuple-element.44.raw_ref, f32[64,64]{1,0:T(8,128)S(1)} %copy-done.15), custom_call_target="tpu_custom_call" | custom-call | tf_op jit(solution)/shard_map/pallas_call | solution.py:408
  250.4 0.1 slice.3
  250.5 18.8 %collective-permute-start.16 = (f32[64,32,128]{2,1,0:T(8,128)S(1)}, f32[64,32,128]{2,1,0:T(8,128)S(1)}, u32[]{:S(2)}, u32[]{:S(2)}) collective-permute-start(f32[64,32,128]{2,1,0:T(8,128)S(1)} %slice.3), channel_id=1, source_target_pairs={{0,4},{4,0},{1,5},{5,1},{2,6},{6,2},{3,7},{7,3},{8,12},{12,8},{9,1... | collective-permute-start | bytes 3145736 | tf_op jit(solution)/shard_map/ppermute | solution.py:192
  269.4 3.0 %shard_map.78 = f32[8,96,128]{2,1,0:T(8,128)S(1)} custom-call(s32[1]{0:T(128)} %bitcast.c_ref, f32[64,40,128]{2,1,0:T(8,128)S(1)} %all-to-all-done.5.z_ref, f32[64,64]{1,0:T(8,128)S(1)} %get-tuple-element.54.inv_ref, f32[64,3712]{1,0:T(8,128)S(1)} %copy-done.6, f32[64,3712]{1,0:T(8,128)S(1)} %copy-done.8, f32[64,1024]{1,0:T(8,128)S(1)} %copy-done.11, ...), custom_call_target="tpu_custom_call" | custom-call | tf_op jit(solution)/shard_map/pallas_call | solution.py:413
  272.4 10.4 %all_to_all.37.got_ref = f32[8,96,128]{2,1,0:T(8,128)S(1)} all-to-all(f32[8,96,128]{2,1,0:T(8,128)S(1)} %shard_map.78), channel_id=1, replica_groups=mesh['y'=8,'z'=8,'c'=2,'x'=4] {'c','x'}, dimensions={0} | all-to-all | bytes 786432 | tf_op jit(solution)/shard_map/all_to_all | solution.py:346
  282.8 5.5 %shard_map.79 = (f32[64,7392]{1,0:T(8,128)}, f32[1,64]{1,0:T(1,128)}) custom-call(s32[1]{0:T(128)} %bitcast.c_ref, f32[8,96,128]{2,1,0:T(8,128)S(1)} %all_to_all.37.got_ref, f32[64,64]{1,0:T(8,128)S(1)} %get-tuple-element.54.inv_ref, f32[64,40,128]{2,1,0:T(8,128)S(1)} %all-to-all-done.5.z_ref, f32[64,32,128]{2,1,0:T(8,128)S(1)} %collective-permute-done.16.w_ref), custom_call_target="tpu_custom_call" | custom-call | tf_op jit(solution)/shard_map/pallas_call | solution.py:415
  (40 shorter events, 0.2 us)
Async XLA Ops:
  0.6 1.5 copy-start.1
  2.2 1.5 copy-start.2
  5.7 16.3 %collective-permute-start = (f32[64,3712]{1,0:T(8,128)S(1)}, f32[64,3712]{1,0:T(8,128)S(1)}, u32[]{:S(2)}, u32[]{:S(2)}) collective-permute-start(f32[64,3712]{1,0:T(8,128)S(1)} %get-tuple-element.34), channel_id=1, source_target_pairs={{0,4},{4,0},{1,5},{5,1},{2,6},{6,2},{3,7},{7,3},{8,12},{12,8},{9,1... | collective-permute-start | bytes 2850824 | tf_op jit(solution)/shard_map/ppermute | solution.py:192
  23.2 1.0 copy-start.4
  24.1 18.1 %copy-start.9 = (f32[64,2048]{1,0:T(8,128)S(1)}, f32[64,2048]{1,0:T(8,128)}, u32[]{:S(2)}) copy-start(f32[64,2048]{1,0:T(8,128)} %a_ref.3) | copy-start | bytes 1572868
  24.1 52.2 %all-to-all-start.1 = ((f32[64,32,128]{2,1,0:T(8,128)}), f32[64,32,128]{2,1,0:T(8,128)S(1)}, u32[]{:S(2)}, u32[]{:S(2)}) async-start(f32[64,32,128]{2,1,0:T(8,128)} %copy-done.4), calls=%async_computation.1 | async-start | bytes 2097152 | tf_op jit(solution)/shard_map/all_to_all | solution.py:346
  37.0 1.5 copy-start.3
  38.7 1.0 copy-start.5
  39.7 35.7 %collective-permute-start.4 = (f32[64,3712]{1,0:T(8,128)S(1)}, f32[64,3712]{1,0:T(8,128)S(1)}, u32[]{:S(2)}, u32[]{:S(2)}) collective-permute-start(f32[64,3712]{1,0:T(8,128)S(1)} %get-tuple-element.38), channel_id=1, source_target_pairs={{0,4},{4,0},{1,5},{5,1},{2,6},{6,2},{3,7},{7,3},{8,12},{12,8},{9,1... | collective-permute-start | bytes 2850824 | tf_op jit(solution)/shard_map/ppermute | solution.py:192
  42.3 0.7 copy-start.10
  43.0 31.6 %collective-permute-start.5 = (f32[64,1024]{1,0:T(8,128)S(1)}, f32[64,1024]{1,0:T(8,128)S(1)}, u32[]{:S(2)}, u32[]{:S(2)}) collective-permute-start(f32[64,1024]{1,0:T(8,128)S(1)} %get-tuple-element.40), channel_id=1, source_target_pairs={{0,4},{4,0},{1,5},{5,1},{2,6},{6,2},{3,7},{7,3},{8,12},{12,8},{9,1... | collective-permute-start | bytes 786440 | tf_op jit(solution)/shard_map/ppermute | solution.py:192
  44.9 15.7 %collective-permute-start.1 = (f32[32,128]{1,0:T(8,128)S(1)}, f32[32,128]{1,0:T(8,128)S(1)}, u32[]{:S(2)}, u32[]{:S(2)}) collective-permute-start(f32[32,128]{1,0:T(8,128)S(1)} %get-tuple-element.36), channel_id=1, source_target_pairs={{0,64},{64,0},{128,192},{192,128},{256,320},{320,256},{384,448},{4... | collective-permute-start | bytes 49160 | tf_op jit(solution)/shard_map/ppermute | solution.py:352
  60.6 5.7 %collective-permute-start.2 = (f32[32,128]{1,0:T(8,128)S(1)}, f32[32,128]{1,0:T(8,128)S(1)}, u32[]{:S(2)}, u32[]{:S(2)}) collective-permute-start(f32[32,128]{1,0:T(8,128)S(1)} %add.42), channel_id=1, source_target_pairs={{0,128},{64,192},{128,0},{192,64},{256,384},{320,448},{384,256},{4... | collective-permute-start | bytes 49160 | tf_op jit(solution)/shard_map/ppermute | solution.py:352
  66.3 8.4 %collective-permute-start.3 = (f32[32,128]{1,0:T(8,128)S(1)}, f32[32,128]{1,0:T(8,128)S(1)}, u32[]{:S(2)}, u32[]{:S(2)}) collective-permute-start(f32[32,128]{1,0:T(8,128)S(1)} %add.43), channel_id=1, source_target_pairs={{0,256},{64,320},{128,384},{192,448},{256,0},{320,64},{384,128},{4... | collective-permute-start | bytes 49160 | tf_op jit(solution)/shard_map/ppermute | solution.py:352
  74.7 0.7 copy-start.12
  75.4 0.9 copy-start.7
  76.5 1.0 copy-start
  77.5 42.8 %all-to-all-start.2 = ((f32[64,32,128]{2,1,0:T(8,128)}), f32[64,32,128]{2,1,0:T(8,128)S(1)}, u32[]{:S(2)}, u32[]{:S(2)}) async-start(f32[64,32,128]{2,1,0:T(8,128)} %copy-done), calls=%async_computation.2 | async-start | bytes 2097152 | tf_op jit(solution)/shard_map/all_to_all | solution.py:346
  89.2 6.8 %collective-permute-start.6 = (f32[32,128]{1,0:T(8,128)S(1)}, f32[32,128]{1,0:T(8,128)S(1)}, u32[]{:S(2)}, u32[]{:S(2)}) collective-permute-start(f32[32,128]{1,0:T(8,128)S(1)} %add.44), channel_id=1, source_target_pairs={{0,8},{8,0},{16,24},{24,16},{32,40},{40,32},{48,56},{56,48},{1,9},... | collective-permute-start | bytes 49160 | tf_op jit(solution)/shard_map/ppermute | solution.py:352
  96.1 12.3 %collective-permute-start.7 = (f32[32,128]{1,0:T(8,128)S(1)}, f32[32,128]{1,0:T(8,128)S(1)}, u32[]{:S(2)}, u32[]{:S(2)}) collective-permute-start(f32[32,128]{1,0:T(8,128)S(1)} %add.45), channel_id=1, source_target_pairs={{0,16},{8,24},{16,0},{24,8},{32,48},{40,56},{48,32},{56,40},{1,17}... | collective-permute-start | bytes 49160 | tf_op jit(solution)/shard_map/ppermute | solution.py:352
  108.4 9.5 %collective-permute-start.8 = (f32[32,128]{1,0:T(8,128)S(1)}, f32[32,128]{1,0:T(8,128)S(1)}, u32[]{:S(2)}, u32[]{:S(2)}) collective-permute-start(f32[32,128]{1,0:T(8,128)S(1)} %add.46), channel_id=1, source_target_pairs={{0,32},{8,40},{16,48},{24,56},{32,0},{40,8},{48,16},{56,24},{1,33}... | collective-permute-start | bytes 49160 | tf_op jit(solution)/shard_map/ppermute | solution.py:352
  148.8 53.1 %all-to-all-start.4 = ((f32[64,32,128]{2,1,0:T(8,128)}), f32[64,32,128]{2,1,0:T(8,128)S(1)}, u32[]{:S(2)}, u32[]{:S(2)}) async-start(f32[64,32,128]{2,1,0:T(8,128)} %get-tuple-element.43), calls=%async_computation.4 | async-start | bytes 2097152 | tf_op jit(solution)/shard_map/all_to_all | solution.py:346
  162.3 0.7 copy-start.14
  163.0 19.9 %collective-permute-start.9 = (f32[32,128]{1,0:T(8,128)S(1)}, f32[32,128]{1,0:T(8,128)S(1)}, u32[]{:S(2)}, u32[]{:S(2)}) collective-permute-start(f32[32,128]{1,0:T(8,128)S(1)} %get-tuple-element.45), channel_id=1, source_target_pairs={{0,64},{64,0},{128,192},{192,128},{256,320},{320,256},{384,448},{4... | collective-permute-start | bytes 49160 | tf_op jit(solution)/shard_map/ppermute | solution.py:352
  182.9 5.7 %collective-permute-start.10 = (f32[32,128]{1,0:T(8,128)S(1)}, f32[32,128]{1,0:T(8,128)S(1)}, u32[]{:S(2)}, u32[]{:S(2)}) collective-permute-start(f32[32,128]{1,0:T(8,128)S(1)} %add.48), channel_id=1, source_target_pairs={{0,128},{64,192},{128,0},{192,64},{256,384},{320,448},{384,256},{4... | collective-permute-start | bytes 49160 | tf_op jit(solution)/shard_map/ppermute | solution.py:352
  188.6 12.0 %collective-permute-start.11 = (f32[32,128]{1,0:T(8,128)S(1)}, f32[32,128]{1,0:T(8,128)S(1)}, u32[]{:S(2)}, u32[]{:S(2)}) collective-permute-start(f32[32,128]{1,0:T(8,128)S(1)} %add.49), channel_id=1, source_target_pairs={{0,256},{64,320},{128,384},{192,448},{256,0},{320,64},{384,128},{4... | collective-permute-start | bytes 49160 | tf_op jit(solution)/shard_map/ppermute | solution.py:352
  194.6 7.3 %collective-permute-start.12 = (f32[8,128]{1,0:T(8,128)S(1)}, f32[8,128]{1,0:T(8,128)S(1)}, u32[]{:S(2)}, u32[]{:S(2)}) collective-permute-start(f32[8,128]{1,0:T(8,128)S(1)} %constant_dynamic-slice_fusion), channel_id=1, source_target_pairs={{0,0},{1,128},{2,256},{3,384},{4,64},{5,192},{6,320},{7,448},{64,4... | collective-permute-start | bytes 12296 | tf_op jit(solution)/shard_map/ppermute | solution.py:403
  203.2 66.2 %copy-start.6 = (f32[64,3712]{1,0:T(8,128)S(1)}, f32[64,3712]{1,0:T(8,128)}, u32[]{:S(2)}) copy-start(f32[64,3712]{1,0:T(8,128)} %copy-done.5) | copy-start | bytes 2850820
  203.2 66.2 %copy-start.8 = (f32[64,3712]{1,0:T(8,128)S(1)}, f32[64,3712]{1,0:T(8,128)}, u32[]{:S(2)}) copy-start(f32[64,3712]{1,0:T(8,128)} %copy-done.7) | copy-start | bytes 2850820
  203.2 66.2 %copy-start.11 = (f32[64,1024]{1,0:T(8,128)S(1)}, f32[64,1024]{1,0:T(8,128)}, u32[]{:S(2)}) copy-start(f32[64,1024]{1,0:T(8,128)} %copy-done.10) | copy-start | bytes 786436
  203.2 47.2 %all-to-all-start.5 = ((f32[64,40,128]{2,1,0:T(8,128)}), f32[64,40,128]{2,1,0:T(8,128)S(1)}, u32[]{:S(2)}, u32[]{:S(2)}) async-start(f32[64,40,128]{2,1,0:T(8,128)} %shard_map.76), calls=%async_computation.5 | async-start | bytes 2621440 | tf_op jit(solution)/shard_map/all_to_all | solution.py:346
  215.2 8.6 %collective-permute-start.13 = (f32[32,128]{1,0:T(8,128)S(1)}, f32[32,128]{1,0:T(8,128)S(1)}, u32[]{:S(2)}, u32[]{:S(2)}) collective-permute-start(f32[32,128]{1,0:T(8,128)S(1)} %add.50), channel_id=1, source_target_pairs={{0,8},{8,0},{16,24},{24,16},{32,40},{40,32},{48,56},{56,48},{1,9},... | collective-permute-start | bytes 49160 | tf_op jit(solution)/shard_map/ppermute | solution.py:352
  223.9 12.9 %collective-permute-start.14 = (f32[32,128]{1,0:T(8,128)S(1)}, f32[32,128]{1,0:T(8,128)S(1)}, u32[]{:S(2)}, u32[]{:S(2)}) collective-permute-start(f32[32,128]{1,0:T(8,128)S(1)} %add.53), channel_id=1, source_target_pairs={{0,16},{8,24},{16,0},{24,8},{32,48},{40,56},{48,32},{56,40},{1,17}... | collective-permute-start | bytes 49160 | tf_op jit(solution)/shard_map/ppermute | solution.py:352
  236.8 9.5 %collective-permute-start.15 = (f32[32,128]{1,0:T(8,128)S(1)}, f32[32,128]{1,0:T(8,128)S(1)}, u32[]{:S(2)}, u32[]{:S(2)}) collective-permute-start(f32[32,128]{1,0:T(8,128)S(1)} %add.54), channel_id=1, source_target_pairs={{0,32},{8,40},{16,48},{24,56},{32,0},{40,8},{48,16},{56,24},{1,33}... | collective-permute-start | bytes 49160 | tf_op jit(solution)/shard_map/ppermute | solution.py:352
  246.3 0.8 copy-start.15
  250.4 19.0 %copy-start.13 = (f32[64,1024]{1,0:T(8,128)S(1)}, f32[64,1024]{1,0:T(8,128)}, u32[]{:S(2)}) copy-start(f32[64,1024]{1,0:T(8,128)} %copy-done.12) | copy-start | bytes 786436
  250.5 32.2 %collective-permute-start.16 = (f32[64,32,128]{2,1,0:T(8,128)S(1)}, f32[64,32,128]{2,1,0:T(8,128)S(1)}, u32[]{:S(2)}, u32[]{:S(2)}) collective-permute-start(f32[64,32,128]{2,1,0:T(8,128)S(1)} %slice.3), channel_id=1, source_target_pairs={{0,4},{4,0},{1,5},{5,1},{2,6},{6,2},{3,7},{7,3},{8,12},{12,8},{9,1... | collective-permute-start | bytes 3145736 | tf_op jit(solution)/shard_map/ppermute | solution.py:192

commit v4 on v3

--- a/solution.py
+++ b/solution.py
@@ -1,3 +1,5 @@
+import functools
+
 import jax
 import jax.numpy as jnp
 from jax import lax
@@ -199,19 +201,19 @@
     halves(c_ref[0], g_ref, keep_ref, send_ref)
 
 
-def put_slots(yt, g_refs, core, out_ref):
+def put_lines(yt, gram, g_refs, core, out_ref):
     lines = jnp.concatenate([g_refs[0][...], g_refs[1][...]], axis=0)
     z = product(in_turn(core, yt), lines)
     tiles = z.shape[1] // LANES
     for t in range(tiles):
-        part = z[:, t * LANES : (t + 1) * LANES]
-        out_ref[2 * t] = part[:H]
-        out_ref[2 * t + 1] = part[H:]
-    for s in range(2 * tiles, out_ref.shape[0]):
-        out_ref[s] = jnp.zeros((H, LANES), F32)
-
-
-def spread_first_body(c_ref, got_ref, g_ref, h_ref, out_ref, gram_ref):
+        out_ref[t * R : (t + 1) * R] = z[:, t * LANES : (t + 1) * LANES]
+    out_ref[tiles * R : tiles * R + H] = fold(gram)
+    rest = out_ref.shape[0] - tiles * R - H
+    if rest:
+        out_ref[tiles * R + H :] = jnp.zeros((rest, LANES), F32)
+
+
+def spread_first_body(c_ref, got_ref, g_ref, h_ref, out_ref):
     n = got_ref.shape[0] // 2
     parts = []
     for c in range(2):
@@ -220,64 +222,67 @@
             s = s + got_ref[c * n + i]
         parts.append(unfold(s))
     yt = jnp.concatenate(parts, axis=1)
-    put_slots(yt, (g_ref, h_ref), c_ref[0], out_ref)
-    gram_ref[...] = fold(nt(yt, yt))
-
-
-def spread_body(c_ref, got_ref, g_ref, h_ref, out_ref, raw_ref):
+    put_lines(yt, nt(yt, yt), (g_ref, h_ref), c_ref[0], out_ref)
+
+
+def spread_body(c_ref, got_ref, g_ref, h_ref, out_ref, yt_ref, rows_ref):
+    s = total_of(got_ref)
+    factor(unfold(s[R:]), rows_ref)
+    yt = nn(inverse_of(rows_ref), s[:R])
+    yt_ref[...] = yt
+    put_lines(yt, nt(yt, yt), (g_ref, h_ref), c_ref[0], out_ref)
+
+
+def total_of(got_ref):
     s = got_ref[0]
     for i in range(1, got_ref.shape[0]):
         s = s + got_ref[i]
-    raw_ref[...] = s
-    put_slots(s[:R], (g_ref, h_ref), c_ref[0], out_ref)
-
-
-def factor_body(gram_ref, inv_ref, rows_ref):
-    factor(unfold(gram_ref[...]), rows_ref)
-    inv_ref[...] = inverse_of(rows_ref)
-
-
-def normal_body(raw_ref, inv_ref, gram_ref, rows_ref):
-    factor(unfold(raw_ref[R:]), rows_ref)
-    inv = inverse_of(rows_ref)
-    inv_ref[...] = inv
-    yt = nn(inv, raw_ref[:R])
-    gram_ref[...] = fold(nt(yt, yt))
-
-
-def left_body(c_ref, gram_ref, raw_ref, prior_ref, inv_ref, left_ref, rows_ref):
-    factor(unfold(gram_ref[...]), rows_ref)
-    inv = inverse_of(rows_ref)
-    left = nn(inv, nn(prior_ref[...], raw_ref[:R]))
-    left_ref[...] = jnp.where(c_ref[0] == 0, left[:, :R], left[:, R:]).T
-    inv_ref[...] = nn(inv, prior_ref[...])
+    return s
+
+
+def cut_body(got_ref, out_ref):
+    s = total_of(got_ref)
+    n = out_ref.shape[1]
+    for i in range(out_ref.shape[0]):
+        out_ref[i] = s[i * n : (i + 1) * n]
 
 
 def total_body(got_ref, out_ref):
+    s = total_of(got_ref)
+    for i in range(out_ref.shape[0]):
+        out_ref[i] = s
+
+
+def total_with_body(got_ref, more_ref, out_ref):
+    s = total_of(got_ref)
+    n = s.shape[0]
+    more = more_ref[...]
+    for i in range(out_ref.shape[0]):
+        out_ref[i, :n] = s
+        out_ref[i, n:] = more
+
+
+def joined_body(lines, got_ref, out_ref):
     n = got_ref.shape[0]
-    s = got_ref[0]
-    for i in range(1, n):
-        s = s + got_ref[i]
-    for i in range(n):
+    heads = [got_ref[i, :lines] for i in range(n)]
+    tails = [got_ref[i, lines:] for i in range(n) if got_ref.shape[1] > lines]
+    s = jnp.concatenate(heads + tails, axis=0)
+    for i in range(out_ref.shape[0]):
         out_ref[i] = s
 
 
-def total_with_body(got_ref, more_ref, out_ref):
-    n = got_ref.shape[0]
-    s = got_ref[0]
-    for i in range(1, n):
-        s = s + got_ref[i]
-    more = more_ref[...]
-    for i in range(n):
-        out_ref[i, :H] = s
-        out_ref[i, H:] = more
-
-
-def gathered(z_ref, tiles):
-    parts = [
-        jnp.concatenate([z_ref[2 * t, :H], z_ref[2 * t + 1, :H]], axis=0) for t in range(tiles)
-    ]
-    return jnp.concatenate(parts, axis=1)
+def lines_of(z_ref, start, length, per):
+    parts = []
+    while length:
+        i, at = divmod(start, per)
+        n = min(length, per - at)
+        parts.append(z_ref[i, at : at + n])
+        start, length = start + n, length - n
+    return jnp.concatenate(parts, axis=0) if len(parts) > 1 else parts[0]
+
+
+def gathered(z_ref, tiles, per):
+    return jnp.concatenate([lines_of(z_ref, t * R, R, per) for t in range(tiles)], axis=1)
 
 
 def in_turn(core, pair):
@@ -285,9 +290,11 @@
     return jnp.where(core == 0, pair, turned)
 
 
-def back_body(c_ref, z_ref, g_ref, h_ref, inv_ref, out_ref):
+def back_body(c_ref, z_ref, g_ref, h_ref, out_ref, rows_ref):
     tiles = g_ref.shape[1] // LANES
-    z = product(inv_ref[...], gathered(z_ref, tiles))
+    per = z_ref.shape[1]
+    factor(unfold(lines_of(z_ref, tiles * R, H, per)), rows_ref)
+    z = product(inverse_of(rows_ref), gathered(z_ref, tiles, per))
     y, gram = against(jnp.concatenate([g_ref[...], h_ref[...]], axis=0), z)
     y = in_turn(c_ref[0], y)
     gram = fold(gram)
@@ -296,22 +303,23 @@
         out_ref[i, R:] = gram
 
 
-def last_body(c_ref, z_ref, inv_ref, a_ref, b_ref, o_ref, p_ref, out_ref):
+def last_body(c_ref, z_ref, a_ref, b_ref, o_ref, p_ref, out_ref):
     core = c_ref[0]
     tiles = a_ref.shape[1] // LANES
-    inv = inv_ref[...]
-    z = product(inv, gathered(z_ref, tiles))
+    near = o_ref.shape[1] // LANES
+    far = z_ref.shape[0]
+    piece = R // far
+    per = z_ref.shape[1] - near * piece
+    z = gathered(z_ref, tiles, per)
     rights, gram = against(jnp.concatenate([a_ref[...], b_ref[...]], axis=0), z)
-    near = o_ref.shape[1] // LANES
-    far = z_ref.shape[0] // near
-    feats = jnp.concatenate(
-        [
-            jnp.concatenate([z_ref[e * near + q, H:] for e in range(far)], axis=0)
-            for q in range(near)
-        ],
-        axis=1,
-    )
-    lefts, _ = against(jnp.concatenate([o_ref[...], p_ref[...]], axis=0), nn(inv, feats))
+
+    def feature(i, j):
+        return z_ref[i, per + j * piece : per + (j + 1) * piece]
+
+    by_y = [jnp.concatenate([feature(e, q) for e in range(far)], axis=0) for q in range(near)]
+    by_z = [jnp.concatenate([feature(q, e) for e in range(far)], axis=0) for q in range(near)]
+    feats = jnp.where(core == 0, jnp.concatenate(by_y, axis=1), jnp.concatenate(by_z, axis=1))
+    lefts, _ = against(jnp.concatenate([o_ref[...], p_ref[...]], axis=0), feats)
     gram = fold(gram)
     n = out_ref.shape[0] // 2
     mine = jnp.concatenate([lefts[:, :R], rights[:, :R]], axis=1)
@@ -323,48 +331,59 @@
             out_ref[c * n + i, R:] = gram
 
 
-def finish_body(c_ref, got_ref, inv_ref, z_ref, w_ref, right_ref, scores_ref, rows_ref):
-    s = got_ref[0]
-    for i in range(1, got_ref.shape[0]):
-        s = s + got_ref[i]
-    factor(unfold(s[R:]), rows_ref)
+def left_body(per, tiles, c_ref, z_ref, yt_ref, inv_ref, left_ref, rows_ref):
+    factor(unfold(lines_of(z_ref, tiles * R, H, per)), rows_ref)
     inv = inverse_of(rows_ref)
-    mixed = nn(lower_t_of(rows_ref), s[:R, :R])
-    token_right = nn(inv, s[:R, R:])
+    inv_ref[...] = inv
+    left = nn(inv, yt_ref[...])
+    left_ref[...] = jnp.where(c_ref[0] == 0, left[:, :R], left[:, R:]).T
+
+
+def finish_body(per, c_ref, got_ref, inv_ref, z_ref, w_ref, right_ref, scores_ref, rows_ref):
+    s = total_of(got_ref)
+    prior = inv_ref[...]
+    factor(nt(nn(prior, unfold(s[R:])), prior), rows_ref)
+    inv = inverse_of(rows_ref)
+    tokens = nn(prior, s[:R])
+    mixed = nn(lower_t_of(rows_ref), tokens[:, :R])
+    token_right = nn(inv, tokens[:, R:])
     scores_ref[...] = jnp.sum(mixed * token_right, axis=0, keepdims=True)
-    whole = nn(inv, inv_ref[...])
+    whole = nn(inv, prior)
     core = c_ref[0]
     n = right_ref.shape[1]
     tiles = -(-n // (2 * LANES))
     width = tiles * LANES
-    mine, other = gathered(z_ref, tiles), gathered(w_ref, tiles)
+    mine, other = gathered(z_ref, tiles, per), gathered(w_ref, tiles, per)
     right_ref[:, :width] = product(whole, jnp.where(core == 0, mine, other))
     right_ref[:, width:] = product(whole, jnp.where(core == 0, other, mine))[:, : n - width]
 
 
-def exchanged(a, axes):
-    return lax.all_to_all(a, axes, split_axis=0, concat_axis=0, tiled=True)
-
-
-def summed(part, rounds):
-    for axis, bit in rounds:
-        pairs = [(i, i ^ bit) for i in range(lax.axis_size(axis))]
-        part = part + lax.ppermute(part, axis, pairs)
-    return part
+def exchanged(a, axes, groups=None):
+    return lax.all_to_all(
+        a, axes, split_axis=0, concat_axis=0, tiled=True, axis_index_groups=groups
+    )
+
+
+def lanes_of_chips(far, near):
+    def along_y(c):
+        return [[(y * near + z) * 2 + c for y in range(far)] for z in range(near)]
+
+    def along_z(c):
+        return [[(y * near + z) * 2 + c for z in range(near)] for y in range(far)]
+
+    return along_y(0) + along_z(1), along_z(0) + along_y(1)
 
 
 def per_device(gradient, start_block, activations, out_grads):
     far, near = lax.axis_size("y"), lax.axis_size("z")
     cols = lax.axis_size("x")
-    slots, peers = far * near, 2 * cols
+    peers = 2 * cols
     core_at = lax.axis_index("c")
     core = core_at.astype(jnp.int32).reshape(1)
     n = gradient.shape[1]
     width = -(-n // (2 * LANES)) * LANES
     piece = R // peers
 
-    rounds = [(axis, 1 << k) for axis in CHIPS for k in range(lax.axis_size(axis).bit_length() - 1)]
-    early, late = rounds[: len(rounds) // 2], rounds[len(rounds) // 2 :]
     lines = gradient.shape[0]
     first, g, send = call(
         first_body, (shape(peers, H, LANES), shape(lines, width), shape(lines, width)), 3, scalars=1
@@ -374,25 +393,36 @@
     a, b = swapped(core, activations, width)
     o, p = swapped(core, out_grads, out_grads.shape[1] // 2)
     square = [pltpu.VMEM((R, LANES), F32)]
-    block, whole = shape(slots, H, LANES), shape(peers, R + H, LANES)
-    half, small = shape(H, LANES), shape(R, R)
-
-    parts, gram = call(spread_first_body, (block, half), 4, scalars=1)(core, got, g, h)
-    arrived = exchanged(parts, CHIPS)
-    gram = summed(gram, early)
-    arrived, gram, a, b, o, p = lax.optimization_barrier((arrived, gram, a, b, o, p))
-    z = exchanged(call(total_body, block, 1)(arrived), CHIPS)
-    inv = call(factor_body, small, 1, scratch=square)(summed(gram, late))
-    partial = call(back_body, whole, 5, scalars=1)(core, z, g, h, inv)
+    tiles = width // LANES
+    each = -(-(tiles * R + H) // (far * near))
+    each += -each % (8 // near if near < 8 else 1)
+    per = near * each
+    first, second = lanes_of_chips(far, near)
+    flat = shape(far * per, LANES)
+    whole = shape(peers, R + H, LANES)
+
+    def summed(parts, *beside):
+        arrived = exchanged(parts.reshape(far, per, LANES), ROWS, first)
+        arrived, *beside = lax.optimization_barrier((arrived, *beside))
+        cut = call(cut_body, shape(near, each, LANES), 1)(arrived)
+        return exchanged(cut, ROWS, second), *beside
+
+    def spread_out(parts, more):
+        got = exchanged(parts, ROWS, second)
+        body = functools.partial(joined_body, each)
+        return exchanged(call(body, shape(far, per + more, LANES), 1)(got), ROWS, first)
+
+    parts = call(spread_first_body, flat, 4, scalars=1)(core, got, g, h)
+    arrived, a, b, o, p = summed(parts, a, b, o, p)
+    z = spread_out(call(total_body, shape(near, each, LANES), 1)(arrived), 0)
+    partial = call(back_body, whole, 4, scalars=1, scratch=square)(core, z, g, h)
 
     got = exchanged(partial, PEERS)
-    raw_shape = shape(R + H, LANES)
-    parts, raw = call(spread_body, (block, raw_shape), 4, scalars=1)(core, got, g, h)
-    arrived = exchanged(parts, CHIPS)
-    prior, gram = call(normal_body, (small, half), 1, scratch=square)(raw)
-    gram = summed(gram, early)
+    parts, yt = call(
+        spread_body, (flat, shape(R, LANES)), 4, scalars=1, scratch=square
+    )(core, got, g, h)
     eighth = lax.axis_index("x") * 2 + core_at
-    mine = lax.dynamic_slice_in_dim(raw, eighth * piece, piece, 0)
+    mine = lax.dynamic_slice_in_dim(yt, eighth * piece, piece, 0)
     moves = []
     for ys in range(far):
         for cs in range(2):
@@ -401,19 +431,25 @@
                 target = ((2 * xs + cs) * 2 + ys % 2) * cols + ys // 2
                 moves.append((source, target))
     lines = lax.ppermute(mine, ("y", "c", "x"), moves)
-    arrived, gram, lines = lax.optimization_barrier((arrived, gram, lines))
-    z = exchanged(
-        call(total_with_body, shape(slots, H + piece, LANES), 2)(arrived, lines), CHIPS
-    )
-    inv, left = call(left_body, (small, small), 4, scalars=1, scratch=square)(
-        core, summed(gram, late), raw, prior
-    )
-    z, inv, left = lax.optimization_barrier((z, inv, left))
-    w = other_core(z[:, :H])
-    partial = call(last_body, whole, 7, scalars=1)(core, z, inv, a, b, o, p)
+    arrived, lines = summed(parts, lines)
+    sums = call(total_with_body, shape(near, each + piece, LANES), 2)(arrived, lines)
+    z = spread_out(sums, near * piece)
+    w = other_core(z)
+    partial = call(last_body, whole, 6, scalars=1)(core, z, a, b, o, p)
     got = exchanged(partial, PEERS)
+    inv, left = call(
+        functools.partial(left_body, per, tiles),
+        (shape(R, R), shape(R, R)),
+        3,
+        scalars=1,
+        scratch=square,
+    )(core, z, yt)
     right, scores = call(
-        finish_body, (shape(R, n), shape(1, R)), 5, scalars=1, scratch=square
+        functools.partial(finish_body, per),
+        (shape(R, n), shape(1, R)),
+        5,
+        scalars=1,
+        scratch=square,
     )(core, got, inv, z, w)
     return (left, right.T, scores.reshape(-1))
 

time: 289 us -> 211 us (0.73)
  starting transfers between devices: 125 us -> 38.1 us
  blocking collectives: 42 us -> 112 us
  waiting for transfers between devices: 82.5 us -> 26.6 us
  local copies, waits for them, and re-layouts: 11.4 us -> 8.11 us
    ppermute x12 -> x0, waiting for transfers between devices: 81.2 us -> none  [summed(): part = part + lax.ppermute(part, axis, pairs)]
    all_to_all x3 -> x8, blocking collectives: 42 us -> 112 us  [exchanged(): lax.all_to_all(a, axes, split_axis=0, concat_axis=0, tiled=True, axis_ind...]
    ppermute x12 -> x0, starting transfers between devices: 39.8 us -> none  [summed(): part = part + lax.ppermute(part, axis, pairs)]
    all_to_all x4 -> x3, starting transfers between devices: 47.4 us -> 14.6 us  [exchanged(): lax.all_to_all(a, axes, split_axis=0, concat_axis=0, tiled=True, axis_ind...]
    all_to_all x4 -> x3, waiting for transfers between devices: 0.01 us -> 15.3 us  [exchanged(): lax.all_to_all(a, axes, split_axis=0, concat_axis=0, tiled=True, axis_ind...]
    ppermute x4, starting transfers between devices: 32 us -> 19.8 us  [other_core(): return lax.ppermute(a, 'c', [(0, 1), (1, 0)])]
    ppermute x1, waiting for transfers between devices: 1.28 us -> 10.2 us  [per_device(): lines = lax.ppermute(mine, ('y', 'c', 'x'), moves)]
    unnamed x32 -> x22, local copies, waits for them, and re-layouts: 11.2 us -> 8.1 us
  transfers between devices with their start and end apart: 21 -> 8, of which waited for: 12 -> 5; matrix products, arithmetic and copies ran while one was open for 0% -> 0% of each run, Pallas kernels for 4% -> 3%
where the time goes in v4:
time: 211 us; the launch traced here: 210 us
  blocking collectives  112 us (53%)
  starting transfers between devices  38.1 us (18%)
  waiting for transfers between devices  26.6 us (13%)
  Pallas kernels  24.7 us (12%)
  local copies, waits for them, and re-layouts  8.11 us (4%)
    all_to_all x8, blocking collectives, exchanged(): lax.all_to_all(a, axes, split_axis=0, concat_axis=0, tiled=True, axis_ind...  112 us
    ppermute x4, starting transfers between devices, other_core(): return lax.ppermute(a, 'c', [(0, 1), (1, 0)])  19.8 us
    all_to_all x3, waiting for transfers between devices, exchanged(): lax.all_to_all(a, axes, split_axis=0, concat_axis=0, tiled=True, axis_ind...  15.3 us
    all_to_all x3, starting transfers between devices, exchanged(): lax.all_to_all(a, axes, split_axis=0, concat_axis=0, tiled=True, axis_ind...  14.6 us
    ppermute x1, waiting for transfers between devices, per_device(): lines = lax.ppermute(mine, ('y', 'c', 'x'), moves)  10.2 us
    unnamed x22, local copies, waits for them, and re-layouts  8.1 us
    pallas_call x1, Pallas kernels, per_device(): call(functools.partial(finish_body, per), (shape(R, n), shape(1, R)), 5,...  5.8 us
    pallas_call x1, Pallas kernels, per_device(): call(back_body, whole, 4, scalars=1, scratch=square)(core, z, g, h)  4.81 us
  transfers between devices with their start and end apart: 8, of which 5 were waited for; matrix products, arithmetic and copies ran while one was open for 0% of the time, Pallas kernels for 3%

profile of v4, /device:TPU:1, one launch (start us, length us, event | category | flops | bytes accessed | tf_op | source)
XLA Modules:
  0.0 210.0 jit_solution(11412354902790374284)
XLA Ops:
  0.6 0.0 copy-start.1
  0.6 1.5 copy-done.1
  2.2 0.0 copy-start.2
  2.2 1.5 copy-done.2
  3.7 2.0 shard_map.67
  5.7 8.7 %collective-permute-start = (f32[64,3712]{1,0:T(8,128)S(1)}, f32[64,3712]{1,0:T(8,128)S(1)}, u32[]{:S(2)}, u32[]{:S(2)}) collective-permute-start(f32[64,3712]{1,0:T(8,128)S(1)} %get-tuple-element.25), channel_id=1, source_target_pairs={{0,4},{4,0},{1,5},{5,1},{2,6},{6,2},{3,7},{7,3},{8,12},{12,8},{9,1... | collective-permute-start | bytes 2850824 | tf_op jit(solution)/shard_map/ppermute | solution.py:194
  14.4 7.5 %all_to_all.55.got_ref = f32[8,32,128]{2,1,0:T(8,128)S(1)} all-to-all(f32[8,32,128]{2,1,0:T(8,128)S(1)} %get-tuple-element.23), channel_id=1, replica_groups=mesh['y'=8,'z'=8,'c'=2,'x'=4] {'c','x'}, dimensions={0} | all-to-all | bytes 262144 | tf_op jit(solution)/shard_map/all_to_all | solution.py:362
  22.0 0.0 collective-permute-done.h_ref
  22.0 1.1 shard_map.68
  23.1 0.0 copy-start
  23.1 0.9 copy-done
  24.0 0.0 copy-start.8
  24.0 6.6 %all-to-all-start.1 = ((f32[8,240,128]{2,1,0:T(8,128)}), f32[8,240,128]{2,1,0:T(8,128)S(1)}, u32[]{:S(2)}, u32[]{:S(2)}) async-start(f32[8,240,128]{2,1,0:T(8,128)} %bitcast.6), calls=%async_computation.1 | async-start | bytes 1966080 | tf_op jit(solution)/shard_map/all_to_all | solution.py:362
  30.6 0.0 copy-start.3
  30.6 1.5 copy-done.3
  32.2 0.1 shard_map.69
  32.3 0.0 copy-start.4
  32.3 0.9 copy-done.4
  33.2 1.9 collective-permute-start.1
  35.2 0.0 copy-done.8
  35.2 0.0 copy-start.9
  35.2 0.7 copy-done.9
  35.9 2.4 %collective-permute-start.2 = (f32[64,1024]{1,0:T(8,128)S(1)}, f32[64,1024]{1,0:T(8,128)S(1)}, u32[]{:S(2)}, u32[]{:S(2)}) collective-permute-start(f32[64,1024]{1,0:T(8,128)S(1)} %get-tuple-element.29), channel_id=1, source_target_pairs={{0,4},{4,0},{1,5},{5,1},{2,6},{6,2},{3,7},{7,3},{8,12},{12,8},{9,1... | collective-permute-start | bytes 786440 | tf_op jit(solution)/shard_map/ppermute | solution.py:194
  38.3 1.1 collective-permute-done.2.p_ref
  39.5 0.0 collective-permute-done.1.b_ref
  39.5 0.0 copy-start.6
  39.5 0.9 copy-done.6
  40.4 7.3 %all-to-all-done.1.got_ref = f32[8,240,128]{2,1,0:T(8,128)S(1)} async-done(((f32[8,240,128]{2,1,0:T(8,128)}), f32[8,240,128]{2,1,0:T(8,128)S(1)}, u32[]{:S(2)}, u32[]{:S(2)}) %all-to-all-start.1) | async-done | bytes 983072 | tf_op jit(solution)/shard_map/all_to_all | solution.py:362
  47.8 14.6 %all_to_all.56.got_ref = f32[8,30,128]{2,1,0:T(8,128)S(1)} all-to-all(f32[8,30,128]{2,1,0:T(8,128)S(1)} %shard_map.71), channel_id=1, replica_groups={{0,8,16,24,32,40,48,56},{64,72,80,88,96,104,112,120},{128,136,144,152,1..., dimensions={0} | all-to-all | bytes 245760 | tf_op jit(solution)/shard_map/all_to_all | solution.py:362
  62.4 10.3 %all_to_all.57.got_ref = f32[8,30,128]{2,1,0:T(8,128)S(1)} all-to-all(f32[8,30,128]{2,1,0:T(8,128)S(1)} %shard_map.72), channel_id=1, replica_groups={{0,8,16,24,32,40,48,56},{64,72,80,88,96,104,112,120},{128,136,144,152,1..., dimensions={0} | all-to-all | bytes 245760 | tf_op jit(solution)/shard_map/all_to_all | solution.py:362
  72.7 0.1 shard_map.73
  72.7 19.5 %all_to_all.58.z_ref = f32[8,240,128]{2,1,0:T(8,128)S(1)} all-to-all(f32[8,240,128]{2,1,0:T(8,128)S(1)} %shard_map.73), channel_id=1, replica_groups={{0,64,128,192,256,320,384,448},{8,72,136,200,264,328,392,456},{16,80,14..., dimensions={0} | all-to-all | bytes 1966080 | tf_op jit(solution)/shard_map/all_to_all | solution.py:362
  92.2 4.8 %shard_map.74 = f32[8,96,128]{2,1,0:T(8,128)S(1)} custom-call(s32[1]{0:T(128)} %bitcast.c_ref, f32[8,240,128]{2,1,0:T(8,128)S(1)} %all_to_all.58.z_ref, f32[64,3712]{1,0:T(8,128)S(1)} %get-tuple-element.24.g_ref, f32[64,3712]{1,0:T(8,128)S(1)} %collective-permute-done.h_ref), custom_call_target="tpu_custom_call" | custom-call | tf_op jit(solution)/shard_map/pallas_call | solution.py:418
  97.0 16.3 %all_to_all.59.got_ref = f32[8,96,128]{2,1,0:T(8,128)S(1)} all-to-all(f32[8,96,128]{2,1,0:T(8,128)S(1)} %shard_map.74), channel_id=1, replica_groups=mesh['y'=8,'z'=8,'c'=2,'x'=4] {'c','x'}, dimensions={0} | all-to-all | bytes 786432 | tf_op jit(solution)/shard_map/all_to_all | solution.py:362
  113.4 4.4 %shard_map.75 = (f32[1920,128]{1,0:T(8,128)}, f32[64,128]{1,0:T(8,128)S(1)}) custom-call(s32[1]{0:T(128)} %bitcast.c_ref, f32[8,96,128]{2,1,0:T(8,128)S(1)} %all_to_all.59.got_ref, f32[64,3712]{1,0:T(8,128)S(1)} %get-tuple-element.24.g_ref, f32[64,3712]{1,0:T(8,128)S(1)} %collective-permute-done.h_ref), custom_call_target="tpu_custom_call" | custom-call | tf_op jit(solution)/shard_map/pallas_call | solution.py:421
  117.8 3.6 %all-to-all-start.6 = ((f32[8,240,128]{2,1,0:T(8,128)}), f32[8,240,128]{2,1,0:T(8,128)S(1)}, u32[]{:S(2)}, u32[]{:S(2)}) async-start(f32[8,240,128]{2,1,0:T(8,128)} %bitcast.3), calls=%async_computation.6 | async-start | bytes 1966080 | tf_op jit(solution)/shard_map/all_to_all | solution.py:362
  121.4 3.8 %collective-permute-start.3 = (f32[8,128]{1,0:T(8,128)S(1)}, f32[8,128]{1,0:T(8,128)S(1)}, u32[]{:S(2)}, u32[]{:S(2)}) collective-permute-start(f32[8,128]{1,0:T(8,128)S(1)} %constant_dynamic-slice_fusion), channel_id=1, source_target_pairs={{0,0},{1,128},{2,256},{3,384},{4,64},{5,192},{6,320},{7,448},{64,4... | collective-permute-start | bytes 12296 | tf_op jit(solution)/shard_map/ppermute | solution.py:433
  125.2 10.2 %collective-permute-done.3.more_ref = f32[8,128]{1,0:T(8,128)S(1)} collective-permute-done((f32[8,128]{1,0:T(8,128)S(1)}, f32[8,128]{1,0:T(8,128)S(1)}, u32[]{:S(2)}, u32[]{:S(2)}) %collective-permute-start.3) | collective-permute-done | bytes 4128 | tf_op jit(solution)/shard_map/ppermute | solution.py:433
  135.4 3.3 %all-to-all-done.6.got_ref = f32[8,240,128]{2,1,0:T(8,128)S(1)} async-done(((f32[8,240,128]{2,1,0:T(8,128)}), f32[8,240,128]{2,1,0:T(8,128)S(1)}, u32[]{:S(2)}, u32[]{:S(2)}) %all-to-all-start.6) | async-done | bytes 983072 | tf_op jit(solution)/shard_map/all_to_all | solution.py:362
  138.7 10.3 %all_to_all.60.got_ref = f32[8,30,128]{2,1,0:T(8,128)S(1)} all-to-all(f32[8,30,128]{2,1,0:T(8,128)S(1)} %shard_map.76), channel_id=1, replica_groups={{0,8,16,24,32,40,48,56},{64,72,80,88,96,104,112,120},{128,136,144,152,1..., dimensions={0} | all-to-all | bytes 245760 | tf_op jit(solution)/shard_map/all_to_all | solution.py:362
  149.1 10.7 %all_to_all.61.got_ref = f32[8,38,128]{2,1,0:T(8,128)S(1)} all-to-all(f32[8,38,128]{2,1,0:T(8,128)S(1)} %shard_map.77), channel_id=1, replica_groups={{0,8,16,24,32,40,48,56},{64,72,80,88,96,104,112,120},{128,136,144,152,1..., dimensions={0} | all-to-all | bytes 311296 | tf_op jit(solution)/shard_map/all_to_all | solution.py:362
  159.7 0.0 copy-start.5
  159.7 0.0 copy-start.7
  159.7 0.0 copy-start.10
  159.7 0.1 shard_map.78
  159.8 22.4 %all_to_all.62.z_ref = f32[8,304,128]{2,1,0:T(8,128)S(1)} all-to-all(f32[8,304,128]{2,1,0:T(8,128)S(1)} %shard_map.78), channel_id=1, replica_groups={{0,64,128,192,256,320,384,448},{8,72,136,200,264,328,392,456},{16,80,14..., dimensions={0} | all-to-all | bytes 2490368 | tf_op jit(solution)/shard_map/all_to_all | solution.py:362
  182.2 6.8 %collective-permute-start.4 = (f32[8,304,128]{2,1,0:T(8,128)S(1)}, f32[8,304,128]{2,1,0:T(8,128)S(1)}, u32[]{:S(2)}, u32[]{:S(2)}) collective-permute-start(f32[8,304,128]{2,1,0:T(8,128)S(1)} %all_to_all.62.z_ref), channel_id=1, source_target_pairs={{0,4},{4,0},{1,5},{5,1},{2,6},{6,2},{3,7},{7,3},{8,12},{12,8},{9,1... | collective-permute-start | bytes 3735560 | tf_op jit(solution)/shard_map/ppermute | solution.py:194
  189.0 0.0 copy-done.5
  189.0 0.0 copy-done.7
  189.1 0.0 copy-done.10
  189.1 2.7 %shard_map.80 = f32[8,96,128]{2,1,0:T(8,128)} custom-call(s32[1]{0:T(128)} %bitcast.c_ref, f32[8,304,128]{2,1,0:T(8,128)S(1)} %all_to_all.62.z_ref, f32[64,3712]{1,0:T(8,128)S(1)} %copy-done.5, f32[64,3712]{1,0:T(8,128)S(1)} %copy-done.7, f32[64,1024]{1,0:T(8,128)S(1)} %copy-done.10, f32[64,1024]{1,0:T(8,128)S(1)} %collective-permute-done.2.p_ref), custom_call_target="tpu_custom_call" | custom-call | tf_op jit(solution)/shard_map/pallas_call | solution.py:438
  191.8 4.4 %all-to-all-start.10 = ((f32[8,96,128]{2,1,0:T(8,128)}), f32[8,96,128]{2,1,0:T(8,128)S(1)}, u32[]{:S(2)}, u32[]{:S(2)}) async-start(f32[8,96,128]{2,1,0:T(8,128)} %shard_map.80), calls=%async_computation.10 | async-start | bytes 786432 | tf_op jit(solution)/shard_map/all_to_all | solution.py:362
  196.2 3.3 %shard_map.79 = (f32[64,64]{1,0:T(8,128)S(1)}, f32[64,64]{1,0:T(8,128)}) custom-call(s32[1]{0:T(128)} %bitcast.c_ref, f32[8,304,128]{2,1,0:T(8,128)S(1)} %all_to_all.62.z_ref, f32[64,128]{1,0:T(8,128)S(1)} %get-tuple-element.32.yt_ref), custom_call_target="tpu_custom_call" | custom-call | tf_op jit(solution)/shard_map/pallas_call | solution.py:440
  199.5 4.7 %all-to-all-done.10.got_ref = f32[8,96,128]{2,1,0:T(8,128)S(1)} async-done(((f32[8,96,128]{2,1,0:T(8,128)}), f32[8,96,128]{2,1,0:T(8,128)S(1)}, u32[]{:S(2)}, u32[]{:S(2)}) %all-to-all-start.10) | async-done | bytes 393248 | tf_op jit(solution)/shard_map/all_to_all | solution.py:362
  204.2 0.0 collective-permute-done.4.w_ref
  204.2 5.8 %shard_map.81 = (f32[64,7392]{1,0:T(8,128)}, f32[1,64]{1,0:T(1,128)}) custom-call(s32[1]{0:T(128)} %bitcast.c_ref, f32[8,96,128]{2,1,0:T(8,128)S(1)} %all-to-all-done.10.got_ref, f32[64,64]{1,0:T(8,128)S(1)} %get-tuple-element.40.inv_ref, f32[8,304,128]{2,1,0:T(8,128)S(1)} %all_to_all.62.z_ref, f32[8,304,128]{2,1,0:T(8,128)S(1)} %collective-permute-done.4.w_ref), custom_call_target="tpu_custom_call" | custom-call | tf_op jit(solution)/shard_map/pallas_call | solution.py:447
  (6 shorter events, 0.2 us)
Async XLA Ops:
  0.6 1.5 copy-start.1
  2.2 1.5 copy-start.2
  5.7 16.3 %collective-permute-start = (f32[64,3712]{1,0:T(8,128)S(1)}, f32[64,3712]{1,0:T(8,128)S(1)}, u32[]{:S(2)}, u32[]{:S(2)}) collective-permute-start(f32[64,3712]{1,0:T(8,128)S(1)} %get-tuple-element.25), channel_id=1, source_target_pairs={{0,4},{4,0},{1,5},{5,1},{2,6},{6,2},{3,7},{7,3},{8,12},{12,8},{9,1... | collective-permute-start | bytes 2850824 | tf_op jit(solution)/shard_map/ppermute | solution.py:194
  23.1 0.9 copy-start
  24.0 11.1 %copy-start.8 = (f32[64,2048]{1,0:T(8,128)S(1)}, f32[64,2048]{1,0:T(8,128)}, u32[]{:S(2)}) copy-start(f32[64,2048]{1,0:T(8,128)} %a_ref.3) | copy-start | bytes 1572868
  24.0 23.7 %all-to-all-start.1 = ((f32[8,240,128]{2,1,0:T(8,128)}), f32[8,240,128]{2,1,0:T(8,128)S(1)}, u32[]{:S(2)}, u32[]{:S(2)}) async-start(f32[8,240,128]{2,1,0:T(8,128)} %bitcast.6), calls=%async_computation.1 | async-start | bytes 1966080 | tf_op jit(solution)/shard_map/all_to_all | solution.py:362
  30.6 1.5 copy-start.3
  32.3 1.0 copy-start.4
  33.2 6.2 %collective-permute-start.1 = (f32[64,3712]{1,0:T(8,128)S(1)}, f32[64,3712]{1,0:T(8,128)S(1)}, u32[]{:S(2)}, u32[]{:S(2)}) collective-permute-start(f32[64,3712]{1,0:T(8,128)S(1)} %get-tuple-element.27), channel_id=1, source_target_pairs={{0,4},{4,0},{1,5},{5,1},{2,6},{6,2},{3,7},{7,3},{8,12},{12,8},{9,1... | collective-permute-start | bytes 2850824 | tf_op jit(solution)/shard_map/ppermute | solution.py:194
  35.2 0.7 copy-start.9
  35.9 3.5 %collective-permute-start.2 = (f32[64,1024]{1,0:T(8,128)S(1)}, f32[64,1024]{1,0:T(8,128)S(1)}, u32[]{:S(2)}, u32[]{:S(2)}) collective-permute-start(f32[64,1024]{1,0:T(8,128)S(1)} %get-tuple-element.29), channel_id=1, source_target_pairs={{0,4},{4,0},{1,5},{5,1},{2,6},{6,2},{3,7},{7,3},{8,12},{12,8},{9,1... | collective-permute-start | bytes 786440 | tf_op jit(solution)/shard_map/ppermute | solution.py:194
  39.5 0.9 copy-start.6
  117.8 20.9 %all-to-all-start.6 = ((f32[8,240,128]{2,1,0:T(8,128)}), f32[8,240,128]{2,1,0:T(8,128)S(1)}, u32[]{:S(2)}, u32[]{:S(2)}) async-start(f32[8,240,128]{2,1,0:T(8,128)} %bitcast.3), calls=%async_computation.6 | async-start | bytes 1966080 | tf_op jit(solution)/shard_map/all_to_all | solution.py:362
  121.4 14.0 %collective-permute-start.3 = (f32[8,128]{1,0:T(8,128)S(1)}, f32[8,128]{1,0:T(8,128)S(1)}, u32[]{:S(2)}, u32[]{:S(2)}) collective-permute-start(f32[8,128]{1,0:T(8,128)S(1)} %constant_dynamic-slice_fusion), channel_id=1, source_target_pairs={{0,0},{1,128},{2,256},{3,384},{4,64},{5,192},{6,320},{7,448},{64,4... | collective-permute-start | bytes 12296 | tf_op jit(solution)/shard_map/ppermute | solution.py:433
  159.7 29.3 %copy-start.5 = (f32[64,3712]{1,0:T(8,128)S(1)}, f32[64,3712]{1,0:T(8,128)}, u32[]{:S(2)}) copy-start(f32[64,3712]{1,0:T(8,128)} %copy-done.4) | copy-start | bytes 2850820
  159.7 29.3 %copy-start.7 = (f32[64,3712]{1,0:T(8,128)S(1)}, f32[64,3712]{1,0:T(8,128)}, u32[]{:S(2)}) copy-start(f32[64,3712]{1,0:T(8,128)} %copy-done.6) | copy-start | bytes 2850820
  159.7 29.3 %copy-start.10 = (f32[64,1024]{1,0:T(8,128)S(1)}, f32[64,1024]{1,0:T(8,128)}, u32[]{:S(2)}) copy-start(f32[64,1024]{1,0:T(8,128)} %copy-done.9) | copy-start | bytes 786436
  182.2 21.9 %collective-permute-start.4 = (f32[8,304,128]{2,1,0:T(8,128)S(1)}, f32[8,304,128]{2,1,0:T(8,128)S(1)}, u32[]{:S(2)}, u32[]{:S(2)}) collective-permute-start(f32[8,304,128]{2,1,0:T(8,128)S(1)} %all_to_all.62.z_ref), channel_id=1, source_target_pairs={{0,4},{4,0},{1,5},{5,1},{2,6},{6,2},{3,7},{7,3},{8,12},{12,8},{9,1... | collective-permute-start | bytes 3735560 | tf_op jit(solution)/shard_map/ppermute | solution.py:194
  191.8 12.4 %all-to-all-start.10 = ((f32[8,96,128]{2,1,0:T(8,128)}), f32[8,96,128]{2,1,0:T(8,128)S(1)}, u32[]{:S(2)}, u32[]{:S(2)}) async-start(f32[8,96,128]{2,1,0:T(8,128)} %shard_map.80), calls=%async_computation.10 | async-start | bytes 786432 | tf_op jit(solution)/shard_map/all_to_all | solution.py:362

commit v5 on v4

--- a/solution.py
+++ b/solution.py
@@ -83,11 +83,6 @@
 
 def shape(*dims):
     return jax.ShapeDtypeStruct(dims, F32)
-
-
-def rsqrt(s):
-    t = lax.rsqrt(s)
-    return t * (1.5 - 0.5 * s * t * t)
 
 
 def fold(square):
@@ -125,7 +120,7 @@
             d = splat[i]
             for q in range(i):
                 d = d - low[i][q] * low[i][q]
-            inv[i] = rsqrt(d)
+            inv[i] = lax.rsqrt(d)
 
         def solved(lines):
             done = []
@@ -240,13 +235,6 @@
     return s
 
 
-def cut_body(got_ref, out_ref):
-    s = total_of(got_ref)
-    n = out_ref.shape[1]
-    for i in range(out_ref.shape[0]):
-        out_ref[i] = s[i * n : (i + 1) * n]
-
-
 def total_body(got_ref, out_ref):
     s = total_of(got_ref)
     for i in range(out_ref.shape[0]):
@@ -264,9 +252,11 @@
 
 def joined_body(lines, got_ref, out_ref):
     n = got_ref.shape[0]
-    heads = [got_ref[i, :lines] for i in range(n)]
+    s = got_ref[0, :lines]
+    for i in range(1, n):
+        s = s + got_ref[i, :lines]
     tails = [got_ref[i, lines:] for i in range(n) if got_ref.shape[1] > lines]
-    s = jnp.concatenate(heads + tails, axis=0)
+    s = jnp.concatenate([s] + tails, axis=0)
     for i in range(out_ref.shape[0]):
         out_ref[i] = s
 
@@ -394,27 +384,23 @@
     o, p = swapped(core, out_grads, out_grads.shape[1] // 2)
     square = [pltpu.VMEM((R, LANES), F32)]
     tiles = width // LANES
-    each = -(-(tiles * R + H) // (far * near))
-    each += -each % (8 // near if near < 8 else 1)
-    per = near * each
+    per = -(-(tiles * R + H) // (8 * far)) * 8
     first, second = lanes_of_chips(far, near)
     flat = shape(far * per, LANES)
     whole = shape(peers, R + H, LANES)
 
     def summed(parts, *beside):
         arrived = exchanged(parts.reshape(far, per, LANES), ROWS, first)
-        arrived, *beside = lax.optimization_barrier((arrived, *beside))
-        cut = call(cut_body, shape(near, each, LANES), 1)(arrived)
-        return exchanged(cut, ROWS, second), *beside
+        return lax.optimization_barrier((arrived, *beside))
 
     def spread_out(parts, more):
         got = exchanged(parts, ROWS, second)
-        body = functools.partial(joined_body, each)
-        return exchanged(call(body, shape(far, per + more, LANES), 1)(got), ROWS, first)
+        body = functools.partial(joined_body, per)
+        return exchanged(call(body, shape(far, per + near * more, LANES), 1)(got), ROWS, first)
 
     parts = call(spread_first_body, flat, 4, scalars=1)(core, got, g, h)
     arrived, a, b, o, p = summed(parts, a, b, o, p)
-    z = spread_out(call(total_body, shape(near, each, LANES), 1)(arrived), 0)
+    z = spread_out(call(total_body, shape(near, per, LANES), 1)(arrived), 0)
     partial = call(back_body, whole, 4, scalars=1, scratch=square)(core, z, g, h)
 
     got = exchanged(partial, PEERS)
@@ -432,8 +418,8 @@
                 moves.append((source, target))
     lines = lax.ppermute(mine, ("y", "c", "x"), moves)
     arrived, lines = summed(parts, lines)
-    sums = call(total_with_body, shape(near, each + piece, LANES), 2)(arrived, lines)
-    z = spread_out(sums, near * piece)
+    sums = call(total_with_body, shape(near, per + piece, LANES), 2)(arrived, lines)
+    z = spread_out(sums, piece)
     w = other_core(z)
     partial = call(last_body, whole, 6, scalars=1)(core, z, a, b, o, p)
     got = exchanged(partial, PEERS)

time: 211 us -> 205 us (0.972)
  blocking collectives: 112 us -> 108 us
    all_to_all x8 -> x6, blocking collectives: 112 us -> 108 us  [exchanged(): lax.all_to_all(a, axes, split_axis=0, concat_axis=0, tiled=True, axis_ind...]
where the time goes in v5:
time: 205 us; the launch traced here: 204 us
  blocking collectives  108 us (53%)
  starting transfers between devices  36.7 us (18%)
  waiting for transfers between devices  27.1 us (13%)
  Pallas kernels  23 us (11%)
  local copies, waits for them, and re-layouts  8.11 us (4%)
    all_to_all x6, blocking collectives, exchanged(): lax.all_to_all(a, axes, split_axis=0, concat_axis=0, tiled=True, axis_ind...  108 us
    ppermute x4, starting transfers between devices, other_core(): return lax.ppermute(a, 'c', [(0, 1), (1, 0)])  18.3 us
    all_to_all x3, waiting for transfers between devices, exchanged(): lax.all_to_all(a, axes, split_axis=0, concat_axis=0, tiled=True, axis_ind...  15.7 us
    all_to_all x3, starting transfers between devices, exchanged(): lax.all_to_all(a, axes, split_axis=0, concat_axis=0, tiled=True, axis_ind...  14.6 us
    ppermute x1, waiting for transfers between devices, per_device(): lines = lax.ppermute(mine, ('y', 'c', 'x'), moves)  10.2 us
    unnamed x22, local copies, waits for them, and re-layouts  8.1 us
    pallas_call x1, Pallas kernels, per_device(): call(functools.partial(finish_body, per), (shape(R, n), shape(1, R)), 5,...  5.42 us
    pallas_call x1, Pallas kernels, per_device(): call(back_body, whole, 4, scalars=1, scratch=square)(core, z, g, h)  4.36 us
  transfers between devices with their start and end apart: 8, of which 5 were waited for; matrix products, arithmetic and copies ran while one was open for 0% of the time, Pallas kernels for 3%

profile of v5, /device:TPU:1, one launch (start us, length us, event | category | flops | bytes accessed | tf_op | source)
XLA Modules:
  0.0 204.1 jit_solution(13552882457327704621)
XLA Ops:
  0.6 0.0 copy-start.1
  0.6 1.5 copy-done.1
  2.2 0.0 copy-start.2
  2.2 1.5 copy-done.2
  3.7 2.0 shard_map.67
  5.7 8.7 %collective-permute-start = (f32[64,3712]{1,0:T(8,128)S(1)}, f32[64,3712]{1,0:T(8,128)S(1)}, u32[]{:S(2)}, u32[]{:S(2)}) collective-permute-start(f32[64,3712]{1,0:T(8,128)S(1)} %get-tuple-element.25), channel_id=1, source_target_pairs={{0,4},{4,0},{1,5},{5,1},{2,6},{6,2},{3,7},{7,3},{8,12},{12,8},{9,1... | collective-permute-start | bytes 2850824 | tf_op jit(solution)/shard_map/ppermute | solution.py:189
  14.4 7.5 %all_to_all.45.got_ref = f32[8,32,128]{2,1,0:T(8,128)S(1)} all-to-all(f32[8,32,128]{2,1,0:T(8,128)S(1)} %get-tuple-element.23), channel_id=1, replica_groups=mesh['y'=8,'z'=8,'c'=2,'x'=4] {'c','x'}, dimensions={0} | all-to-all | bytes 262144 | tf_op jit(solution)/shard_map/all_to_all | solution.py:352
  22.0 0.0 collective-permute-done.h_ref
  22.0 1.1 shard_map.68
  23.1 0.0 copy-start
  23.1 0.9 copy-done
  24.0 0.0 copy-start.8
  24.0 6.6 %all-to-all-start.1 = ((f32[8,240,128]{2,1,0:T(8,128)}), f32[8,240,128]{2,1,0:T(8,128)S(1)}, u32[]{:S(2)}, u32[]{:S(2)}) async-start(f32[8,240,128]{2,1,0:T(8,128)} %bitcast.6), calls=%async_computation.1 | async-start | bytes 1966080 | tf_op jit(solution)/shard_map/all_to_all | solution.py:352
  30.6 0.0 copy-start.3
  30.6 1.5 copy-done.3
  32.2 0.1 shard_map.69
  32.3 0.0 copy-start.4
  32.3 0.9 copy-done.4
  33.2 1.9 collective-permute-start.1
  35.2 0.0 copy-done.8
  35.2 0.0 copy-start.9
  35.2 0.7 copy-done.9
  35.9 2.4 %collective-permute-start.2 = (f32[64,1024]{1,0:T(8,128)S(1)}, f32[64,1024]{1,0:T(8,128)S(1)}, u32[]{:S(2)}, u32[]{:S(2)}) collective-permute-start(f32[64,1024]{1,0:T(8,128)S(1)} %get-tuple-element.29), channel_id=1, source_target_pairs={{0,4},{4,0},{1,5},{5,1},{2,6},{6,2},{3,7},{7,3},{8,12},{12,8},{9,1... | collective-permute-start | bytes 786440 | tf_op jit(solution)/shard_map/ppermute | solution.py:189
  38.3 1.1 collective-permute-done.2.p_ref
  39.5 0.0 collective-permute-done.1.b_ref
  39.5 0.0 copy-start.6
  39.5 0.9 copy-done.6
  40.4 7.3 %all-to-all-done.1.got_ref = f32[8,240,128]{2,1,0:T(8,128)S(1)} async-done(((f32[8,240,128]{2,1,0:T(8,128)}), f32[8,240,128]{2,1,0:T(8,128)S(1)}, u32[]{:S(2)}, u32[]{:S(2)}) %all-to-all-start.1) | async-done | bytes 983072 | tf_op jit(solution)/shard_map/all_to_all | solution.py:352
  47.7 0.1 shard_map.71
  47.8 24.0 %all_to_all.46.got_ref = f32[8,240,128]{2,1,0:T(8,128)S(1)} all-to-all(f32[8,240,128]{2,1,0:T(8,128)S(1)} %shard_map.71), channel_id=1, replica_groups={{0,8,16,24,32,40,48,56},{64,72,80,88,96,104,112,120},{128,136,144,152,1..., dimensions={0} | all-to-all | bytes 1966080 | tf_op jit(solution)/shard_map/all_to_all | solution.py:352
  71.8 0.1 shard_map.72
  71.9 19.5 %all_to_all.47.z_ref = f32[8,240,128]{2,1,0:T(8,128)S(1)} all-to-all(f32[8,240,128]{2,1,0:T(8,128)S(1)} %shard_map.72), channel_id=1, replica_groups={{0,64,128,192,256,320,384,448},{8,72,136,200,264,328,392,456},{16,80,14..., dimensions={0} | all-to-all | bytes 1966080 | tf_op jit(solution)/shard_map/all_to_all | solution.py:352
  91.3 4.4 %shard_map.73 = f32[8,96,128]{2,1,0:T(8,128)S(1)} custom-call(s32[1]{0:T(128)} %bitcast.c_ref, f32[8,240,128]{2,1,0:T(8,128)S(1)} %all_to_all.47.z_ref, f32[64,3712]{1,0:T(8,128)S(1)} %get-tuple-element.24.g_ref, f32[64,3712]{1,0:T(8,128)S(1)} %collective-permute-done.h_ref), custom_call_target="tpu_custom_call" | custom-call | tf_op jit(solution)/shard_map/pallas_call | solution.py:404
  95.7 14.9 %all_to_all.48.got_ref = f32[8,96,128]{2,1,0:T(8,128)S(1)} all-to-all(f32[8,96,128]{2,1,0:T(8,128)S(1)} %shard_map.73), channel_id=1, replica_groups=mesh['y'=8,'z'=8,'c'=2,'x'=4] {'c','x'}, dimensions={0} | all-to-all | bytes 786432 | tf_op jit(solution)/shard_map/all_to_all | solution.py:352
  110.6 4.0 %shard_map.74 = (f32[1920,128]{1,0:T(8,128)}, f32[64,128]{1,0:T(8,128)S(1)}) custom-call(s32[1]{0:T(128)} %bitcast.c_ref, f32[8,96,128]{2,1,0:T(8,128)S(1)} %all_to_all.48.got_ref, f32[64,3712]{1,0:T(8,128)S(1)} %get-tuple-element.24.g_ref, f32[64,3712]{1,0:T(8,128)S(1)} %collective-permute-done.h_ref), custom_call_target="tpu_custom_call" | custom-call | tf_op jit(solution)/shard_map/pallas_call | solution.py:407
  114.7 3.6 %all-to-all-start.5 = ((f32[8,240,128]{2,1,0:T(8,128)}), f32[8,240,128]{2,1,0:T(8,128)S(1)}, u32[]{:S(2)}, u32[]{:S(2)}) async-start(f32[8,240,128]{2,1,0:T(8,128)} %bitcast.3), calls=%async_computation.5 | async-start | bytes 1966080 | tf_op jit(solution)/shard_map/all_to_all | solution.py:352
  118.2 3.8 %collective-permute-start.3 = (f32[8,128]{1,0:T(8,128)S(1)}, f32[8,128]{1,0:T(8,128)S(1)}, u32[]{:S(2)}, u32[]{:S(2)}) collective-permute-start(f32[8,128]{1,0:T(8,128)S(1)} %constant_dynamic-slice_fusion), channel_id=1, source_target_pairs={{0,0},{1,128},{2,256},{3,384},{4,64},{5,192},{6,320},{7,448},{64,4... | collective-permute-start | bytes 12296 | tf_op jit(solution)/shard_map/ppermute | solution.py:419
  122.0 10.2 %collective-permute-done.3.more_ref = f32[8,128]{1,0:T(8,128)S(1)} collective-permute-done((f32[8,128]{1,0:T(8,128)S(1)}, f32[8,128]{1,0:T(8,128)S(1)}, u32[]{:S(2)}, u32[]{:S(2)}) %collective-permute-start.3) | collective-permute-done | bytes 4128 | tf_op jit(solution)/shard_map/ppermute | solution.py:419
  132.3 3.3 %all-to-all-done.5.got_ref = f32[8,240,128]{2,1,0:T(8,128)S(1)} async-done(((f32[8,240,128]{2,1,0:T(8,128)}), f32[8,240,128]{2,1,0:T(8,128)S(1)}, u32[]{:S(2)}, u32[]{:S(2)}) %all-to-all-start.5) | async-done | bytes 983072 | tf_op jit(solution)/shard_map/all_to_all | solution.py:352
  135.5 0.1 shard_map.75
  135.6 19.8 %all_to_all.49.got_ref = f32[8,248,128]{2,1,0:T(8,128)S(1)} all-to-all(f32[8,248,128]{2,1,0:T(8,128)S(1)} %shard_map.75), channel_id=1, replica_groups={{0,8,16,24,32,40,48,56},{64,72,80,88,96,104,112,120},{128,136,144,152,1..., dimensions={0} | all-to-all | bytes 2031616 | tf_op jit(solution)/shard_map/all_to_all | solution.py:352
  155.4 0.0 copy-start.5
  155.4 0.0 copy-start.7
  155.4 0.0 copy-start.10
  155.4 0.1 shard_map.76
  155.5 22.7 %all_to_all.50.z_ref = f32[8,304,128]{2,1,0:T(8,128)S(1)} all-to-all(f32[8,304,128]{2,1,0:T(8,128)S(1)} %shard_map.76), channel_id=1, replica_groups={{0,64,128,192,256,320,384,448},{8,72,136,200,264,328,392,456},{16,80,14..., dimensions={0} | all-to-all | bytes 2490368 | tf_op jit(solution)/shard_map/all_to_all | solution.py:352
  178.2 5.3 %collective-permute-start.4 = (f32[8,304,128]{2,1,0:T(8,128)S(1)}, f32[8,304,128]{2,1,0:T(8,128)S(1)}, u32[]{:S(2)}, u32[]{:S(2)}) collective-permute-start(f32[8,304,128]{2,1,0:T(8,128)S(1)} %all_to_all.50.z_ref), channel_id=1, source_target_pairs={{0,4},{4,0},{1,5},{5,1},{2,6},{6,2},{3,7},{7,3},{8,12},{12,8},{9,1... | collective-permute-start | bytes 3735560 | tf_op jit(solution)/shard_map/ppermute | solution.py:189
  183.6 0.0 copy-done.5
  183.6 0.0 copy-done.7
  183.6 0.0 copy-done.10
  183.6 2.7 %shard_map.78 = f32[8,96,128]{2,1,0:T(8,128)} custom-call(s32[1]{0:T(128)} %bitcast.c_ref, f32[8,304,128]{2,1,0:T(8,128)S(1)} %all_to_all.50.z_ref, f32[64,3712]{1,0:T(8,128)S(1)} %copy-done.5, f32[64,3712]{1,0:T(8,128)S(1)} %copy-done.7, f32[64,1024]{1,0:T(8,128)S(1)} %copy-done.10, f32[64,1024]{1,0:T(8,128)S(1)} %collective-permute-done.2.p_ref), custom_call_target="tpu_custom_call" | custom-call | tf_op jit(solution)/shard_map/pallas_call | solution.py:424
  186.3 4.4 %all-to-all-start.8 = ((f32[8,96,128]{2,1,0:T(8,128)}), f32[8,96,128]{2,1,0:T(8,128)S(1)}, u32[]{:S(2)}, u32[]{:S(2)}) async-start(f32[8,96,128]{2,1,0:T(8,128)} %shard_map.78), calls=%async_computation.8 | async-start | bytes 786432 | tf_op jit(solution)/shard_map/all_to_all | solution.py:352
  190.7 2.9 %shard_map.77 = (f32[64,64]{1,0:T(8,128)S(1)}, f32[64,64]{1,0:T(8,128)}) custom-call(s32[1]{0:T(128)} %bitcast.c_ref, f32[8,304,128]{2,1,0:T(8,128)S(1)} %all_to_all.50.z_ref, f32[64,128]{1,0:T(8,128)S(1)} %get-tuple-element.32.yt_ref), custom_call_target="tpu_custom_call" | custom-call | tf_op jit(solution)/shard_map/pallas_call | solution.py:426
  193.6 5.1 %all-to-all-done.8.got_ref = f32[8,96,128]{2,1,0:T(8,128)S(1)} async-done(((f32[8,96,128]{2,1,0:T(8,128)}), f32[8,96,128]{2,1,0:T(8,128)S(1)}, u32[]{:S(2)}, u32[]{:S(2)}) %all-to-all-start.8) | async-done | bytes 393248 | tf_op jit(solution)/shard_map/all_to_all | solution.py:352
  198.7 0.0 collective-permute-done.4.w_ref
  198.7 5.4 %shard_map.79 = (f32[64,7392]{1,0:T(8,128)}, f32[1,64]{1,0:T(1,128)}) custom-call(s32[1]{0:T(128)} %bitcast.c_ref, f32[8,96,128]{2,1,0:T(8,128)S(1)} %all-to-all-done.8.got_ref, f32[64,64]{1,0:T(8,128)S(1)} %get-tuple-element.40.inv_ref, f32[8,304,128]{2,1,0:T(8,128)S(1)} %all_to_all.50.z_ref, f32[8,304,128]{2,1,0:T(8,128)S(1)} %collective-permute-done.4.w_ref), custom_call_target="tpu_custom_call" | custom-call | tf_op jit(solution)/shard_map/pallas_call | solution.py:433
  (2 shorter events, 0.1 us)
Async XLA Ops:
  0.6 1.5 copy-start.1
  2.2 1.5 copy-start.2
  5.7 16.3 %collective-permute-start = (f32[64,3712]{1,0:T(8,128)S(1)}, f32[64,3712]{1,0:T(8,128)S(1)}, u32[]{:S(2)}, u32[]{:S(2)}) collective-permute-start(f32[64,3712]{1,0:T(8,128)S(1)} %get-tuple-element.25), channel_id=1, source_target_pairs={{0,4},{4,0},{1,5},{5,1},{2,6},{6,2},{3,7},{7,3},{8,12},{12,8},{9,1... | collective-permute-start | bytes 2850824 | tf_op jit(solution)/shard_map/ppermute | solution.py:189
  23.1 0.9 copy-start
  24.0 11.1 %copy-start.8 = (f32[64,2048]{1,0:T(8,128)S(1)}, f32[64,2048]{1,0:T(8,128)}, u32[]{:S(2)}) copy-start(f32[64,2048]{1,0:T(8,128)} %a_ref.3) | copy-start | bytes 1572868
  24.0 23.7 %all-to-all-start.1 = ((f32[8,240,128]{2,1,0:T(8,128)}), f32[8,240,128]{2,1,0:T(8,128)S(1)}, u32[]{:S(2)}, u32[]{:S(2)}) async-start(f32[8,240,128]{2,1,0:T(8,128)} %bitcast.6), calls=%async_computation.1 | async-start | bytes 1966080 | tf_op jit(solution)/shard_map/all_to_all | solution.py:352
  30.6 1.5 copy-start.3
  32.3 1.0 copy-start.4
  33.2 6.2 %collective-permute-start.1 = (f32[64,3712]{1,0:T(8,128)S(1)}, f32[64,3712]{1,0:T(8,128)S(1)}, u32[]{:S(2)}, u32[]{:S(2)}) collective-permute-start(f32[64,3712]{1,0:T(8,128)S(1)} %get-tuple-element.27), channel_id=1, source_target_pairs={{0,4},{4,0},{1,5},{5,1},{2,6},{6,2},{3,7},{7,3},{8,12},{12,8},{9,1... | collective-permute-start | bytes 2850824 | tf_op jit(solution)/shard_map/ppermute | solution.py:189
  35.2 0.7 copy-start.9
  35.9 3.5 %collective-permute-start.2 = (f32[64,1024]{1,0:T(8,128)S(1)}, f32[64,1024]{1,0:T(8,128)S(1)}, u32[]{:S(2)}, u32[]{:S(2)}) collective-permute-start(f32[64,1024]{1,0:T(8,128)S(1)} %get-tuple-element.29), channel_id=1, source_target_pairs={{0,4},{4,0},{1,5},{5,1},{2,6},{6,2},{3,7},{7,3},{8,12},{12,8},{9,1... | collective-permute-start | bytes 786440 | tf_op jit(solution)/shard_map/ppermute | solution.py:189
  39.5 0.9 copy-start.6
  114.7 20.9 %all-to-all-start.5 = ((f32[8,240,128]{2,1,0:T(8,128)}), f32[8,240,128]{2,1,0:T(8,128)S(1)}, u32[]{:S(2)}, u32[]{:S(2)}) async-start(f32[8,240,128]{2,1,0:T(8,128)} %bitcast.3), calls=%async_computation.5 | async-start | bytes 1966080 | tf_op jit(solution)/shard_map/all_to_all | solution.py:352
  118.2 14.0 %collective-permute-start.3 = (f32[8,128]{1,0:T(8,128)S(1)}, f32[8,128]{1,0:T(8,128)S(1)}, u32[]{:S(2)}, u32[]{:S(2)}) collective-permute-start(f32[8,128]{1,0:T(8,128)S(1)} %constant_dynamic-slice_fusion), channel_id=1, source_target_pairs={{0,0},{1,128},{2,256},{3,384},{4,64},{5,192},{6,320},{7,448},{64,4... | collective-permute-start | bytes 12296 | tf_op jit(solution)/shard_map/ppermute | solution.py:419
  155.4 28.1 %copy-start.5 = (f32[64,3712]{1,0:T(8,128)S(1)}, f32[64,3712]{1,0:T(8,128)}, u32[]{:S(2)}) copy-start(f32[64,3712]{1,0:T(8,128)} %copy-done.4) | copy-start | bytes 2850820
  155.4 28.1 %copy-start.7 = (f32[64,3712]{1,0:T(8,128)S(1)}, f32[64,3712]{1,0:T(8,128)}, u32[]{:S(2)}) copy-start(f32[64,3712]{1,0:T(8,128)} %copy-done.6) | copy-start | bytes 2850820
  155.4 28.2 %copy-start.10 = (f32[64,1024]{1,0:T(8,128)S(1)}, f32[64,1024]{1,0:T(8,128)}, u32[]{:S(2)}) copy-start(f32[64,1024]{1,0:T(8,128)} %copy-done.9) | copy-start | bytes 786436
  178.2 20.5 %collective-permute-start.4 = (f32[8,304,128]{2,1,0:T(8,128)S(1)}, f32[8,304,128]{2,1,0:T(8,128)S(1)}, u32[]{:S(2)}, u32[]{:S(2)}) collective-permute-start(f32[8,304,128]{2,1,0:T(8,128)S(1)} %all_to_all.50.z_ref), channel_id=1, source_target_pairs={{0,4},{4,0},{1,5},{5,1},{2,6},{6,2},{3,7},{7,3},{8,12},{12,8},{9,1... | collective-permute-start | bytes 3735560 | tf_op jit(solution)/shard_map/ppermute | solution.py:189
  186.3 12.4 %all-to-all-start.8 = ((f32[8,96,128]{2,1,0:T(8,128)}), f32[8,96,128]{2,1,0:T(8,128)S(1)}, u32[]{:S(2)}, u32[]{:S(2)}) async-start(f32[8,96,128]{2,1,0:T(8,128)} %shard_map.78), calls=%async_computation.8 | async-start | bytes 786432 | tf_op jit(solution)/shard_map/all_to_all | solution.py:352

commit v6 on v5

--- a/solution.py
+++ b/solution.py
@@ -399,7 +399,7 @@
         return exchanged(call(body, shape(far, per + near * more, LANES), 1)(got), ROWS, first)
 
     parts = call(spread_first_body, flat, 4, scalars=1)(core, got, g, h)
-    arrived, a, b, o, p = summed(parts, a, b, o, p)
+    (arrived,) = summed(parts)
     z = spread_out(call(total_body, shape(near, per, LANES), 1)(arrived), 0)
     partial = call(back_body, whole, 4, scalars=1, scratch=square)(core, z, g, h)
 
@@ -417,7 +417,7 @@
                 target = ((2 * xs + cs) * 2 + ys % 2) * cols + ys // 2
                 moves.append((source, target))
     lines = lax.ppermute(mine, ("y", "c", "x"), moves)
-    arrived, lines = summed(parts, lines)
+    arrived, lines, a, b, o, p = summed(parts, lines, a, b, o, p)
     sums = call(total_with_body, shape(near, per + piece, LANES), 2)(arrived, lines)
     z = spread_out(sums, piece)
     w = other_core(z)

time: 205 us -> 208 us (1.015)
  blocking collectives: 108 us -> 136 us
  waiting for transfers between devices: 27.1 us -> 11.4 us
  starting transfers between devices: 36.7 us -> 30.4 us
  local copies, waits for them, and re-layouts: 8.11 us -> 5.65 us
    all_to_all x6 -> x7, blocking collectives: 108 us -> 136 us  [exchanged(): lax.all_to_all(a, axes, split_axis=0, concat_axis=0, tiled=True, axis_ind...]
    all_to_all x3 -> x2, starting transfers between devices: 14.6 us -> 6.96 us  [exchanged(): lax.all_to_all(a, axes, split_axis=0, concat_axis=0, tiled=True, axis_ind...]
    all_to_all x3 -> x2, waiting for transfers between devices: 15.7 us -> 8.41 us  [exchanged(): lax.all_to_all(a, axes, split_axis=0, concat_axis=0, tiled=True, axis_ind...]
    ppermute x1, waiting for transfers between devices: 10.2 us -> 2.98 us  [per_device(): lines = lax.ppermute(mine, ('y', 'c', 'x'), moves)]
    unnamed x22, local copies, waits for them, and re-layouts: 8.1 us -> 5.64 us
  transfers between devices with their start and end apart: 8 -> 7, of which waited for: 5 -> 3; matrix products, arithmetic and copies ran while one was open for 0% -> 0% of each run, Pallas kernels for 3% -> 3%
where the time goes in v6:
time: 208 us; the launch traced here: 207 us
  blocking collectives  136 us (65%)
  starting transfers between devices  30.4 us (15%)
  Pallas kernels  23 us (11%)
  waiting for transfers between devices  11.4 us (5%)
  local copies, waits for them, and re-layouts  5.65 us (3%)
    all_to_all x7, blocking collectives, exchanged(): lax.all_to_all(a, axes, split_axis=0, concat_axis=0, tiled=True, axis_ind...  136 us
    ppermute x4, starting transfers between devices, other_core(): return lax.ppermute(a, 'c', [(0, 1), (1, 0)])  19.6 us
    all_to_all x2, waiting for transfers between devices, exchanged(): lax.all_to_all(a, axes, split_axis=0, concat_axis=0, tiled=True, axis_ind...  8.41 us
    all_to_all x2, starting transfers between devices, exchanged(): lax.all_to_all(a, axes, split_axis=0, concat_axis=0, tiled=True, axis_ind...  6.96 us
    unnamed x22, local copies, waits for them, and re-layouts  5.64 us
    pallas_call x1, Pallas kernels, per_device(): call(functools.partial(finish_body, per), (shape(R, n), shape(1, R)), 5,...  5.42 us
    pallas_call x1, Pallas kernels, per_device(): call(back_body, whole, 4, scalars=1, scratch=square)(core, z, g, h)  4.36 us
  transfers between devices with their start and end apart: 7, of which 3 were waited for; matrix products, arithmetic and copies ran while one was open for 0% of the time, Pallas kernels for 3%

profile of v6, /device:TPU:1, one launch (start us, length us, event | category | flops | bytes accessed | tf_op | source)
XLA Modules:
  0.0 207.1 jit_solution(12984195486733271048)
XLA Ops:
  0.6 0.0 copy-start
  0.6 1.5 copy-done
  2.2 0.0 copy-start.1
  2.2 1.5 copy-done.1
  3.7 2.0 shard_map.67
  5.7 8.7 %collective-permute-start = (f32[64,3712]{1,0:T(8,128)S(1)}, f32[64,3712]{1,0:T(8,128)S(1)}, u32[]{:S(2)}, u32[]{:S(2)}) collective-permute-start(f32[64,3712]{1,0:T(8,128)S(1)} %get-tuple-element.24), channel_id=1, source_target_pairs={{0,4},{4,0},{1,5},{5,1},{2,6},{6,2},{3,7},{7,3},{8,12},{12,8},{9,1... | collective-permute-start | bytes 2850824 | tf_op jit(solution)/shard_map/ppermute | solution.py:189
  14.4 7.5 %all_to_all.45.got_ref = f32[8,32,128]{2,1,0:T(8,128)S(1)} all-to-all(f32[8,32,128]{2,1,0:T(8,128)S(1)} %get-tuple-element.22), channel_id=1, replica_groups=mesh['y'=8,'z'=8,'c'=2,'x'=4] {'c','x'}, dimensions={0} | all-to-all | bytes 262144 | tf_op jit(solution)/shard_map/all_to_all | solution.py:352
  22.0 0.0 collective-permute-done.h_ref
  22.0 1.1 shard_map.68
  23.1 23.3 %all_to_all.46.got_ref = f32[8,240,128]{2,1,0:T(8,128)S(1)} all-to-all(f32[8,240,128]{2,1,0:T(8,128)S(1)} %bitcast.6), channel_id=1, replica_groups={{0,64,128,192,256,320,384,448},{8,72,136,200,264,328,392,456},{16,80,14..., dimensions={0} | all-to-all | bytes 1966080 | tf_op jit(solution)/shard_map/all_to_all | solution.py:352
  46.4 0.1 shard_map.69
  46.5 24.0 %all_to_all.47.got_ref = f32[8,240,128]{2,1,0:T(8,128)S(1)} all-to-all(f32[8,240,128]{2,1,0:T(8,128)S(1)} %shard_map.69), channel_id=1, replica_groups={{0,8,16,24,32,40,48,56},{64,72,80,88,96,104,112,120},{128,136,144,152,1..., dimensions={0} | all-to-all | bytes 1966080 | tf_op jit(solution)/shard_map/all_to_all | solution.py:352
  70.5 0.1 shard_map.70
  70.5 19.5 %all_to_all.48.z_ref = f32[8,240,128]{2,1,0:T(8,128)S(1)} all-to-all(f32[8,240,128]{2,1,0:T(8,128)S(1)} %shard_map.70), channel_id=1, replica_groups={{0,64,128,192,256,320,384,448},{8,72,136,200,264,328,392,456},{16,80,14..., dimensions={0} | all-to-all | bytes 1966080 | tf_op jit(solution)/shard_map/all_to_all | solution.py:352
  90.0 4.4 %shard_map.71 = f32[8,96,128]{2,1,0:T(8,128)S(1)} custom-call(s32[1]{0:T(128)} %bitcast.c_ref, f32[8,240,128]{2,1,0:T(8,128)S(1)} %all_to_all.48.z_ref, f32[64,3712]{1,0:T(8,128)S(1)} %get-tuple-element.23.g_ref, f32[64,3712]{1,0:T(8,128)S(1)} %collective-permute-done.h_ref), custom_call_target="tpu_custom_call" | custom-call | tf_op jit(solution)/shard_map/pallas_call | solution.py:404
  94.4 14.9 %all_to_all.49.got_ref = f32[8,96,128]{2,1,0:T(8,128)S(1)} all-to-all(f32[8,96,128]{2,1,0:T(8,128)S(1)} %shard_map.71), channel_id=1, replica_groups=mesh['y'=8,'z'=8,'c'=2,'x'=4] {'c','x'}, dimensions={0} | all-to-all | bytes 786432 | tf_op jit(solution)/shard_map/all_to_all | solution.py:352
  109.3 0.0 copy-start.2
  109.3 3.1 %shard_map.72 = (f32[1920,128]{1,0:T(8,128)S(1)}, f32[64,128]{1,0:T(8,128)S(1)}) custom-call(s32[1]{0:T(128)} %bitcast.c_ref, f32[8,96,128]{2,1,0:T(8,128)S(1)} %all_to_all.49.got_ref, f32[64,3712]{1,0:T(8,128)S(1)} %get-tuple-element.23.g_ref, f32[64,3712]{1,0:T(8,128)S(1)} %collective-permute-done.h_ref), custom_call_target="tpu_custom_call" | custom-call | tf_op jit(solution)/shard_map/pallas_call | solution.py:407
  112.4 0.0 copy-start.3
  112.4 0.9 copy-done.3
  113.3 3.6 %all-to-all-start.5 = ((f32[8,240,128]{2,1,0:T(8,128)}), f32[8,240,128]{2,1,0:T(8,128)S(1)}, u32[]{:S(2)}, u32[]{:S(2)}) async-start(f32[8,240,128]{2,1,0:T(8,128)} %bitcast.8), calls=%async_computation.5 | async-start | bytes 1966080 | tf_op jit(solution)/shard_map/all_to_all | solution.py:352
  116.9 0.0 copy-done.2
  116.9 0.0 copy-start.6
  116.9 1.1 shard_map.73
  118.0 0.0 copy-start.4
  118.0 0.9 copy-done.4
  119.0 2.3 %collective-permute-start.2 = (f32[64,3712]{1,0:T(8,128)}, f32[64,3712]{1,0:T(8,128)S(1)}, u32[]{:S(2)}, u32[]{:S(2)}) collective-permute-start(f32[64,3712]{1,0:T(8,128)} %get-tuple-element.28), channel_id=1, source_target_pairs={{0,4},{4,0},{1,5},{5,1},{2,6},{6,2},{3,7},{7,3},{8,12},{12,8},{9,1... | collective-permute-start | bytes 2850824 | tf_op jit(solution)/shard_map/ppermute | solution.py:189
  121.3 0.0 copy-done.6
  121.3 0.0 copy-start.7
  121.3 0.7 copy-done.7
  122.0 2.0 collective-permute-start.3
  124.1 3.8 %collective-permute-start.1 = (f32[8,128]{1,0:T(8,128)S(1)}, f32[8,128]{1,0:T(8,128)S(1)}, u32[]{:S(2)}, u32[]{:S(2)}) collective-permute-start(f32[8,128]{1,0:T(8,128)S(1)} %constant_dynamic-slice_fusion), channel_id=1, source_target_pairs={{0,0},{1,128},{2,256},{3,384},{4,64},{5,192},{6,320},{7,448},{64,4... | collective-permute-start | bytes 12296 | tf_op jit(solution)/shard_map/ppermute | solution.py:419
  127.9 0.0 collective-permute-done.3.p_ref
  127.9 0.0 copy-start.9
  127.9 0.0 collective-permute-done.2.b_ref
  127.9 3.0 %collective-permute-done.1.more_ref = f32[8,128]{1,0:T(8,128)S(1)} collective-permute-done((f32[8,128]{1,0:T(8,128)S(1)}, f32[8,128]{1,0:T(8,128)S(1)}, u32[]{:S(2)}, u32[]{:S(2)}) %collective-permute-start.1) | collective-permute-done | bytes 4128 | tf_op jit(solution)/shard_map/ppermute | solution.py:419
  130.9 3.3 %all-to-all-done.5.got_ref = f32[8,240,128]{2,1,0:T(8,128)S(1)} async-done(((f32[8,240,128]{2,1,0:T(8,128)}), f32[8,240,128]{2,1,0:T(8,128)S(1)}, u32[]{:S(2)}, u32[]{:S(2)}) %all-to-all-start.5) | async-done | bytes 983072 | tf_op jit(solution)/shard_map/all_to_all | solution.py:352
  134.2 0.1 shard_map.75
  134.3 24.1 %all_to_all.50.got_ref = f32[8,248,128]{2,1,0:T(8,128)S(1)} all-to-all(f32[8,248,128]{2,1,0:T(8,128)S(1)} %shard_map.75), channel_id=1, replica_groups={{0,8,16,24,32,40,48,56},{64,72,80,88,96,104,112,120},{128,136,144,152,1..., dimensions={0} | all-to-all | bytes 2031616 | tf_op jit(solution)/shard_map/all_to_all | solution.py:352
  158.4 0.0 copy-done.9
  158.4 0.0 copy-start.5
  158.4 0.0 copy-start.8
  158.4 0.1 shard_map.76
  158.5 0.0 copy-start.10
  158.5 22.4 %all_to_all.51.z_ref = f32[8,304,128]{2,1,0:T(8,128)S(1)} all-to-all(f32[8,304,128]{2,1,0:T(8,128)S(1)} %shard_map.76), channel_id=1, replica_groups={{0,64,128,192,256,320,384,448},{8,72,136,200,264,328,392,456},{16,80,14..., dimensions={0} | all-to-all | bytes 2490368 | tf_op jit(solution)/shard_map/all_to_all | solution.py:352
  180.9 6.6 %collective-permute-start.4 = (f32[8,304,128]{2,1,0:T(8,128)S(1)}, f32[8,304,128]{2,1,0:T(8,128)S(1)}, u32[]{:S(2)}, u32[]{:S(2)}) collective-permute-start(f32[8,304,128]{2,1,0:T(8,128)S(1)} %all_to_all.51.z_ref), channel_id=1, source_target_pairs={{0,4},{4,0},{1,5},{5,1},{2,6},{6,2},{3,7},{7,3},{8,12},{12,8},{9,1... | collective-permute-start | bytes 3735560 | tf_op jit(solution)/shard_map/ppermute | solution.py:189
  187.6 0.0 copy-done.5
  187.6 0.0 copy-done.8
  187.6 0.0 copy-done.10
  187.6 2.7 %shard_map.78 = f32[8,96,128]{2,1,0:T(8,128)} custom-call(s32[1]{0:T(128)} %bitcast.c_ref, f32[8,304,128]{2,1,0:T(8,128)S(1)} %all_to_all.51.z_ref, f32[64,3712]{1,0:T(8,128)S(1)} %copy-done.5, f32[64,3712]{1,0:T(8,128)S(1)} %collective-permute-done.2.b_ref, f32[64,1024]{1,0:T(8,128)S(1)} %copy-done.8, f32[64,1024]{1,0:T(8,128)S(1)} %copy-done.10), custom_call_target="tpu_custom_call" | custom-call | tf_op jit(solution)/shard_map/pallas_call | solution.py:424
  190.3 3.4 %all-to-all-start.8 = ((f32[8,96,128]{2,1,0:T(8,128)}), f32[8,96,128]{2,1,0:T(8,128)S(1)}, u32[]{:S(2)}, u32[]{:S(2)}) async-start(f32[8,96,128]{2,1,0:T(8,128)} %shard_map.78), calls=%async_computation.8 | async-start | bytes 786432 | tf_op jit(solution)/shard_map/all_to_all | solution.py:352
  193.7 2.9 %shard_map.77 = (f32[64,64]{1,0:T(8,128)S(1)}, f32[64,64]{1,0:T(8,128)}) custom-call(s32[1]{0:T(128)} %bitcast.c_ref, f32[8,304,128]{2,1,0:T(8,128)S(1)} %all_to_all.51.z_ref, f32[64,128]{1,0:T(8,128)S(1)} %get-tuple-element.26.yt_ref), custom_call_target="tpu_custom_call" | custom-call | tf_op jit(solution)/shard_map/pallas_call | solution.py:426
  196.6 5.1 %all-to-all-done.8.got_ref = f32[8,96,128]{2,1,0:T(8,128)S(1)} async-done(((f32[8,96,128]{2,1,0:T(8,128)}), f32[8,96,128]{2,1,0:T(8,128)S(1)}, u32[]{:S(2)}, u32[]{:S(2)}) %all-to-all-start.8) | async-done | bytes 393248 | tf_op jit(solution)/shard_map/all_to_all | solution.py:352
  201.7 0.0 collective-permute-done.4.w_ref
  201.7 5.4 %shard_map.79 = (f32[64,7392]{1,0:T(8,128)}, f32[1,64]{1,0:T(1,128)}) custom-call(s32[1]{0:T(128)} %bitcast.c_ref, f32[8,96,128]{2,1,0:T(8,128)S(1)} %all-to-all-done.8.got_ref, f32[64,64]{1,0:T(8,128)S(1)} %get-tuple-element.38.inv_ref, f32[8,304,128]{2,1,0:T(8,128)S(1)} %all_to_all.51.z_ref, f32[8,304,128]{2,1,0:T(8,128)S(1)} %collective-permute-done.4.w_ref), custom_call_target="tpu_custom_call" | custom-call | tf_op jit(solution)/shard_map/pallas_call | solution.py:433
  (2 shorter events, 0.1 us)
Async XLA Ops:
  0.6 1.5 copy-start
  2.2 1.5 copy-start.1
  5.7 16.3 %collective-permute-start = (f32[64,3712]{1,0:T(8,128)S(1)}, f32[64,3712]{1,0:T(8,128)S(1)}, u32[]{:S(2)}, u32[]{:S(2)}) collective-permute-start(f32[64,3712]{1,0:T(8,128)S(1)} %get-tuple-element.24), channel_id=1, source_target_pairs={{0,4},{4,0},{1,5},{5,1},{2,6},{6,2},{3,7},{7,3},{8,12},{12,8},{9,1... | collective-permute-start | bytes 2850824 | tf_op jit(solution)/shard_map/ppermute | solution.py:189
  109.3 7.6 %copy-start.2 = (f32[64,7392]{1,0:T(8,128)S(1)}, f32[64,7392]{1,0:T(8,128)}, u32[]{:S(2)}) copy-start(f32[64,7392]{1,0:T(8,128)} %a_ref.2) | copy-start | bytes 5677060
  112.4 0.9 copy-start.3
  113.3 20.9 %all-to-all-start.5 = ((f32[8,240,128]{2,1,0:T(8,128)}), f32[8,240,128]{2,1,0:T(8,128)S(1)}, u32[]{:S(2)}, u32[]{:S(2)}) async-start(f32[8,240,128]{2,1,0:T(8,128)} %bitcast.8), calls=%async_computation.5 | async-start | bytes 1966080 | tf_op jit(solution)/shard_map/all_to_all | solution.py:352
  116.9 4.3 %copy-start.6 = (f32[64,2048]{1,0:T(8,128)S(1)}, f32[64,2048]{1,0:T(8,128)}, u32[]{:S(2)}) copy-start(f32[64,2048]{1,0:T(8,128)} %a_ref.3) | copy-start | bytes 1572868
  118.0 0.9 copy-start.4
  119.0 8.9 %collective-permute-start.2 = (f32[64,3712]{1,0:T(8,128)}, f32[64,3712]{1,0:T(8,128)S(1)}, u32[]{:S(2)}, u32[]{:S(2)}) collective-permute-start(f32[64,3712]{1,0:T(8,128)} %get-tuple-element.28), channel_id=1, source_target_pairs={{0,4},{4,0},{1,5},{5,1},{2,6},{6,2},{3,7},{7,3},{8,12},{12,8},{9,1... | collective-permute-start | bytes 2850824 | tf_op jit(solution)/shard_map/ppermute | solution.py:189
  121.3 0.7 copy-start.7
  122.0 5.9 %collective-permute-start.3 = (f32[64,1024]{1,0:T(8,128)S(1)}, f32[64,1024]{1,0:T(8,128)S(1)}, u32[]{:S(2)}, u32[]{:S(2)}) collective-permute-start(f32[64,1024]{1,0:T(8,128)S(1)} %get-tuple-element.30), channel_id=1, source_target_pairs={{0,4},{4,0},{1,5},{5,1},{2,6},{6,2},{3,7},{7,3},{8,12},{12,8},{9,1... | collective-permute-start | bytes 786440 | tf_op jit(solution)/shard_map/ppermute | solution.py:189
  124.1 6.8 %collective-permute-start.1 = (f32[8,128]{1,0:T(8,128)S(1)}, f32[8,128]{1,0:T(8,128)S(1)}, u32[]{:S(2)}, u32[]{:S(2)}) collective-permute-start(f32[8,128]{1,0:T(8,128)S(1)} %constant_dynamic-slice_fusion), channel_id=1, source_target_pairs={{0,0},{1,128},{2,256},{3,384},{4,64},{5,192},{6,320},{7,448},{64,4... | collective-permute-start | bytes 12296 | tf_op jit(solution)/shard_map/ppermute | solution.py:419
  127.9 30.5 %copy-start.9 = (f32[64,1024]{1,0:T(8,128)}, f32[64,1024]{1,0:T(8,128)S(1)}, u32[]{:S(2)}) copy-start(f32[64,1024]{1,0:T(8,128)S(1)} %collective-permute-done.3.p_ref) | copy-start | bytes 786436
  158.4 29.1 %copy-start.5 = (f32[64,3712]{1,0:T(8,128)S(1)}, f32[64,3712]{1,0:T(8,128)}, u32[]{:S(2)}) copy-start(f32[64,3712]{1,0:T(8,128)} %copy-done.4) | copy-start | bytes 2850820
  158.4 29.2 %copy-start.8 = (f32[64,1024]{1,0:T(8,128)S(1)}, f32[64,1024]{1,0:T(8,128)}, u32[]{:S(2)}) copy-start(f32[64,1024]{1,0:T(8,128)} %copy-done.7) | copy-start | bytes 786436
  158.5 29.1 %copy-start.10 = (f32[64,1024]{1,0:T(8,128)S(1)}, f32[64,1024]{1,0:T(8,128)}, u32[]{:S(2)}) copy-start(f32[64,1024]{1,0:T(8,128)} %copy-done.9) | copy-start | bytes 786436
  180.9 20.8 %collective-permute-start.4 = (f32[8,304,128]{2,1,0:T(8,128)S(1)}, f32[8,304,128]{2,1,0:T(8,128)S(1)}, u32[]{:S(2)}, u32[]{:S(2)}) collective-permute-start(f32[8,304,128]{2,1,0:T(8,128)S(1)} %all_to_all.51.z_ref), channel_id=1, source_target_pairs={{0,4},{4,0},{1,5},{5,1},{2,6},{6,2},{3,7},{7,3},{8,12},{12,8},{9,1... | collective-permute-start | bytes 3735560 | tf_op jit(solution)/shard_map/ppermute | solution.py:189
  190.3 11.4 %all-to-all-start.8 = ((f32[8,96,128]{2,1,0:T(8,128)}), f32[8,96,128]{2,1,0:T(8,128)S(1)}, u32[]{:S(2)}, u32[]{:S(2)}) async-start(f32[8,96,128]{2,1,0:T(8,128)} %shard_map.78), calls=%async_computation.8 | async-start | bytes 786432 | tf_op jit(solution)/shard_map/all_to_all | solution.py:352
